TPU v7x, 32 devices: a whole 2x2x4 slice. The times are simulated.
32 devices in a mesh: sect: 2 (over x), grp: 16 (over z, y, core), tp: 1.
Axes of the slice: x: 2, y: 2, z: 4, core: 2. Of those that a mesh axis runs over, the one named last changes fastest.
Arguments:
- queries: bfloat16 [512, 128, 576], P('grp', ('sect', 'tp')), may hold values from -400 to 400, as said below
- latent_cache: bfloat16 [512, 128, 576], P('grp'), may hold values from -6 to 6, as said below
- cache_len: int32 [512], P('grp'), may hold values from 1 to 128, 32768 in all
- value_up: bfloat16 [128, 512, 128], P(('sect', 'tp')), may hold values from -0.25 to 0.25
- out_proj: bfloat16 [16384, 7168], P(('sect', 'tp'), 'grp'), may hold values from -0.046875 to 0.046875
- residual: bfloat16 [512, 7168], P(None, 'grp'), may hold values from -3 to 3
- w_gate: bfloat16 [16, 7168, 2048], P('grp', None, ('sect', 'tp')), may hold values from -0.0625 to 0.0625
- w_up: bfloat16 [16, 7168, 2048], P('grp', None, ('sect', 'tp')), may hold values from -0.0625 to 0.0625
- w_down: bfloat16 [16, 2048, 7168], P('grp', ('sect', 'tp')), may hold values from -0.1875 to 0.1875
- route_ids: int32 [512, 8], replicated, may hold values from 0 to 15, all different within a row; in each aligned block of 512 rows (0 to 511, 512 to 1023, ...) at most 384 rows name the same one
- route_weights: float32 [512, 8], replicated, may hold values from 0.1 to 0.6
Outputs:
- layer_out: bfloat16 [512, 7168], P(('sect', 'tp'), 'grp')
Inputs may be any that keep to these rules, and one draw needn't show every extreme that they name: `queries`: every entry lies in this range. `latent_cache`: every entry lies in this range. `route_ids`: each row names 8 different experts; every expert is named by at most 384 rows, and one expert by exactly 384. `cache_len`: some row has exactly 128 filled positions.
All inputs are finite; a program needn't handle non-finite values. No bound on the sum of `cache_len` on one device may be relied on, other than what follows from the above.
Results may differ from a plain program's by a relative error of at most 0.018.
Values may be sent and summed in bfloat16 or wider, within the bound.
No kernel may reach another device: no remote copies, remote signals or barrier semaphores. Data moves between devices by JAX's collectives and lax.ppermute only.
A program may use at most 128 MiB of HBM per device.

v0:
```python
import jax
import jax.numpy as jnp
from jax import lax
from jax.sharding import PartitionSpec as P

LAT = 512
VDIM = 128
TOP = 8


SOFTMAX_SCALE = 0.0721688
MASK_VALUE = -1e30


def slot_tables(route_ids, route_weights, expert_count, capacity):
    row_total = route_ids.shape[0]
    expert_ids = jnp.arange(expert_count, dtype=jnp.int32)
    matches = route_ids[None, :, :] == expert_ids[:, None, None]
    chosen = jnp.any(matches, axis=2)
    weight = jnp.sum(jnp.where(matches, route_weights[None, :, :], 0.0), axis=2)
    slot_rank = jnp.cumsum(chosen.astype(jnp.int32), axis=1) - 1
    slot_ids = jnp.arange(capacity, dtype=jnp.int32)
    placed = chosen[:, :, None] & (slot_rank[:, :, None] == slot_ids[None, None, :])
    row_ids = jnp.arange(row_total, dtype=jnp.int32)
    slot_rows = jnp.sum(jnp.where(placed, row_ids[None, :, None], 0), axis=1)
    slot_valid = jnp.any(placed, axis=1)
    slot_weight = jnp.sum(jnp.where(placed, weight[:, :, None], 0.0), axis=1)
    return (placed, slot_rows, slot_valid, slot_weight)


def pick_slots(source_rows, slot_rows, slot_valid):
    picked = jnp.take(source_rows, slot_rows, axis=0)
    return jnp.where(slot_valid[:, :, None], picked, jnp.zeros_like(picked))


def on_device(
    queries,
    latent_cache,
    cache_len,
    value_up,
    out_proj,
    residual,
    w_gate,
    w_up,
    w_down,
    route_ids,
    route_weights,
):
    local_rows = queries.shape[0]
    local_heads = queries.shape[1]
    scores = (
        jnp.einsum("rhk,rlk->rhl", queries, latent_cache, preferred_element_type=jnp.float32)
        * SOFTMAX_SCALE
    )
    positions = jnp.arange(latent_cache.shape[1], dtype=jnp.int32)
    in_range = positions[None, None, :] < cache_len[:, None, None]
    masked = jnp.where(in_range, scores, MASK_VALUE)
    row_max = jnp.max(masked, axis=2, keepdims=True)
    exp_scores = jnp.where(in_range, jnp.exp(masked - row_max), 0.0)
    probs = (exp_scores / jnp.sum(exp_scores, axis=2, keepdims=True)).astype(jnp.bfloat16)
    latent_out = jnp.einsum(
        "rhl,rlc->rhc", probs, latent_cache[:, :, :LAT], preferred_element_type=jnp.float32
    ).astype(jnp.bfloat16)
    heads_out = jnp.einsum("rhc,hcv->rhv", latent_out, value_up, preferred_element_type=jnp.float32)
    heads_out = heads_out.astype(jnp.bfloat16).reshape(local_rows, local_heads * VDIM)
    partial_attn = jnp.dot(
        lax.all_gather(heads_out, "grp", axis=0, tiled=True),
        out_proj,
        preferred_element_type=jnp.float32,
    )
    row_total = residual.shape[0]
    expert_count = lax.axis_size("grp")
    tensor_count = lax.axis_size(("sect", "tp"))
    tensor_index = lax.axis_index(("sect", "tp"))
    own_expert = lax.axis_index("grp")
    capacity = min(row_total, row_total * TOP * 3 // (2 * expert_count))
    placed, slot_rows, slot_valid, slot_weight = slot_tables(
        route_ids, route_weights, expert_count, capacity
    )
    share_rows = row_total // tensor_count
    attention = lax.psum(partial_attn, ("sect", "tp"))
    layer_input = (residual.astype(jnp.float32) + attention).astype(jnp.bfloat16)
    own_rows = lax.dynamic_slice_in_dim(layer_input, tensor_index * share_rows, share_rows, 0)
    outgoing = pick_slots(layer_input, slot_rows, slot_valid)
    received = lax.all_to_all(outgoing, "grp", split_axis=0, concat_axis=2, tiled=True)
    expert_in = received[0]
    own_weight = lax.dynamic_index_in_dim(slot_weight, own_expert, 0, keepdims=False)
    gate_value = jnp.dot(expert_in, w_gate[0], preferred_element_type=jnp.float32)
    up_value = jnp.dot(expert_in, w_up[0], preferred_element_type=jnp.float32)
    hidden = (own_weight[:, None] * jax.nn.silu(gate_value) * up_value).astype(jnp.bfloat16)
    own_placed = lax.dynamic_index_in_dim(placed, own_expert, 0, keepdims=False).astype(
        jnp.bfloat16
    )
    hidden_rows = jnp.dot(own_placed, hidden, preferred_element_type=jnp.float32).astype(
        jnp.bfloat16
    )
    expert_term = jnp.dot(hidden_rows, w_down[0], preferred_element_type=jnp.float32)
    column_sums = lax.psum_scatter(
        expert_term.astype(jnp.bfloat16), "grp", scatter_dimension=1, tiled=True
    )
    routed_sum = lax.psum_scatter(
        column_sums, ("sect", "tp"), scatter_dimension=0, tiled=True
    ).astype(jnp.float32)
    return (own_rows.astype(jnp.float32) + routed_sum).astype(jnp.bfloat16)


def solution(mesh):
    return jax.shard_map(
        on_device,
        mesh=mesh,
        in_specs=(
            P("grp", ("sect", "tp"), None),
            P("grp", None, None),
            P("grp"),
            P(("sect", "tp"), None, None),
            P(("sect", "tp"), "grp"),
            P(None, "grp"),
            P("grp", None, ("sect", "tp")),
            P("grp", None, ("sect", "tp")),
            P("grp", ("sect", "tp"), None),
            P(),
            P(),
        ),
        out_specs=P(("sect", "tp"), "grp"),
        check_vma=False,
    )
```

profile of v0, /device:TPU:0, one launch (start us, length us, event | category | flops | bytes accessed | tf_op | source)
XLA Modules:
  0.0 466.7 jit_solution(10396957339783495219)
XLA Ops:
  6.5 0.0 copy-start
  6.5 0.0 all-gather.2.cloned.1.call-start
  6.5 0.9 iota_compare_fusion.2
  7.4 0.9 copy-done
  8.3 4.5 fusion.39
  12.8 4.1 fusion.15
  17.0 0.0 copy-start.3
  17.0 5.4 %fusion.27 = bf16[64,4,8,128]{3,2,1,0:T(8,128)(2,1)S(1)} fusion(bf16[64,512,128]{2,1,0:T(8,128)(2,1)} %param.14, bf16[32,64,512]{2,1,0:T(8,128)(2,1)S(1)} %fusion.15), kind=kOutput, calls=%fused_computation.27 | convolution fusion | flops 268697600 | bytes 11010048 | tf_op jit(solution)/shard_map/rhc,hcv->rhv/dot_general | solution.py:64
  22.4 0.9 copy.42
  23.3 0.0 all-gather.2.cloned.1.call-update
  23.3 0.0 all-reduce.2.cloned.1.call-start
  23.4 0.0 copy-done.3
  23.4 0.1 fusion.35
  23.5 1.2 reduce-window.6
  24.6 0.2 slice_reduce_fusion
  24.9 0.1 copy_bitcast_fusion.1
  25.0 3.3 select_reduce_fusion
  28.3 0.0 copy-start.2
  28.3 72.7 %all-gather.2.cloned.1.call-done = bf16[512,8192]{1,0:T(8,128)(2,1)} async-done(((bf16[32,8192]{1,0:T(8,128)(2,1)}), bf16[512,8192]{1,0:T(8,128)(2,1)}) %all-gather.2.cloned.1.call-update) | async-done | bytes 8388624 | tf_op jit(solution)/shard_map/all_gather | solution.py:67
  101.1 10.4 %fusion.40 = f32[512,448]{0,1:T(8,128)} fusion(bf16[512,8192]{1,0:T(8,128)(2,1)} %all-gather.2.cloned.1.call-done, bf16[8192,448]{0,1:T(8,128)(2,1)} %param.15), kind=kOutput, calls=%fused_computation.52 | convolution fusion | flops 3758096384 | bytes 16646144 | tf_op jit(solution)/shard_map/dot_general | solution.py:66
  111.5 0.0 all-reduce.2.cloned.1.call-update
  111.6 5.1 %fusion.7 = (pred[16,512,384]{2,1,0:T(32,128)(4,1)}, pred[16,384]{1,0:T(8,128)(4,1)S(1)}) fusion(s32[16,512]{1,0:T(8,128)S(1)} %copy_bitcast_fusion.1, pred[16,512]{1,0:T(8,128)(4,1)S(1)} %fusion.35), kind=kLoop, calls=%fused_computation.11 | loop fusion | flops 9431040 | bytes 3192832 | tf_op jit(solution)/shard_map/and | solution.py:23
  116.7 30.4 %all-reduce.2.cloned.1.call-done = f32[512,448]{0,1:T(8,128)} async-done(((f32[512,448]{0,1:T(8,128)}), f32[512,448]{0,1:T(8,128)}) %all-reduce.2.cloned.1.call-update) | async-done | bytes 917520 | tf_op jit(solution)/shard_map/psum | solution.py:81
  147.1 0.0 copy-done.2
  147.1 1.3 add_convert_fusion
  148.5 0.2 copy.27
  148.7 25.4 %gather_fusion = bf16[6144,448]{1,0:T(8,128)(2,1)} fusion(bf16[512,448]{1,0:T(8,128)(2,1)S(1)} %copy.27, s32[6144]{0:T(1024)S(1)} %broadcast_clamp_fusion), kind=kCustom, calls=%fused_computation | custom fusion | bytes 11034624 | tf_op jit(solution)/shard_map/jit(_take)/gather | solution.py:32
  174.1 8.3 %copy.28 = bf16[16,384,448]{1,2,0:T(8,128)(2,1)} copy(bf16[16,384,448]{2,1,0:T(8,128)(2,1)} %bitcast.51) | data formatting | bytes 11010048 | tf_op jit(solution)/shard_map/jit(_take)/gather | solution.py:32
  182.4 5.9 %select_select_fusion = bf16[16,384,448]{1,2,0:T(8,128)(2,1)} fusion(bf16[16,384,448]{1,2,0:T(8,128)(2,1)} %copy.28, pred[16,384]{1,0:T(8,128)(4,1)S(1)} %compare_and_fusion, pred[16,384]{1,0:T(8,128)(4,1)S(1)} %get-tuple-element.6), kind=kLoop, calls=%fused_computation.13 | loop fusion | flops 5505024 | bytes 11022336 | tf_op jit(solution)/shard_map/jit(_where)/select_n | solution.py:33
  188.3 0.0 copy-start.4
  188.3 5.8 %all-to-all-start = ((bf16[16,384,448]{1,2,0:T(8,128)(2,1)}), bf16[16,384,448]{1,2,0:T(8,128)(2,1)}, u32[]{:S(2)}, u32[]{:S(2)}) async-start(bf16[16,384,448]{1,2,0:T(8,128)(2,1)} %select_select_fusion), calls=%async_computation | async-start | bytes 11010048 | tf_op jit(solution)/shard_map/all_to_all | solution.py:85
  194.1 0.2 reduce-scatter.3.cloned.1.call-start
  194.3 0.0 copy-done.4
  194.3 0.1 select_reduce_fusion.2
  194.4 4.6 select_reduce_fusion.1
  199.1 95.5 %all-to-all-done = bf16[16,384,448]{1,2,0:T(8,128)(2,1)} async-done(((bf16[16,384,448]{1,2,0:T(8,128)(2,1)}), bf16[16,384,448]{1,2,0:T(8,128)(2,1)}, u32[]{:S(2)}, u32[]{:S(2)}) %all-to-all-start) | async-done | bytes 5505056 | tf_op jit(solution)/shard_map/all_to_all | solution.py:85
  294.6 10.9 %fusion.5 = f32[384,1024]{1,0:T(8,128)S(1)} fusion(bf16[384,7168]{0,1:T(8,128)(2,1)} %bitcast.6, bf16[1,7168,1024]{2,1,0:T(8,128)(2,1)} %param.17), kind=kOutput, calls=%fused_computation.6 | convolution fusion | flops 5637144576 | bytes 21757952 | tf_op jit(solution)/shard_map/dot_general | solution.py:88
  305.5 11.8 %multiply_convert_fusion = bf16[384,1024]{1,0:T(8,128)(2,1)} fusion(f32[384,1024]{1,0:T(8,128)S(1)} %fusion.5, bf16[384,7168]{0,1:T(8,128)(2,1)} %bitcast.6, bf16[1,7168,1024]{2,1,0:T(8,128)(2,1)} %param.18, f32[384]{0:T(512)S(1)} %dynamic-slice_reduce_fusion), kind=kOutput, calls=%fused_computation.19 | convolution fusion | flops 5639897088 | bytes 22545920 | tf_op jit(solution)/shard_map/dot_general | solution.py:89
  317.3 0.0 copy-start.1
  317.3 14.3 %fusion.8 = bf16[512,7168]{0,1:T(8,128)(2,1)} fusion(bf16[1,1024,7168]{2,1,0:T(8,128)(2,1)} %param.19, bf16[384,1024]{1,0:T(8,128)(2,1)} %multiply_convert_fusion, pred[16,512,384]{2,1,0:T(32,128)(4,1)} %get-tuple-element.5, s32[]{:T(128)S(6)} %select_n.55), kind=kOutput, calls=%fused_computation.12 | convolution fusion | flops 7923040256 | bytes 23003140 | tf_op jit(solution)/shard_map/dot_general | solution.py:97
  331.6 0.0 reduce-scatter.3.cloned.1.call-update
  331.6 0.0 reduce-scatter.5.cloned.1.call-start
  331.6 111.0 %reduce-scatter.3.cloned.1.call-done = bf16[512,448]{0,1:T(8,128)(2,1)} async-done(((bf16[512,7168]{0,1:T(8,128)(2,1)}), bf16[512,448]{0,1:T(8,128)(2,1)}) %reduce-scatter.3.cloned.1.call-update) | async-done | bytes 458768 | tf_op jit(solution)/shard_map/reduce_scatter | solution.py:98
  442.7 0.0 reduce-scatter.5.cloned.1.call-update
  442.7 15.7 %reduce-scatter.5.cloned.1.call-done = bf16[256,448]{0,1:T(8,128)(2,1)} async-done(((bf16[512,448]{0,1:T(8,128)(2,1)}), bf16[256,448]{0,1:T(8,128)(2,1)}) %reduce-scatter.5.cloned.1.call-update) | async-done | bytes 229392 | tf_op jit(solution)/shard_map/reduce_scatter | solution.py:101
  458.5 1.7 add_convert_fusion.1
  460.1 0.0 copy-done.1
  (8 shorter events, 0.1 us)
Async XLA Ops:
  6.5 1.8 copy-start
  6.5 94.5 %all-gather.2.cloned.1.call-start = ((), (), s32[]{:S(2)}) async-start(), calls=%async_computation.3 | async-start | bytes 8912896 | tf_op jit(solution)/shard_map/all_gather | solution.py:67
  17.0 6.4 %copy-start.3 = (s32[512,8]{0,1:T(8,128)S(1)}, s32[512,8]{0,1:T(8,128)}, u32[]{:S(2)}) copy-start(s32[512,8]{0,1:T(8,128)} %param.20) | copy-start | bytes 49156
  23.3 123.8 %all-reduce.2.cloned.1.call-start = ((), (), s32[]{:S(2)}) async-start(), calls=%async_computation.4 | async-start | bytes 1835008 | tf_op jit(solution)/shard_map/psum | solution.py:81
  28.3 118.8 %copy-start.2 = (bf16[512,448]{0,1:T(8,128)(2,1)S(1)}, bf16[512,448]{0,1:T(8,128)(2,1)}, u32[]{:S(2)}) copy-start(bf16[512,448]{0,1:T(8,128)(2,1)} %param.16) | copy-start | bytes 1376260
  188.3 6.0 %copy-start.4 = (f32[512,8]{0,1:T(8,128)S(1)}, f32[512,8]{0,1:T(8,128)}, u32[]{:S(2)}) copy-start(f32[512,8]{0,1:T(8,128)} %param.21) | copy-start | bytes 49156
  188.3 106.3 %all-to-all-start = ((bf16[16,384,448]{1,2,0:T(8,128)(2,1)}), bf16[16,384,448]{1,2,0:T(8,128)(2,1)}, u32[]{:S(2)}, u32[]{:S(2)}) async-start(bf16[16,384,448]{1,2,0:T(8,128)(2,1)} %select_select_fusion), calls=%async_computation | async-start | bytes 11010048 | tf_op jit(solution)/shard_map/all_to_all | solution.py:85
  194.1 248.6 %reduce-scatter.3.cloned.1.call-start = ((), (), s32[]{:S(2)}) async-start(), calls=%async_computation.5 | async-start | bytes 7798784 | tf_op jit(solution)/shard_map/reduce_scatter | solution.py:98
  317.3 142.9 %copy-start.1 = (bf16[32,64,576]{2,1,0:T(8,128)(2,1)S(1)}, bf16[32,64,576]{2,1,0:T(8,128)(2,1)}, u32[]{:S(2)}) copy-start(bf16[32,64,576]{2,1,0:T(8,128)(2,1)} %param.11) | copy-start | bytes 7077892
  331.6 126.9 %reduce-scatter.5.cloned.1.call-start = ((), (), s32[]{:S(2)}) async-start(), calls=%async_computation.6 | async-start | bytes 688128 | tf_op jit(solution)/shard_map/reduce_scatter | solution.py:101
Sparse Core Ops, SparseCore 0:
  23.4 77.5 all-gather.1
  111.7 35.4 all-reduce.1
  331.7 110.9 reduce-scatter.2
  444.9 13.5 reduce-scatter.4
where the time goes:
time: 467 us
  waiting for transfers between devices  326 us (70%)
  matrix products  61.4 us (13%)
  local copies, waits for them, and re-layouts  36.1 us (8%)
  other arithmetic  24.2 us (5%)
  between operations  13.3 us (3%)
  starting transfers between devices  6.1 us (1%)
    reduce_scatter x1, waiting for transfers between devices, on_device(): lax.psum_scatter(expert_term.astype(jnp.bfloat16), 'grp', scatter_dimensi...  111 us
    all_to_all x1, waiting for transfers between devices, on_device(): lax.all_to_all(outgoing, 'grp', split_axis=0, concat_axis=2, tiled=True)  95.5 us
    all_gather x1, waiting for transfers between devices, on_device(): lax.all_gather(heads_out, 'grp', axis=0, tiled=True)  72.7 us
    gather x2, local copies, waits for them, and re-layouts, pick_slots(): picked = jnp.take(source_rows, slot_rows, axis=0)  33.8 us
    psum x1, waiting for transfers between devices, on_device(): attention = lax.psum(partial_attn, ('sect', 'tp'))  30.4 us
    reduce_scatter x1, waiting for transfers between devices, on_device(): lax.psum_scatter(column_sums, ('sect', 'tp'), scatter_dimension=0, tiled=...  15.7 us
    dot_general x1, matrix products, on_device(): jnp.dot(hidden_rows, w_down[0], preferred_element_type=jnp.float32)  14.3 us
    dot_general x1, matrix products, on_device(): up_value = jnp.dot(expert_in, w_up[0], preferred_element_type=jnp.float32)  11.8 us
  transfers between devices with their start and end apart: 5, of which 5 were waited for; matrix products, arithmetic and copies ran while one was open for 3% of the time, Pallas kernels for 0%

commit v1 on v0

v1 whole, which is shorter than its diff:
```python
import functools

import jax
import jax.numpy as jnp
from jax import lax
from jax.experimental import pallas as pl
from jax.experimental.pallas import tpu as pltpu
from jax.sharding import Mesh
from jax.sharding import PartitionSpec as P

LAT = 512
VDIM = 128
SOFTMAX_SCALE = 0.0721688
MASK_VALUE = -1e30
MIB = 1024 * 1024

GRP = ("line", "side", "core")
HID = ("sect", "tp")
F32 = jnp.float32
BF16 = jnp.bfloat16


def swap(value, axis):
    return lax.ppermute(value, axis, [(0, 1), (1, 0)])


def shift(value, amount):
    size = lax.axis_size("line")
    return lax.ppermute(value, "line", [(i, (i + amount) % size) for i in range(size)])


def relative(value, axis, index):
    return jnp.where(index == 0, value, jnp.flip(value, axis))


def attend(queries, latent_cache, cache_len, value_up):
    scores = (
        jnp.einsum("rhk,rlk->rhl", queries, latent_cache, preferred_element_type=F32)
        * SOFTMAX_SCALE
    )
    positions = jnp.arange(latent_cache.shape[1], dtype=jnp.int32)
    in_range = positions[None, None, :] < cache_len[:, None, None]
    masked = jnp.where(in_range, scores, MASK_VALUE)
    row_max = jnp.max(masked, axis=2, keepdims=True)
    exp_scores = jnp.where(in_range, jnp.exp(masked - row_max), 0.0)
    probs = (exp_scores / jnp.sum(exp_scores, axis=2, keepdims=True)).astype(BF16)
    latent_out = jnp.einsum(
        "rhl,rlc->rhc", probs, latent_cache[:, :, :LAT], preferred_element_type=F32
    ).astype(BF16)
    heads_out = jnp.einsum("rhc,hcv->rhv", latent_out, value_up, preferred_element_type=F32)
    return heads_out.astype(BF16).reshape(queries.shape[0], queries.shape[1] * VDIM)


def in_hbm(value):
    return pltpu.with_memory_space_constraint(value, pltpu.HBM)


def project_kernel(count, place_ref, own_ref, sibling_ref, *refs):
    blocks, refs = refs[:-8], refs[-8:]
    out_ref, rows_ref, own_rows, sibling_rows, own_total, sibling_total, total_ref, arrived = refs
    size, depth = blocks[0].shape
    tile = min(1024, depth)
    tiles = depth // tile

    def rows_copy(i, block):
        start = pl.multiple_of(place_ref[2 * i + 1] * size, size)
        return pltpu.make_async_copy(block, rows_ref.at[pl.ds(start, size)], arrived.at[i])

    def weight_copy(half, k):
        columns = pl.ds(pl.multiple_of(k * tile, tile), tile)
        source, target = ((own_ref, own_rows), (sibling_ref, sibling_rows))[half]
        return pltpu.make_async_copy(
            source.at[:, columns], target.at[:, columns], arrived.at[count + half * tiles + k]
        )

    for i in range(count):
        for at, block in enumerate(blocks):

            @pl.when(place_ref[2 * i] == at)
            def _():
                rows_copy(i, block).start()

    for k in range(tiles):
        for half in range(2):
            weight_copy(half, k).start()
    own_total[...] = jnp.zeros_like(own_total)
    sibling_total[...] = jnp.zeros_like(sibling_total)
    for i in range(count):
        rows_copy(i, blocks[0]).wait()

    def step(k, _):
        columns = pl.ds(pl.multiple_of(k * tile, tile), tile)
        rows = rows_ref[:, columns]
        for half, (weight_ref, sum_ref) in enumerate(
            ((own_rows, own_total), (sibling_rows, sibling_total))
        ):
            weight_copy(half, k).wait()
            sum_ref[...] += lax.dot_general(
                weight_ref[:, columns], rows, (((1,), (1,)), ((), ())), preferred_element_type=F32
            )
        return 0

    lax.fori_loop(0, tiles, step, 0)
    width, core = own_total.shape[0], place_ref[2 * count]
    total_ref[pl.ds(pl.multiple_of(core * width, 8), width), :] = own_total[...]
    total_ref[pl.ds(pl.multiple_of((1 - core) * width, 8), width), :] = sibling_total[...]
    out_ref[...] = total_ref[...].T.astype(out_ref.dtype)


def project(place, count, blocks, own, sibling, dtype):
    size, depth = blocks[0].shape
    width = own.shape[0]
    anywhere = pl.BlockSpec(memory_space=pl.ANY)
    return pl.pallas_call(
        functools.partial(project_kernel, count),
        in_specs=[pl.BlockSpec(memory_space=pltpu.SMEM)] + [anywhere] * (2 + len(blocks)),
        out_specs=pl.BlockSpec(memory_space=pltpu.VMEM),
        out_shape=jax.ShapeDtypeStruct((count * size, 2 * width), dtype),
        scratch_shapes=[pltpu.VMEM((count * size, depth), BF16)]
        + [pltpu.VMEM((width, depth), BF16)] * 2
        + [pltpu.VMEM((width, count * size), F32)] * 2
        + [
            pltpu.VMEM((2 * width, count * size), F32),
            pltpu.SemaphoreType.DMA((count + 2 * (depth // min(1024, depth)),)),
        ],
        compiler_params=pltpu.CompilerParams(vmem_limit_bytes=28 * MIB),
        cost_estimate=pl.CostEstimate(
            flops=4 * count * size * depth * width,
            bytes_accessed=2 * depth * (2 * width + count * size),
            transcendentals=0,
        ),
    )(place, in_hbm(own), in_hbm(sibling), *blocks)


def hidden_kernel(layout, first, last, place_ref, *refs):
    total, count = 1 + max(copy[0] for unit in layout for copy in unit), len(layout)
    pieces, (gate_ref, up_ref, *rest) = refs[:total], refs[total:]
    if not first:
        gate_in, up_in, *rest = rest
    if last:
        weight_ref, hidden_ref, *rest = rest
    else:
        gate_out, up_out, *rest = rest
    rows_ref, gate_rows, up_rows, *rest, arrived, fetched, summed = rest
    sums = rest
    size, width = pieces[0].shape[1:]
    depth, columns = 2 * width, gate_ref.shape[1]
    tile = min(512, columns)
    copies = []
    for start, unit in enumerate(layout):
        for piece, entry, row, side in unit:
            column = pl.multiple_of(start * depth + (place_ref[count] + side) % 2 * width, 128)
            copies.append(
                pltpu.make_async_copy(
                    pieces[piece].at[entry],
                    rows_ref.at[pl.ds(row * size, size), pl.ds(column, width)],
                    arrived.at[len(copies)],
                )
            )

    def weight_copies(n, matrix):
        part = pl.ds(pl.multiple_of(n * tile, tile), tile)
        source, target = ((gate_ref, gate_rows), (up_ref, up_rows))[matrix]
        return [
            pltpu.make_async_copy(
                source.at[pl.ds(pl.multiple_of(place_ref[i] * depth + j * width, width), width), part],
                target.at[pl.ds(i * depth + j * width, width), part],
                fetched.at[n, matrix, i, j],
            )
            for i in range(count)
            for j in range(2)
        ]

    def sum_copy(n, matrix, out):
        part = pl.ds(pl.multiple_of(n * tile, tile), tile)
        here = sums[matrix].at[:, part]
        if out:
            there = (gate_out, up_out)[matrix].at[:, part]
            return pltpu.make_async_copy(here, there, summed.at[n, matrix, 1])
        there = (gate_in, up_in)[matrix].at[:, part]
        return pltpu.make_async_copy(there, here, summed.at[n, matrix, 0])

    steps = columns // tile
    for copy in copies:
        copy.start()
    for n in range(steps):
        for matrix in range(2):
            for copy in weight_copies(n, matrix):
                copy.start()
            if not first:
                sum_copy(n, matrix, False).start()
    for copy in copies:
        copy.wait()

    def step(n, _):
        inner = min(256, tile)
        for matrix in range(2):
            for copy in weight_copies(n, matrix):
                copy.wait()
            if not first:
                sum_copy(n, matrix, False).wait()
            for start in range(0, tile, inner):
                part = pl.ds(pl.multiple_of(n * tile + start, inner), inner)
                value = jnp.dot(
                    rows_ref[...], (gate_rows, up_rows)[matrix][:, part], preferred_element_type=F32
                )
                if not first:
                    value += sums[matrix][:, part]
                if last and matrix:
                    gate = sums[0][:, part]
                    hidden_ref[:, part] = (
                        weight_ref[...] * (gate / (1.0 + jnp.exp(-gate))) * value
                    ).astype(hidden_ref.dtype)
                else:
                    sums[matrix][:, part] = value
            if not last:
                sum_copy(n, matrix, True).start()
        return 0

    lax.fori_loop(0, steps, step, 0)
    if not last:
        for n in range(steps):
            for matrix in range(2):
                sum_copy(n, matrix, True).wait()


def hidden_part(units, places, side, pieces, w_gate, w_up, sums=None, weight=None):
    first, last = sums is None, weight is not None
    size, width = pieces[0].shape[1:]
    rows, columns, depth = 4 * size, w_gate.shape[1], 2 * width
    layout, piece = [], 0
    for unit in units:
        layout.append([])
        for core in range(2):
            for place_of in unit:
                for at, (sect, near) in enumerate(place_of):
                    layout[-1].append((piece, at, core * 2 + sect, near))
                piece += 1
    anywhere, vmem = pl.BlockSpec(memory_space=pl.ANY), pl.BlockSpec(memory_space=pltpu.VMEM)
    in_specs = [pl.BlockSpec(memory_space=pltpu.SMEM)] + [anywhere] * (len(pieces) + 2)
    operands = list(pieces) + [in_hbm(w_gate), in_hbm(w_up)]
    if not first:
        in_specs += [anywhere] * 2
        operands += list(sums)
    if last:
        in_specs += [vmem]
        operands += [weight]
        out_shape, out_specs = jax.ShapeDtypeStruct((rows, columns), BF16), vmem
    else:
        out_shape = [jax.ShapeDtypeStruct((rows, columns), F32)] * 2
        out_specs = [anywhere] * 2
    steps = columns // min(512, columns)
    return pl.pallas_call(
        functools.partial(hidden_kernel, layout, first, last),
        in_specs=in_specs,
        out_specs=out_specs,
        out_shape=out_shape,
        scratch_shapes=[pltpu.VMEM((rows, len(units) * depth), BF16)]
        + [pltpu.VMEM((len(units) * depth, columns), BF16)] * 2
        + [pltpu.VMEM((rows, columns), F32)] * 2
        + [
            pltpu.SemaphoreType.DMA((sum(len(unit) for unit in layout),)),
            pltpu.SemaphoreType.DMA((steps, 2, len(units), 2)),
            pltpu.SemaphoreType.DMA((steps, 2, 2)),
        ],
        compiler_params=pltpu.CompilerParams(vmem_limit_bytes=(12 + 10 * len(units)) * MIB),
        cost_estimate=pl.CostEstimate(
            flops=4 * rows * len(units) * depth * columns,
            bytes_accessed=4 * len(units) * depth * columns,
            transcendentals=rows * columns,
        ),
    )(jnp.stack(places + [side]).astype(jnp.int32), *operands)


def add(one, other):
    return (one.astype(F32) + other.astype(F32)).astype(BF16)


def on_device(
    queries,
    latent_cache,
    cache_len,
    value_up,
    out_proj,
    residual,
    w_gate,
    w_up,
    w_down,
    route_ids,
    route_weights,
):
    line = lax.axis_size("line")
    tp = lax.axis_size("tp")
    sect, at, side, core = (lax.axis_index(name) for name in ("sect", "line", "side", "core"))
    block = queries.shape[0]
    row_total, width = residual.shape
    chip_width = 2 * width
    shifts = list(range(line))

    own_proj = out_proj.T
    sibling_proj = swap(own_proj, "core")
    residual_rows = lax.dynamic_slice_in_dim(
        residual.reshape(line, 2, 2, block, width), sect * (line // 2), line // 2, 0
    )
    mine = lax.dynamic_index_in_dim(residual_rows, core, 2, keepdims=False)
    other = swap(lax.dynamic_index_in_dim(residual_rows, 1 - core, 2, keepdims=False), "core")
    residual_rows = jnp.where(
        core == 0, jnp.concatenate([mine, other], axis=3), jnp.concatenate([other, mine], axis=3)
    ).reshape(-1, chip_width)

    heads = attend(queries, latent_cache, cache_len, value_up)
    rights, lefts = [heads], [heads]
    for k in shifts[1:]:
        rights.append(
            lax.ppermute(rights[-1], "line", [(i, i + 1) for i in range(k - 1, line - 1)])
        )
        lefts.append(lax.ppermute(lefts[-1], "line", [(i, i - 1) for i in range(1, line - k + 1)]))
    near = [heads] + [value for pair in zip(rights[1:], lefts[1:]) for value in pair]
    holders = [range(line)] + [
        value for k in shifts[1:] for value in (range(k, line), range(line - k))
    ]
    far = [
        lax.ppermute(value, ("line", "side"), [(2 * i + y, 2 * i + 1 - y) for i in held for y in range(2)])
        for value, held in zip(near, holders)
    ]
    place = []
    for k in shifts:
        origin = jnp.where(at >= k, 2 * k - 1, 2 * (line - k)) if k else 0
        for y in range(2):
            place += [origin + y * len(near), 2 * ((at - k) % line) + (side + y) % 2]
    place = jnp.stack([jnp.int32(value) for value in place] + [core]).astype(jnp.int32)
    partial = project(
        place, 2 * line, near + far, own_proj, sibling_proj, F32 if tp > 1 else BF16
    )
    if tp > 1:
        partial = lax.psum(partial, "tp").astype(BF16)
    partial = partial.reshape(2, -1, chip_width)
    kept = lax.dynamic_index_in_dim(partial, sect, 0, keepdims=False)
    given = lax.dynamic_index_in_dim(partial, 1 - sect, 0, keepdims=False)
    attention = kept.astype(F32) + swap(given, "sect").astype(F32)
    own_rows = (residual_rows.astype(F32) + attention).astype(BF16)

    weight = jnp.sum(jnp.where(route_ids == lax.axis_index(GRP), route_weights, 0.0), axis=1)
    weight = weight.reshape(2, line // 2, 2, 2, block).transpose(3, 0, 1, 2, 4)
    weight = relative(relative(weight, 0, core), 1, sect).reshape(row_total, 1)
    got = {k: shift(own_rows, k) if k else own_rows for k in shifts if k != line // 2}
    right = lax.ppermute(got[1], "line", [(i, i + 1) for i in range(1, line - 1)])
    left = lax.ppermute(got[line - 1], "line", [(i, i - 1) for i in range(1, line - 1)])
    got[line // 2] = jnp.where(at >= line // 2, right, left)
    pairs, opposites = {}, {}
    half, back = line // 2, line - 1
    for k in (0, back, 1, half):
        first, second = ("sect", "side") if k % 2 == 0 else ("side", "sect")
        pairs[k] = jnp.stack([got[k], swap(got[k], first)])
        opposites[k] = swap(pairs[k], second)
    layout = [
        [[(0, 0), (1, 0)], [(0, 1), (1, 1)]] if k % 2 == 0 else [[(0, 0), (0, 1)], [(1, 0), (1, 1)]]
        for k in shifts
    ]
    sums = None
    for group in ([0], [back], [1, half]):
        if group == [back]:
            late = [opposites[k] for k in (back, 1, half)]
            late, sums = lax.optimization_barrier((late, sums))
            opposites.update(zip((back, 1, half), late))
        sums = hidden_part(
            [layout[k] for k in group],
            [(at - k) % line for k in group],
            side,
            [
                piece
                for k in group
                for piece in (
                    pairs[k], opposites[k], swap(pairs[k], "core"), swap(opposites[k], "core")
                )
            ],
            w_gate[0],
            w_up[0],
            sums,
            weight if half in group else None,
        )
    hidden = sums

    def own_side(value):
        return lax.dynamic_slice_in_dim(value, side * chip_width, chip_width, value.ndim - 1)

    def other_side(value):
        return lax.dynamic_slice_in_dim(value, (1 - side) * chip_width, chip_width, value.ndim - 1)

    count = row_total // 2
    send, keep = (
        jnp.dot(rows, w_down[0], preferred_element_type=F32) for rows in (hidden[count:], hidden[:count])
    )
    if tp > 1:
        send, keep = (lax.psum(v, "tp") for v in (send, keep))
    send, keep = send.astype(BF16), keep.astype(BF16)

    def columns_to(value, k):
        return lax.dynamic_slice_in_dim(value, (at + k) % line * 2 * chip_width, 2 * chip_width, 1)

    total, held = own_rows.astype(F32), None
    for group in ((half, 1), (back, 0)):
        arrived = swap(jnp.stack([columns_to(send, k) for k in group]), "core")
        if held is not None:
            arrived, held = lax.optimization_barrier((arrived, held))
        for k, arrival in zip(group, arrived):
            part = add(columns_to(keep, k), arrival).reshape(2, -1, 2 * chip_width)
            if k % 2 == 0:
                part = add(part[0], swap(part[1], "sect"))
                held = part
                part = add(own_side(part), swap(other_side(part), "side"))
            else:
                part = add(own_side(part), swap(other_side(part), "side"))
                part = add(part[0], swap(part[1], "sect"))
            total = total + (shift(part, k) if k else part).astype(F32)
    total = total.astype(BF16)

    mine = jnp.where(core == 0, total[:, :width], total[:, width:])
    other = swap(jnp.where(core == 0, total[:, width:], total[:, :width]), "core")
    out = relative(jnp.stack([mine, other]), 0, core).reshape(2, -1, block, width)
    out = out.transpose(1, 0, 2, 3).reshape(-1, width)
    share = out.shape[0] // tp
    return lax.dynamic_slice_in_dim(out, lax.axis_index("tp") * share, share, 0)


def solution(mesh):
    sizes = dict(mesh.shape)
    fine = Mesh(
        mesh.devices.reshape(sizes["sect"], sizes["grp"] // 4, 2, 2, sizes["tp"]),
        ("sect", "line", "side", "core", "tp"),
    )
    return jax.shard_map(
        on_device,
        mesh=fine,
        in_specs=(
            P(GRP, HID, None),
            P(GRP, None, None),
            P(GRP),
            P(HID, None, None),
            P(HID, GRP),
            P(None, GRP),
            P(GRP, None, HID),
            P(GRP, None, HID),
            P(GRP, HID, None),
            P(),
            P(),
        ),
        out_specs=P(HID, GRP),
        check_vma=False,
    )
```

time: 467 us -> 245 us (0.52)
  waiting for transfers between devices: 326 us -> 80.5 us
  starting transfers between devices: 6.1 us -> 72 us
  Pallas kernels: 0 us -> 43 us
  matrix products: 61.4 us -> 24.3 us
  local copies, waits for them, and re-layouts: 36.1 us -> 15.2 us
  other arithmetic: 24.2 us -> 7.9 us
  between operations: 13.3 us -> 0.92 us
    reduce_scatter x2 -> x0, waiting for transfers between devices: 127 us -> none  [the longest x1 111 us: on_device(): lax.psum_scatter(expert_term.astype(jnp.bfloat16), 'grp', scatter_dimensi...]
    all_to_all x1 -> x0, waiting for transfers between devices: 95.5 us -> none  [on_device(): lax.all_to_all(outgoing, 'grp', split_axis=0, concat_axis=2, tiled=True)]
    ppermute x0 -> x50, waiting for transfers between devices: none -> 80.5 us  [the longest x30 33.2 us: swap(): return lax.ppermute(value, axis, [(0, 1), (1, 0)])]
    all_gather x1 -> x0, waiting for transfers between devices: 72.7 us -> none  [on_device(): lax.all_gather(heads_out, 'grp', axis=0, tiled=True)]
    ppermute x0 -> x50, starting transfers between devices: none -> 72 us  [the longest x30 28.6 us: swap(): return lax.ppermute(value, axis, [(0, 1), (1, 0)])]
    pallas_call x0 -> x4, Pallas kernels: none -> 43 us  [the longest x3 29.1 us: hidden_part(): pl.pallas_call(functools.partial(hidden_kernel, layout, first, last), in_...]
    gather x2 -> x0, local copies, waits for them, and re-layouts: 33.8 us -> none  [pick_slots(): picked = jnp.take(source_rows, slot_rows, axis=0)]
    dot_general x6 -> x5, matrix products: 56.9 us -> 24.3 us  [the longest x2 8.79 us: on_device(): jnp.dot(rows, w_down[0], preferred_element_type=F32)]
  transfers between devices with their start and end apart: 5 -> 50, of which waited for: 5 -> 22; matrix products, arithmetic and copies ran while one was open for 3% -> 12% of each run, Pallas kernels for 0% -> 7%
where the time goes in v1:
time: 245 us; the launch traced here: 244 us
  waiting for transfers between devices  80.5 us (33%)
  starting transfers between devices  72 us (29%)
  Pallas kernels  43 us (18%)
  matrix products  24.3 us (10%)
  local copies, waits for them, and re-layouts  15.2 us (6%)
  other arithmetic  7.9 us (3%)
    ppermute x30, waiting for transfers between devices, swap(): return lax.ppermute(value, axis, [(0, 1), (1, 0)])  33.2 us
    pallas_call x3, Pallas kernels, hidden_part(): pl.pallas_call(functools.partial(hidden_kernel, layout, first, last), in_...  29.1 us
    ppermute x30, starting transfers between devices, swap(): return lax.ppermute(value, axis, [(0, 1), (1, 0)])  28.6 us
    ppermute x3, waiting for transfers between devices, on_device(): lax.ppermute(lefts[-1], 'line', [(i, i - 1) for i in range(1, line - k +...  15.7 us
    ppermute x7, starting transfers between devices, on_device(): lax.ppermute(value, ('line', 'side'), [(2 * i + y, 2 * i + 1 - y) for i i...  15.4 us
    ppermute x5, starting transfers between devices, shift(): lax.ppermute(value, 'line', [(i, (i + amount) % size) for i in range(size)])  14.8 us
    pallas_call x1, Pallas kernels, project(): pl.pallas_call(functools.partial(project_kernel, count), in_specs=[pl.Blo...  13.8 us
    unnamed x51, local copies, waits for them, and re-layouts  12.4 us
  transfers between devices with their start and end apart: 50, of which 22 were waited for; matrix products, arithmetic and copies ran while one was open for 12% of the time, Pallas kernels for 7%

profile of v1, /device:TPU:0, one launch (start us, length us, event | category | flops | bytes accessed | tf_op | source)
XLA Modules:
  0.0 243.8 jit_solution(11838836312586891006)
XLA Ops:
  1.8 3.5 %fusion.21 = f32[32,64,128]{2,1,0:T(8,128)S(1)} fusion(bf16[32,64,576]{2,1,0:T(8,128)(2,1)S(1)} %copy-done, bf16[32,128,576]{1,2,0:T(8,128)(2,1)} %param.12, pred[32,128]{1,0:T(8,128)(4,1)S(1)} %iota_compare_fusion), kind=kOutput, calls=%fused_computation.25 | convolution fusion | flops 302514176 | bytes 8130560 | tf_op jit(solution)/shard_map/rhk,rlk->rhl/dot_general | solution.py:38
  5.3 1.1 copy-done.17
  7.0 6.5 %fusion.11 = bf16[32,64,512]{2,1,0:T(8,128)(2,1)S(1)} fusion(bf16[32,128,576]{1,2,0:T(8,128)(2,1)} %param.12, f32[32,64]{1,0:T(8,128)S(1)} %fusion.33, f32[32,64,128]{2,1,0:T(8,128)} %copy-done.17, pred[32,128]{1,0:T(8,128)(4,1)S(1)} %iota_compare_fusion), kind=kOutput, calls=%fused_computation.8 | convolution fusion | flops 269486208 | bytes 8400896 | tf_op jit(solution)/shard_map/rhl,rlc->rhc/dot_general | solution.py:47
  13.6 5.4 %fusion.23 = bf16[64,4,8,128]{3,2,1,0:T(8,128)(2,1)S(1)} fusion(bf16[64,512,128]{2,1,0:T(8,128)(2,1)} %param.14, bf16[32,64,512]{2,1,0:T(8,128)(2,1)S(1)} %fusion.11), kind=kOutput, calls=%fused_computation.27 | convolution fusion | flops 268697600 | bytes 11010048 | tf_op jit(solution)/shard_map/rhc,hcv->rhv/dot_general | solution.py:50
  19.1 5.0 %collective-permute-start.2 = (bf16[32,8192]{1,0:T(8,128)(2,1)S(1)}, bf16[32,8192]{1,0:T(8,128)(2,1)S(1)}, u32[]{:S(2)}, u32[]{:S(2)}) collective-permute-start(bf16[32,8192]{1,0:T(8,128)(2,1)S(1)} %bitcast.111), channel_id=1, source_target_pairs={{0,4},{4,8},{8,12},{1,5},{5,9},{9,13},{2,6},{6,10},{10,14},{3,7},{... | collective-permute-start | bytes 1572872 | tf_op jit(solution)/shard_map/ppermute | solution.py:315
  24.1 1.3 collective-permute-start.3
  25.4 1.6 collective-permute-start.8
  27.0 8.2 %collective-permute-done.2.refs_1_ = bf16[32,8192]{1,0:T(8,128)(2,1)S(1)} collective-permute-done((bf16[32,8192]{1,0:T(8,128)(2,1)S(1)}, bf16[32,8192]{1,0:T(8,128)(2,1)S(1)}, u32[]{:S(2)}, u32[]{:S(2)}) %collective-permute-start.2) | collective-permute-done | bytes 524320 | tf_op jit(solution)/shard_map/ppermute | solution.py:315
  35.9 3.5 %collective-permute-done.3.refs_2_ = bf16[32,8192]{1,0:T(8,128)(2,1)S(1)} collective-permute-done((bf16[32,8192]{1,0:T(8,128)(2,1)S(1)}, bf16[32,8192]{1,0:T(8,128)(2,1)S(1)}, u32[]{:S(2)}, u32[]{:S(2)}) %collective-permute-start.3) | collective-permute-done | bytes 524320 | tf_op jit(solution)/shard_map/ppermute | solution.py:317
  39.3 1.3 collective-permute-start.5
  40.6 3.4 %collective-permute-start.10 = (bf16[32,8192]{1,0:T(8,128)(2,1)S(1)}, bf16[32,8192]{1,0:T(8,128)(2,1)S(1)}, u32[]{:S(2)}, u32[]{:S(2)}) collective-permute-start(bf16[32,8192]{1,0:T(8,128)(2,1)S(1)} %collective-permute-done.3.refs_2_), channel_id=1, source_target_pairs={{0,2},{2,0},{4,6},{6,4},{8,10},{10,8},{1,3},{3,1},{5,7},{7,5},{9,1... | collective-permute-start | bytes 1572872 | tf_op jit(solution)/shard_map/ppermute | solution.py:323
  44.8 1.5 collective-permute-start.6
  46.3 7.7 %collective-permute-done.5.refs_4_ = bf16[32,8192]{1,0:T(8,128)(2,1)} collective-permute-done((bf16[32,8192]{1,0:T(8,128)(2,1)S(1)}, bf16[32,8192]{1,0:T(8,128)(2,1)}, u32[]{:S(2)}, u32[]{:S(2)}) %collective-permute-start.5) | collective-permute-done | bytes 524320 | tf_op jit(solution)/shard_map/ppermute | solution.py:317
  54.0 1.3 collective-permute-start.7
  56.1 1.5 collective-permute-start.11
  58.3 3.4 %collective-permute-start.12 = (bf16[32,8192]{1,0:T(8,128)(2,1)}, bf16[32,8192]{1,0:T(8,128)(2,1)}, u32[]{:S(2)}, u32[]{:S(2)}) collective-permute-start(bf16[32,8192]{1,0:T(8,128)(2,1)} %collective-permute-done.5.refs_4_), channel_id=1, source_target_pairs={{0,2},{2,0},{4,6},{6,4},{1,3},{3,1},{5,7},{7,5},{16,18},{18,16},{2... | collective-permute-start | bytes 1572872 | tf_op jit(solution)/shard_map/ppermute | solution.py:323
  61.8 1.5 collective-permute-start.13
  63.2 4.6 %collective-permute-done.7.refs_6_ = bf16[32,8192]{1,0:T(8,128)(2,1)} collective-permute-done((bf16[32,8192]{1,0:T(8,128)(2,1)}, bf16[32,8192]{1,0:T(8,128)(2,1)}, u32[]{:S(2)}, u32[]{:S(2)}) %collective-permute-start.7) | collective-permute-done | bytes 524320 | tf_op jit(solution)/shard_map/ppermute | solution.py:317
  67.9 3.4 %collective-permute-start.14 = (bf16[32,8192]{1,0:T(8,128)(2,1)}, bf16[32,8192]{1,0:T(8,128)(2,1)}, u32[]{:S(2)}, u32[]{:S(2)}) collective-permute-start(bf16[32,8192]{1,0:T(8,128)(2,1)} %collective-permute-done.7.refs_6_), channel_id=1, source_target_pairs={{0,2},{2,0},{1,3},{3,1},{16,18},{18,16},{17,19},{19,17}} | collective-permute-start | bytes 1572872 | tf_op jit(solution)/shard_map/ppermute | solution.py:323
  71.4 1.0 copy.16
  72.5 2.3 collective-permute-done.12.refs_11_
  74.8 8.7 %collective-permute-done.14.refs_13_ = bf16[32,8192]{1,0:T(8,128)(2,1)} collective-permute-done((bf16[32,8192]{1,0:T(8,128)(2,1)}, bf16[32,8192]{1,0:T(8,128)(2,1)}, u32[]{:S(2)}, u32[]{:S(2)}) %collective-permute-start.14) | collective-permute-done | bytes 524320 | tf_op jit(solution)/shard_map/ppermute | solution.py:323
  83.5 1.0 copy-done.8
  84.5 1.0 copy-done.10
  85.6 13.8 %shard_map.109 = bf16[256,896]{1,0:T(8,128)(2,1)S(1)} custom-call(s32[17]{0:T(128)S(1)} %stack.152.place_ref, bf16[448,8192]{1,0:T(8,128)(2,1)} %bitcast.124, bf16[448,8192]{1,0:T(8,128)(2,1)} %collective-permute-done.1.sibling_ref, bf16[32,8192]{1,0:T(8,128)(2,1)S(1)} %bitcast.114, bf16[32,8192]{1,0:T(8,128)(2,1)S(1)} %collective-permute-done.2.refs_1_, ...), custom_call_target="tpu_custom_call" | custom-call | flops 3758096384 | bytes 18874368 | tf_op jit(solution)/shard_map/pallas_call | solution.py:114
  99.5 1.5 collective-permute-start.15
  101.1 1.3 collective-permute-done
  102.4 3.2 %collective-permute-done.15 = bf16[128,896]{1,0:T(8,128)(2,1)S(1)} collective-permute-done((bf16[128,896]{1,0:T(8,128)(2,1)S(1)}, bf16[128,896]{1,0:T(8,128)(2,1)S(1)}, u32[]{:S(2)}, u32[]{:S(2)}) %collective-permute-start.15) | collective-permute-done | bytes 229408 | tf_op jit(solution)/shard_map/ppermute | solution.py:24
  105.9 3.8 %collective-permute-start.18 = (bf16[128,896]{1,0:T(8,128)(2,1)S(1)}, bf16[128,896]{1,0:T(8,128)(2,1)S(1)}, u32[]{:S(2)}, u32[]{:S(2)}) collective-permute-start(bf16[128,896]{1,0:T(8,128)(2,1)S(1)} %fusion.30), channel_id=1, source_target_pairs={{0,12},{4,0},{8,4},{12,8},{1,13},{5,1},{9,5},{13,9},{2,14},{6,2},{... | collective-permute-start | bytes 688136 | tf_op jit(solution)/shard_map/ppermute | solution.py:29
  109.7 1.4 collective-permute-start.26
  111.1 3.6 %collective-permute-done.16 = bf16[128,896]{1,0:T(8,128)(2,1)S(1)} collective-permute-done((bf16[128,896]{1,0:T(8,128)(2,1)S(1)}, bf16[128,896]{1,0:T(8,128)(2,1)S(1)}, u32[]{:S(2)}, u32[]{:S(2)}) %collective-permute-start.16) | collective-permute-done | bytes 229408 | tf_op jit(solution)/shard_map/ppermute | solution.py:29
  115.4 1.5 collective-permute-start.23
  117.0 1.7 collective-permute-start.27
  119.4 1.6 collective-permute-start.17
  121.0 2.3 collective-permute-done.23
  123.4 3.6 %collective-permute-start.24 = (bf16[128,896]{1,0:T(8,128)(2,1)S(1)}, bf16[128,896]{1,0:T(8,128)(2,1)S(1)}, u32[]{:S(2)}, u32[]{:S(2)}) collective-permute-start(bf16[128,896]{1,0:T(8,128)(2,1)S(1)} %broadcast_select_fusion), channel_id=1, source_target_pairs={{0,16},{16,0},{1,17},{17,1},{2,18},{18,2},{3,19},{19,3},{4,20},{20... | collective-permute-start | bytes 688136 | tf_op jit(solution)/shard_map/ppermute | solution.py:24
  126.9 2.5 %collective-permute-done.27.refs_1_ = bf16[2,128,896]{2,1,0:T(8,128)(2,1)S(1)} collective-permute-done((bf16[2,128,896]{2,1,0:T(8,128)(2,1)S(1)}, bf16[2,128,896]{2,1,0:T(8,128)(2,1)S(1)}, u32[]{:S(2)}, u32[]{:S(2)}) %collective-permute-start.27) | collective-permute-done | bytes 458784 | tf_op jit(solution)/shard_map/ppermute | solution.py:24
  129.4 3.5 %collective-permute-done.19 = bf16[128,896]{1,0:T(8,128)(2,1)S(1)} collective-permute-done((bf16[128,896]{1,0:T(8,128)(2,1)S(1)}, bf16[128,896]{1,0:T(8,128)(2,1)S(1)}, u32[]{:S(2)}, u32[]{:S(2)}) %collective-permute-start.19) | collective-permute-done | bytes 229408 | tf_op jit(solution)/shard_map/ppermute | solution.py:24
  133.8 1.6 collective-permute-done.17
  136.3 1.8 collective-permute-start.25
  140.2 7.7 %shard_map.110 = (f32[512,1024]{1,0:T(8,128)S(1)}, f32[512,1024]{1,0:T(8,128)S(1)}) custom-call(s32[2]{0:T(128)S(1)} %pad_add_fusion.1.place_ref, bf16[2,128,896]{2,1,0:T(8,128)(2,1)S(1)} %copy-done.5, bf16[2,128,896]{2,1,0:T(8,128)(2,1)S(1)} %copy-done.12, bf16[2,128,896]{2,1,0:T(8,128)(2,1)S(1)} %collective-permute-done.28.refs_2_, ...), custom_call_target="tpu_custom_call" | custom-call | flops 3758096384 | bytes 7340032 | tf_op jit(solution)/shard_map/pallas_call | solution.py:253
  147.9 1.3 copy-done.2
  149.2 3.2 %collective-permute-done.21.refs_1_ = bf16[2,128,896]{2,1,0:T(8,128)(2,1)} collective-permute-done((bf16[2,128,896]{2,1,0:T(8,128)(2,1)S(1)}, bf16[2,128,896]{2,1,0:T(8,128)(2,1)}, u32[]{:S(2)}, u32[]{:S(2)}) %collective-permute-start.21) | collective-permute-done | bytes 458784 | tf_op jit(solution)/shard_map/ppermute | solution.py:24
  154.7 1.6 copy-done.3
  156.3 8.9 %shard_map.111 = (f32[512,1024]{1,0:T(8,128)S(1)}, f32[512,1024]{1,0:T(8,128)S(1)}) custom-call(s32[2]{0:T(128)S(1)} %pad_add_fusion.2.place_ref, bf16[2,128,896]{2,1,0:T(8,128)(2,1)S(1)} %pad_maximum_fusion.3.refs_0_, bf16[2,128,896]{2,1,0:T(8,128)(2,1)} %collective-permute-done.20.refs_1_, bf16[2,128,896]{2,1,0:T(8,128)(2,1)} %collective-permute-done.34.refs_2_, ...), custom_call_target="tpu_custom_call" | custom-call | flops 3758096384 | bytes 7340032 | tf_op jit(solution)/shard_map/pallas_call | solution.py:253
  165.3 12.5 %shard_map.112 = bf16[512,1024]{1,0:T(8,128)(2,1)S(1)} custom-call(s32[3]{0:T(128)S(1)} %pad_add_fusion.place_ref, bf16[2,128,896]{2,1,0:T(8,128)(2,1)S(1)} %pad_maximum_fusion.2.refs_0_, bf16[2,128,896]{2,1,0:T(8,128)(2,1)} %collective-permute-done.21.refs_1_, bf16[2,128,896]{2,1,0:T(8,128)(2,1)S(1)} %collective-permute-done.30.refs_2_, ...), custom_call_target="tpu_custom_call" | custom-call | flops 7516192768 | bytes 14680064 | tf_op jit(solution)/shard_map/pallas_call | solution.py:253
  177.9 4.3 %fusion.8 = bf16[256,7168]{1,0:T(8,128)(2,1)S(1)} fusion(bf16[1,1024,7168]{2,1,0:T(8,128)(2,1)S(1)} %bitcast.145, bf16[512,1024]{1,0:T(8,128)(2,1)S(1)} %shard_map.112), kind=kOutput, calls=%fused_computation.6 | convolution fusion | flops 3759931392 | bytes 18874368 | tf_op jit(solution)/shard_map/dot_general | solution.py:392
  183.2 1.4 pad_maximum_fusion.1
  184.7 4.5 %fusion.5 = bf16[256,7168]{1,0:T(8,128)(2,1)S(1)} fusion(bf16[1,1024,7168]{2,1,0:T(8,128)(2,1)S(1)} %bitcast.145, bf16[512,1024]{1,0:T(8,128)(2,1)S(1)} %shard_map.112), kind=kOutput, calls=%fused_computation.5 | convolution fusion | flops 3759931392 | bytes 18874368 | tf_op jit(solution)/shard_map/dot_general | solution.py:392
  189.7 1.3 copy-done.13
  192.0 2.6 %collective-permute-start.40 = (bf16[2,128,896]{2,1,0:T(8,128)(2,1)S(1)}, bf16[2,128,896]{2,1,0:T(8,128)(2,1)S(1)}, u32[]{:S(2)}, u32[]{:S(2)}) collective-permute-start(bf16[2,128,896]{2,1,0:T(8,128)(2,1)S(1)} %constant_dynamic-slice_fusion.2), channel_id=1, source_target_pairs={{0,2},{2,0},{1,3},{3,1},{4,6},{6,4},{5,7},{7,5},{8,10},{10,8},{9,1... | collective-permute-start | bytes 1376264 | tf_op jit(solution)/shard_map/ppermute | solution.py:24
  194.6 9.4 %collective-permute-done.37 = bf16[128,1792]{1,0:T(8,128)(2,1)S(1)} collective-permute-done((bf16[128,1792]{1,0:T(8,128)(2,1)S(1)}, bf16[128,1792]{1,0:T(8,128)(2,1)S(1)}, u32[]{:S(2)}, u32[]{:S(2)}) %collective-permute-start.37) | collective-permute-done | bytes 458784 | tf_op jit(solution)/shard_map/ppermute | solution.py:24
  204.1 2.4 %fusion.14 = (bf16[256,1792]{1,0:T(8,128)(2,1)S(1)}, bf16[256,1792]{1,0:T(8,128)(2,1)S(1)}) fusion(bf16[2,256,1792]{2,1,0:T(8,128)(2,1)} %collective-permute-done.43, bf16[256,7168]{1,0:T(8,128)(2,1)} %copy-done.13, s32[]{:T(128)S(6)} %select_n.239, s32[]{:T(128)S(6)} %select_n.238), kind=kLoop, calls=%fused_computation.14 | loop fusion | flops 3670016 | bytes 5505032 | tf_op jit(solution)/shard_map/convert_element_type | solution.py:276
  207.5 2.5 %collective-permute-start.38 = (bf16[128,896]{1,0:T(8,128)(2,1)S(1)}, bf16[128,896]{1,0:T(8,128)(2,1)S(1)}, u32[]{:S(2)}, u32[]{:S(2)}) collective-permute-start(bf16[128,896]{1,0:T(8,128)(2,1)S(1)} %constant_dynamic-slice_fusion.3), channel_id=1, source_target_pairs={{0,2},{2,0},{1,3},{3,1},{4,6},{6,4},{5,7},{7,5},{8,10},{10,8},{9,1... | collective-permute-start | bytes 688136 | tf_op jit(solution)/shard_map/ppermute | solution.py:24
  210.2 1.3 collective-permute-start.41
  211.6 4.9 %collective-permute-done.38 = bf16[128,896]{1,0:T(8,128)(2,1)S(1)} collective-permute-done((bf16[128,896]{1,0:T(8,128)(2,1)S(1)}, bf16[128,896]{1,0:T(8,128)(2,1)S(1)}, u32[]{:S(2)}, u32[]{:S(2)}) %collective-permute-start.38) | collective-permute-done | bytes 229408 | tf_op jit(solution)/shard_map/ppermute | solution.py:24
  216.7 6.7 %collective-permute-start.39 = (bf16[128,896]{1,0:T(8,128)(2,1)S(1)}, bf16[128,896]{1,0:T(8,128)(2,1)S(1)}, u32[]{:S(2)}, u32[]{:S(2)}) collective-permute-start(bf16[128,896]{1,0:T(8,128)(2,1)S(1)} %add_convert_fusion.6), channel_id=1, source_target_pairs={{0,8},{4,12},{8,0},{12,4},{1,9},{5,13},{9,1},{13,5},{2,10},{6,14},... | collective-permute-start | bytes 688136 | tf_op jit(solution)/shard_map/ppermute | solution.py:29
  223.7 4.3 %collective-permute-start.42 = (bf16[128,896]{1,0:T(8,128)(2,1)S(1)}, bf16[128,896]{1,0:T(8,128)(2,1)S(1)}, u32[]{:S(2)}, u32[]{:S(2)}) collective-permute-start(bf16[128,896]{1,0:T(8,128)(2,1)S(1)} %fusion.28), channel_id=1, source_target_pairs={{0,4},{4,8},{8,12},{12,0},{1,5},{5,9},{9,13},{13,1},{2,6},{6,10},{... | collective-permute-start | bytes 688136 | tf_op jit(solution)/shard_map/ppermute | solution.py:29
  228.2 1.8 collective-permute-start.45
  230.1 2.6 %collective-permute-start.48 = (bf16[128,896]{1,0:T(8,128)(2,1)S(1)}, bf16[128,896]{1,0:T(8,128)(2,1)S(1)}, u32[]{:S(2)}, u32[]{:S(2)}) collective-permute-start(bf16[128,896]{1,0:T(8,128)(2,1)S(1)} %constant_dynamic-slice_fusion), channel_id=1, source_target_pairs={{0,2},{2,0},{1,3},{3,1},{4,6},{6,4},{5,7},{7,5},{8,10},{10,8},{9,1... | collective-permute-start | bytes 688136 | tf_op jit(solution)/shard_map/ppermute | solution.py:24
  232.7 1.6 collective-permute-done.45
  234.4 2.0 collective-permute-done.39
  236.7 4.5 %collective-permute-done.46 = bf16[128,896]{1,0:T(8,128)(2,1)S(1)} collective-permute-done((bf16[128,896]{1,0:T(8,128)(2,1)S(1)}, bf16[128,896]{1,0:T(8,128)(2,1)S(1)}, u32[]{:S(2)}, u32[]{:S(2)}) %collective-permute-start.46) | collective-permute-done | bytes 229408 | tf_op jit(solution)/shard_map/ppermute | solution.py:29
  241.6 1.3 collective-permute-done.49
  (145 shorter events, 20.1 us)
Async XLA Ops:
  0.0 83.5 %collective-permute-start.1 = (bf16[448,8192]{1,0:T(8,128)(2,1)}, bf16[448,8192]{1,0:T(8,128)(2,1)}, u32[]{:S(2)}, u32[]{:S(2)}) collective-permute-start(bf16[448,8192]{1,0:T(8,128)(2,1)} %bitcast.123), channel_id=1, source_target_pairs={{0,1},{1,0},{2,3},{3,2},{4,5},{5,4},{6,7},{7,6},{8,9},{9,8},{10,11... | collective-permute-start | bytes 22020104 | tf_op jit(solution)/shard_map/ppermute | solution.py:24
  13.6 57.8 %copy-start.18 = (bf16[512,448]{0,1:T(8,128)(2,1)S(1)}, bf16[512,448]{0,1:T(8,128)(2,1)}, u32[]{:S(2)}) copy-start(bf16[512,448]{0,1:T(8,128)(2,1)} %param.16) | copy-start | bytes 1376260
  19.1 16.1 %collective-permute-start.2 = (bf16[32,8192]{1,0:T(8,128)(2,1)S(1)}, bf16[32,8192]{1,0:T(8,128)(2,1)S(1)}, u32[]{:S(2)}, u32[]{:S(2)}) collective-permute-start(bf16[32,8192]{1,0:T(8,128)(2,1)S(1)} %bitcast.111), channel_id=1, source_target_pairs={{0,4},{4,8},{8,12},{1,5},{5,9},{9,13},{2,6},{6,10},{10,14},{3,7},{... | collective-permute-start | bytes 1572872 | tf_op jit(solution)/shard_map/ppermute | solution.py:315
  24.1 15.3 %collective-permute-start.3 = (bf16[32,8192]{1,0:T(8,128)(2,1)S(1)}, bf16[32,8192]{1,0:T(8,128)(2,1)S(1)}, u32[]{:S(2)}, u32[]{:S(2)}) collective-permute-start(bf16[32,8192]{1,0:T(8,128)(2,1)S(1)} %bitcast.112), channel_id=1, source_target_pairs={{4,0},{8,4},{12,8},{5,1},{9,5},{13,9},{6,2},{10,6},{14,10},{7,3},{... | collective-permute-start | bytes 1572872 | tf_op jit(solution)/shard_map/ppermute | solution.py:317
  25.4 18.7 %collective-permute-start.8 = (bf16[32,8192]{1,0:T(8,128)(2,1)S(1)}, bf16[32,8192]{1,0:T(8,128)(2,1)S(1)}, u32[]{:S(2)}, u32[]{:S(2)}) collective-permute-start(bf16[32,8192]{1,0:T(8,128)(2,1)S(1)} %bitcast.113), channel_id=1, source_target_pairs={{0,2},{2,0},{4,6},{6,4},{8,10},{10,8},{12,14},{14,12},{1,3},{3,1},... | collective-permute-start | bytes 1572872 | tf_op jit(solution)/shard_map/ppermute | solution.py:323
  35.2 9.6 %collective-permute-start.4 = (bf16[32,8192]{1,0:T(8,128)(2,1)S(1)}, bf16[32,8192]{1,0:T(8,128)(2,1)S(1)}, u32[]{:S(2)}, u32[]{:S(2)}) collective-permute-start(bf16[32,8192]{1,0:T(8,128)(2,1)S(1)} %collective-permute-done.2.refs_1_), channel_id=1, source_target_pairs={{4,8},{8,12},{5,9},{9,13},{6,10},{10,14},{7,11},{11,15},{20,24},{2... | collective-permute-start | bytes 1572872 | tf_op jit(solution)/shard_map/ppermute | solution.py:315
  39.3 14.6 %collective-permute-start.5 = (bf16[32,8192]{1,0:T(8,128)(2,1)S(1)}, bf16[32,8192]{1,0:T(8,128)(2,1)}, u32[]{:S(2)}, u32[]{:S(2)}) collective-permute-start(bf16[32,8192]{1,0:T(8,128)(2,1)S(1)} %collective-permute-done.3.refs_2_), channel_id=1, source_target_pairs={{4,0},{8,4},{5,1},{9,5},{6,2},{10,6},{7,3},{11,7},{20,16},{24,20},... | collective-permute-start | bytes 1572872 | tf_op jit(solution)/shard_map/ppermute | solution.py:317
  40.6 14.6 %collective-permute-start.10 = (bf16[32,8192]{1,0:T(8,128)(2,1)S(1)}, bf16[32,8192]{1,0:T(8,128)(2,1)S(1)}, u32[]{:S(2)}, u32[]{:S(2)}) collective-permute-start(bf16[32,8192]{1,0:T(8,128)(2,1)S(1)} %collective-permute-done.3.refs_2_), channel_id=1, source_target_pairs={{0,2},{2,0},{4,6},{6,4},{8,10},{10,8},{1,3},{3,1},{5,7},{7,5},{9,1... | collective-permute-start | bytes 1572872 | tf_op jit(solution)/shard_map/ppermute | solution.py:323
  44.1 13.5 %collective-permute-start.9 = (bf16[32,8192]{1,0:T(8,128)(2,1)S(1)}, bf16[32,8192]{1,0:T(8,128)(2,1)S(1)}, u32[]{:S(2)}, u32[]{:S(2)}) collective-permute-start(bf16[32,8192]{1,0:T(8,128)(2,1)S(1)} %collective-permute-done.2.refs_1_), channel_id=1, source_target_pairs={{4,6},{6,4},{8,10},{10,8},{12,14},{14,12},{5,7},{7,5},{9,11},{11,9... | collective-permute-start | bytes 1572872 | tf_op jit(solution)/shard_map/ppermute | solution.py:323
  44.8 17.0 %collective-permute-start.6 = (bf16[32,8192]{1,0:T(8,128)(2,1)S(1)}, bf16[32,8192]{1,0:T(8,128)(2,1)}, u32[]{:S(2)}, u32[]{:S(2)}) collective-permute-start(bf16[32,8192]{1,0:T(8,128)(2,1)S(1)} %collective-permute-done.4.refs_3_), channel_id=1, source_target_pairs={{8,12},{9,13},{10,14},{11,15},{24,28},{25,29},{26,30},{27,31}} | collective-permute-start | bytes 1572872 | tf_op jit(solution)/shard_map/ppermute | solution.py:315
  54.0 13.9 %collective-permute-start.7 = (bf16[32,8192]{1,0:T(8,128)(2,1)}, bf16[32,8192]{1,0:T(8,128)(2,1)}, u32[]{:S(2)}, u32[]{:S(2)}) collective-permute-start(bf16[32,8192]{1,0:T(8,128)(2,1)} %collective-permute-done.5.refs_4_), channel_id=1, source_target_pairs={{4,0},{5,1},{6,2},{7,3},{20,16},{21,17},{22,18},{23,19}} | collective-permute-start | bytes 1572872 | tf_op jit(solution)/shard_map/ppermute | solution.py:317
  56.1 16.5 %collective-permute-start.11 = (bf16[32,8192]{1,0:T(8,128)(2,1)S(1)}, bf16[32,8192]{1,0:T(8,128)(2,1)}, u32[]{:S(2)}, u32[]{:S(2)}) collective-permute-start(bf16[32,8192]{1,0:T(8,128)(2,1)S(1)} %collective-permute-done.4.refs_3_), channel_id=1, source_target_pairs={{8,10},{10,8},{12,14},{14,12},{9,11},{11,9},{13,15},{15,13},{24,26... | collective-permute-start | bytes 1572872 | tf_op jit(solution)/shard_map/ppermute | solution.py:323
  58.3 16.5 %collective-permute-start.12 = (bf16[32,8192]{1,0:T(8,128)(2,1)}, bf16[32,8192]{1,0:T(8,128)(2,1)}, u32[]{:S(2)}, u32[]{:S(2)}) collective-permute-start(bf16[32,8192]{1,0:T(8,128)(2,1)} %collective-permute-done.5.refs_4_), channel_id=1, source_target_pairs={{0,2},{2,0},{4,6},{6,4},{1,3},{3,1},{5,7},{7,5},{16,18},{18,16},{2... | collective-permute-start | bytes 1572872 | tf_op jit(solution)/shard_map/ppermute | solution.py:323
  61.8 13.1 %collective-permute-start.13 = (bf16[32,8192]{1,0:T(8,128)(2,1)}, bf16[32,8192]{1,0:T(8,128)(2,1)}, u32[]{:S(2)}, u32[]{:S(2)}) collective-permute-start(bf16[32,8192]{1,0:T(8,128)(2,1)} %collective-permute-done.6.refs_5_), channel_id=1, source_target_pairs={{12,14},{14,12},{13,15},{15,13},{28,30},{30,28},{29,31},{31,29}} | collective-permute-start | bytes 1572872 | tf_op jit(solution)/shard_map/ppermute | solution.py:323
  67.9 15.6 %collective-permute-start.14 = (bf16[32,8192]{1,0:T(8,128)(2,1)}, bf16[32,8192]{1,0:T(8,128)(2,1)}, u32[]{:S(2)}, u32[]{:S(2)}) collective-permute-start(bf16[32,8192]{1,0:T(8,128)(2,1)} %collective-permute-done.7.refs_6_), channel_id=1, source_target_pairs={{0,2},{2,0},{1,3},{3,1},{16,18},{18,16},{17,19},{19,17}} | collective-permute-start | bytes 1572872 | tf_op jit(solution)/shard_map/ppermute | solution.py:323
  85.6 15.4 %copy-start.16 = (bf16[512,448]{1,0:T(8,128)(2,1)S(1)}, bf16[512,448]{1,0:T(8,128)(2,1)}, u32[]{:S(2)}) copy-start(bf16[512,448]{1,0:T(8,128)(2,1)} %copy.16) | copy-start | bytes 1376260
  99.4 19.3 %copy-start.19 = (f32[512,8]{0,1:T(8,128)S(1)}, f32[512,8]{0,1:T(8,128)}, u32[]{:S(2)}) copy-start(f32[512,8]{0,1:T(8,128)} %param.21) | copy-start | bytes 49156
  99.4 19.2 %copy-start.20 = (s32[512,8]{0,1:T(8,128)S(1)}, s32[512,8]{0,1:T(8,128)}, u32[]{:S(2)}) copy-start(s32[512,8]{0,1:T(8,128)} %param.20) | copy-start | bytes 49156
  99.5 6.1 %collective-permute-start.15 = (bf16[128,896]{1,0:T(8,128)(2,1)S(1)}, bf16[128,896]{1,0:T(8,128)(2,1)S(1)}, u32[]{:S(2)}, u32[]{:S(2)}) collective-permute-start(bf16[128,896]{1,0:T(8,128)(2,1)S(1)} %dynamic-slice_bitcast_fusion.4), channel_id=1, source_target_pairs={{0,16},{16,0},{1,17},{17,1},{2,18},{18,2},{3,19},{19,3},{4,20},{20... | collective-permute-start | bytes 688136 | tf_op jit(solution)/shard_map/ppermute | solution.py:24
  101.0 1.4 collective-permute-start
  105.8 11.1 %copy-start.14 = (bf16[128,896]{1,0:T(8,128)(2,1)}, bf16[128,896]{1,0:T(8,128)(2,1)S(1)}, u32[]{:S(2)}) copy-start(bf16[128,896]{1,0:T(8,128)(2,1)S(1)} %fusion.30) | copy-start | bytes 688132
  105.8 8.9 %collective-permute-start.16 = (bf16[128,896]{1,0:T(8,128)(2,1)S(1)}, bf16[128,896]{1,0:T(8,128)(2,1)S(1)}, u32[]{:S(2)}, u32[]{:S(2)}) collective-permute-start(bf16[128,896]{1,0:T(8,128)(2,1)S(1)} %fusion.30), channel_id=1, source_target_pairs={{0,4},{4,8},{8,12},{12,0},{1,5},{5,9},{9,13},{13,1},{2,6},{6,10},{... | collective-permute-start | bytes 688136 | tf_op jit(solution)/shard_map/ppermute | solution.py:29
  105.9 9.5 %collective-permute-start.18 = (bf16[128,896]{1,0:T(8,128)(2,1)S(1)}, bf16[128,896]{1,0:T(8,128)(2,1)S(1)}, u32[]{:S(2)}, u32[]{:S(2)}) collective-permute-start(bf16[128,896]{1,0:T(8,128)(2,1)S(1)} %fusion.30), channel_id=1, source_target_pairs={{0,12},{4,0},{8,4},{12,8},{1,13},{5,1},{9,5},{13,9},{2,14},{6,2},{... | collective-permute-start | bytes 688136 | tf_op jit(solution)/shard_map/ppermute | solution.py:29
  109.7 7.2 %collective-permute-start.26 = (bf16[128,896]{1,0:T(8,128)(2,1)S(1)}, bf16[128,896]{1,0:T(8,128)(2,1)S(1)}, u32[]{:S(2)}, u32[]{:S(2)}) collective-permute-start(bf16[128,896]{1,0:T(8,128)(2,1)S(1)} %fusion.30), channel_id=1, source_target_pairs={{0,16},{16,0},{1,17},{17,1},{2,18},{18,2},{3,19},{19,3},{4,20},{20... | collective-permute-start | bytes 688136 | tf_op jit(solution)/shard_map/ppermute | solution.py:24
  114.7 4.6 %collective-permute-start.22 = (bf16[128,896]{1,0:T(8,128)(2,1)S(1)}, bf16[128,896]{1,0:T(8,128)(2,1)S(1)}, u32[]{:S(2)}, u32[]{:S(2)}) collective-permute-start(bf16[128,896]{1,0:T(8,128)(2,1)S(1)} %collective-permute-done.16), channel_id=1, source_target_pairs={{4,8},{8,12},{5,9},{9,13},{6,10},{10,14},{7,11},{11,15},{20,24},{2... | collective-permute-start | bytes 688136 | tf_op jit(solution)/shard_map/ppermute | solution.py:347
  115.4 7.9 %collective-permute-start.23 = (bf16[128,896]{1,0:T(8,128)(2,1)S(1)}, bf16[128,896]{1,0:T(8,128)(2,1)S(1)}, u32[]{:S(2)}, u32[]{:S(2)}) collective-permute-start(bf16[128,896]{1,0:T(8,128)(2,1)S(1)} %collective-permute-done.18), channel_id=1, source_target_pairs={{4,0},{8,4},{5,1},{9,5},{6,2},{10,6},{7,3},{11,7},{20,16},{24,20},... | collective-permute-start | bytes 688136 | tf_op jit(solution)/shard_map/ppermute | solution.py:348
  117.0 21.2 %copy-start.4 = (bf16[2,128,896]{2,1,0:T(8,128)(2,1)}, bf16[2,128,896]{2,1,0:T(8,128)(2,1)S(1)}, u32[]{:S(2)}) copy-start(bf16[2,128,896]{2,1,0:T(8,128)(2,1)S(1)} %pad_maximum_fusion.5.refs_0_) | copy-start | bytes 1376260
  117.0 12.4 %collective-permute-start.27 = (bf16[2,128,896]{2,1,0:T(8,128)(2,1)S(1)}, bf16[2,128,896]{2,1,0:T(8,128)(2,1)S(1)}, u32[]{:S(2)}, u32[]{:S(2)}) collective-permute-start(bf16[2,128,896]{2,1,0:T(8,128)(2,1)S(1)} %pad_maximum_fusion.5.refs_0_), channel_id=1, source_target_pairs={{0,2},{2,0},{1,3},{3,1},{4,6},{6,4},{5,7},{7,5},{8,10},{10,8},{9,1... | collective-permute-start | bytes 1376264 | tf_op jit(solution)/shard_map/ppermute | solution.py:24
  118.8 19.3 %collective-permute-start.28 = (bf16[2,128,896]{2,1,0:T(8,128)(2,1)S(1)}, bf16[2,128,896]{2,1,0:T(8,128)(2,1)S(1)}, u32[]{:S(2)}, u32[]{:S(2)}) collective-permute-start(bf16[2,128,896]{2,1,0:T(8,128)(2,1)S(1)} %pad_maximum_fusion.5.refs_0_), channel_id=1, source_target_pairs={{0,1},{1,0},{2,3},{3,2},{4,5},{5,4},{6,7},{7,6},{8,9},{9,8},{10,11... | collective-permute-start | bytes 1376264 | tf_op jit(solution)/shard_map/ppermute | solution.py:24
  118.9 14.0 %collective-permute-start.19 = (bf16[128,896]{1,0:T(8,128)(2,1)S(1)}, bf16[128,896]{1,0:T(8,128)(2,1)S(1)}, u32[]{:S(2)}, u32[]{:S(2)}) collective-permute-start(bf16[128,896]{1,0:T(8,128)(2,1)S(1)} %collective-permute-done.18), channel_id=1, source_target_pairs={{0,2},{2,0},{1,3},{3,1},{4,6},{6,4},{5,7},{7,5},{8,10},{10,8},{9,1... | collective-permute-start | bytes 688136 | tf_op jit(solution)/shard_map/ppermute | solution.py:24
  119.4 16.0 %collective-permute-start.17 = (bf16[128,896]{1,0:T(8,128)(2,1)S(1)}, bf16[128,896]{1,0:T(8,128)(2,1)S(1)}, u32[]{:S(2)}, u32[]{:S(2)}) collective-permute-start(bf16[128,896]{1,0:T(8,128)(2,1)S(1)} %collective-permute-done.16), channel_id=1, source_target_pairs={{0,2},{2,0},{1,3},{3,1},{4,6},{6,4},{5,7},{7,5},{8,10},{10,8},{9,1... | collective-permute-start | bytes 688136 | tf_op jit(solution)/shard_map/ppermute | solution.py:24
  123.4 12.9 %collective-permute-start.24 = (bf16[128,896]{1,0:T(8,128)(2,1)S(1)}, bf16[128,896]{1,0:T(8,128)(2,1)S(1)}, u32[]{:S(2)}, u32[]{:S(2)}) collective-permute-start(bf16[128,896]{1,0:T(8,128)(2,1)S(1)} %broadcast_select_fusion), channel_id=1, source_target_pairs={{0,16},{16,0},{1,17},{17,1},{2,18},{18,2},{3,19},{19,3},{4,20},{20... | collective-permute-start | bytes 688136 | tf_op jit(solution)/shard_map/ppermute | solution.py:24
  129.4 8.8 %copy-start.11 = (bf16[2,128,896]{2,1,0:T(8,128)(2,1)}, bf16[2,128,896]{2,1,0:T(8,128)(2,1)S(1)}, u32[]{:S(2)}) copy-start(bf16[2,128,896]{2,1,0:T(8,128)(2,1)S(1)} %collective-permute-done.27.refs_1_) | copy-start | bytes 1376260
  129.4 8.7 %collective-permute-start.29 = (bf16[2,128,896]{2,1,0:T(8,128)(2,1)S(1)}, bf16[2,128,896]{2,1,0:T(8,128)(2,1)S(1)}, u32[]{:S(2)}, u32[]{:S(2)}) collective-permute-start(bf16[2,128,896]{2,1,0:T(8,128)(2,1)S(1)} %collective-permute-done.27.refs_1_), channel_id=1, source_target_pairs={{0,1},{1,0},{2,3},{3,2},{4,5},{5,4},{6,7},{7,6},{8,9},{9,8},{10,11... | collective-permute-start | bytes 1376264 | tf_op jit(solution)/shard_map/ppermute | solution.py:24
  133.0 16.3 %collective-permute-start.20 = (bf16[2,128,896]{2,1,0:T(8,128)(2,1)S(1)}, bf16[2,128,896]{2,1,0:T(8,128)(2,1)}, u32[]{:S(2)}, u32[]{:S(2)}) collective-permute-start(bf16[2,128,896]{2,1,0:T(8,128)(2,1)S(1)} %pad_maximum_fusion.3.refs_0_), channel_id=1, source_target_pairs={{0,16},{16,0},{1,17},{17,1},{2,18},{18,2},{3,19},{19,3},{4,20},{20... | collective-permute-start | bytes 1376264 | tf_op jit(solution)/shard_map/ppermute | solution.py:24
  135.4 17.0 %collective-permute-start.21 = (bf16[2,128,896]{2,1,0:T(8,128)(2,1)S(1)}, bf16[2,128,896]{2,1,0:T(8,128)(2,1)}, u32[]{:S(2)}, u32[]{:S(2)}) collective-permute-start(bf16[2,128,896]{2,1,0:T(8,128)(2,1)S(1)} %pad_maximum_fusion.2.refs_0_), channel_id=1, source_target_pairs={{0,16},{16,0},{1,17},{17,1},{2,18},{18,2},{3,19},{19,3},{4,20},{20... | collective-permute-start | bytes 1376264 | tf_op jit(solution)/shard_map/ppermute | solution.py:24
  136.3 16.1 %collective-permute-start.25 = (bf16[2,128,896]{2,1,0:T(8,128)(2,1)S(1)}, bf16[2,128,896]{2,1,0:T(8,128)(2,1)}, u32[]{:S(2)}, u32[]{:S(2)}) collective-permute-start(bf16[2,128,896]{2,1,0:T(8,128)(2,1)S(1)} %pad_maximum_fusion.4.refs_4_), channel_id=1, source_target_pairs={{0,2},{2,0},{1,3},{3,1},{4,6},{6,4},{5,7},{7,5},{8,10},{10,8},{9,1... | collective-permute-start | bytes 1376264 | tf_op jit(solution)/shard_map/ppermute | solution.py:24
  138.1 16.4 %collective-permute-start.34 = (bf16[2,128,896]{2,1,0:T(8,128)(2,1)S(1)}, bf16[2,128,896]{2,1,0:T(8,128)(2,1)}, u32[]{:S(2)}, u32[]{:S(2)}) collective-permute-start(bf16[2,128,896]{2,1,0:T(8,128)(2,1)S(1)} %pad_maximum_fusion.3.refs_0_), channel_id=1, source_target_pairs={{0,1},{1,0},{2,3},{3,2},{4,5},{5,4},{6,7},{7,6},{8,9},{9,8},{10,11... | collective-permute-start | bytes 1376264 | tf_op jit(solution)/shard_map/ppermute | solution.py:24
  152.4 2.3 collective-permute-start.35
  153.6 11.6 %collective-permute-start.30 = (bf16[2,128,896]{2,1,0:T(8,128)(2,1)S(1)}, bf16[2,128,896]{2,1,0:T(8,128)(2,1)S(1)}, u32[]{:S(2)}, u32[]{:S(2)}) collective-permute-start(bf16[2,128,896]{2,1,0:T(8,128)(2,1)S(1)} %pad_maximum_fusion.2.refs_0_), channel_id=1, source_target_pairs={{0,1},{1,0},{2,3},{3,2},{4,5},{5,4},{6,7},{7,6},{8,9},{9,8},{10,11... | collective-permute-start | bytes 1376264 | tf_op jit(solution)/shard_map/ppermute | solution.py:24
  154.0 11.2 %collective-permute-start.32 = (bf16[2,128,896]{2,1,0:T(8,128)(2,1)S(1)}, bf16[2,128,896]{2,1,0:T(8,128)(2,1)S(1)}, u32[]{:S(2)}, u32[]{:S(2)}) collective-permute-start(bf16[2,128,896]{2,1,0:T(8,128)(2,1)S(1)} %pad_maximum_fusion.4.refs_4_), channel_id=1, source_target_pairs={{0,1},{1,0},{2,3},{3,2},{4,5},{5,4},{6,7},{7,6},{8,9},{9,8},{10,11... | collective-permute-start | bytes 1376264 | tf_op jit(solution)/shard_map/ppermute | solution.py:24
  154.1 11.2 %collective-permute-start.31 = (bf16[2,128,896]{2,1,0:T(8,128)(2,1)}, bf16[2,128,896]{2,1,0:T(8,128)(2,1)S(1)}, u32[]{:S(2)}, u32[]{:S(2)}) collective-permute-start(bf16[2,128,896]{2,1,0:T(8,128)(2,1)} %collective-permute-done.21.refs_1_), channel_id=1, source_target_pairs={{0,1},{1,0},{2,3},{3,2},{4,5},{5,4},{6,7},{7,6},{8,9},{9,8},{10,11... | collective-permute-start | bytes 1376264 | tf_op jit(solution)/shard_map/ppermute | solution.py:24
  154.5 10.7 %collective-permute-start.33 = (bf16[2,128,896]{2,1,0:T(8,128)(2,1)}, bf16[2,128,896]{2,1,0:T(8,128)(2,1)S(1)}, u32[]{:S(2)}, u32[]{:S(2)}) collective-permute-start(bf16[2,128,896]{2,1,0:T(8,128)(2,1)} %collective-permute-done.25.refs_5_), channel_id=1, source_target_pairs={{0,1},{1,0},{2,3},{3,2},{4,5},{5,4},{6,7},{7,6},{8,9},{9,8},{10,11... | collective-permute-start | bytes 1376264 | tf_op jit(solution)/shard_map/ppermute | solution.py:24
  156.3 9.0 %copy-start.6 = (f32[512,1]{1,0:T(8,128)S(1)}, f32[512,1]{1,0:T(8,128)}, u32[]{:S(2)}) copy-start(f32[512,1]{1,0:T(8,128)} %reshape.97.refs_12_) | copy-start | bytes 6148
  156.3 21.5 %slice-start = ((s8[14680064]{0:T(1024)(128)(4,1)}), s8[4194304]{0:T(1024)(128)(4,1)S(1)}, s32[]{:S(2)}) async-start(s8[14680064]{0:T(1024)(128)(4,1)} %bitcast.144), calls=%async_computation | async-start | bytes 8388608
  156.3 21.6 %slice-start.1 = ((s8[14680064]{0:T(1024)(128)(4,1)}), s8[4194304]{0:T(1024)(128)(4,1)S(1)}, s32[]{:S(2)}) async-start(s8[14680064]{0:T(1024)(128)(4,1)} %bitcast.144), calls=%async_computation.1 | async-start | bytes 8388608
  165.3 12.6 %slice-start.2 = ((s8[14680064]{0:T(1024)(128)(4,1)}), s8[4194304]{0:T(1024)(128)(4,1)S(1)}, s32[]{:S(2)}) async-start(s8[14680064]{0:T(1024)(128)(4,1)} %bitcast.144), calls=%async_computation.2 | async-start | bytes 8388608
  165.3 12.6 %slice-start.3 = ((s8[14680064]{0:T(1024)(128)(4,1)}), s8[2097152]{0:T(1024)(128)(4,1)S(1)}, s32[]{:S(2)}) async-start(s8[14680064]{0:T(1024)(128)(4,1)} %bitcast.144), calls=%async_computation.3 | async-start | bytes 4194304
  182.7 6.5 %collective-permute-start.36 = (bf16[2,256,1792]{2,1,0:T(8,128)(2,1)S(1)}, bf16[2,256,1792]{2,1,0:T(8,128)(2,1)S(1)}, u32[]{:S(2)}, u32[]{:S(2)}) collective-permute-start(bf16[2,256,1792]{2,1,0:T(8,128)(2,1)S(1)} %pad_maximum_fusion), channel_id=1, source_target_pairs={{0,1},{1,0},{2,3},{3,2},{4,5},{5,4},{6,7},{7,6},{8,9},{9,8},{10,11... | collective-permute-start | bytes 5505032 | tf_op jit(solution)/shard_map/ppermute | solution.py:24
  184.7 19.5 %collective-permute-start.43 = (bf16[2,256,1792]{2,1,0:T(8,128)(2,1)}, bf16[2,256,1792]{2,1,0:T(8,128)(2,1)}, u32[]{:S(2)}, u32[]{:S(2)}) collective-permute-start(bf16[2,256,1792]{2,1,0:T(8,128)(2,1)} %pad_maximum_fusion.1), channel_id=1, source_target_pairs={{0,1},{1,0},{2,3},{3,2},{4,5},{5,4},{6,7},{7,6},{8,9},{9,8},{10,11... | collective-permute-start | bytes 5505032 | tf_op jit(solution)/shard_map/ppermute | solution.py:24
  191.1 12.9 %collective-permute-start.37 = (bf16[128,1792]{1,0:T(8,128)(2,1)S(1)}, bf16[128,1792]{1,0:T(8,128)(2,1)S(1)}, u32[]{:S(2)}, u32[]{:S(2)}) collective-permute-start(bf16[128,1792]{1,0:T(8,128)(2,1)S(1)} %slice.61), channel_id=1, source_target_pairs={{0,16},{16,0},{1,17},{17,1},{2,18},{18,2},{3,19},{19,3},{4,20},{20... | collective-permute-start | bytes 1376264 | tf_op jit(solution)/shard_map/ppermute | solution.py:24
  192.0 18.1 %collective-permute-start.40 = (bf16[2,128,896]{2,1,0:T(8,128)(2,1)S(1)}, bf16[2,128,896]{2,1,0:T(8,128)(2,1)S(1)}, u32[]{:S(2)}, u32[]{:S(2)}) collective-permute-start(bf16[2,128,896]{2,1,0:T(8,128)(2,1)S(1)} %constant_dynamic-slice_fusion.2), channel_id=1, source_target_pairs={{0,2},{2,0},{1,3},{3,1},{4,6},{6,4},{5,7},{7,5},{8,10},{10,8},{9,1... | collective-permute-start | bytes 1376264 | tf_op jit(solution)/shard_map/ppermute | solution.py:24
  206.6 23.3 %collective-permute-start.47 = (bf16[128,1792]{1,0:T(8,128)(2,1)S(1)}, bf16[128,1792]{1,0:T(8,128)(2,1)S(1)}, u32[]{:S(2)}, u32[]{:S(2)}) collective-permute-start(bf16[128,1792]{1,0:T(8,128)(2,1)S(1)} %slice.67), channel_id=1, source_target_pairs={{0,16},{16,0},{1,17},{17,1},{2,18},{18,2},{3,19},{19,3},{4,20},{20... | collective-permute-start | bytes 1376264 | tf_op jit(solution)/shard_map/ppermute | solution.py:24
  207.5 9.0 %collective-permute-start.38 = (bf16[128,896]{1,0:T(8,128)(2,1)S(1)}, bf16[128,896]{1,0:T(8,128)(2,1)S(1)}, u32[]{:S(2)}, u32[]{:S(2)}) collective-permute-start(bf16[128,896]{1,0:T(8,128)(2,1)S(1)} %constant_dynamic-slice_fusion.3), channel_id=1, source_target_pairs={{0,2},{2,0},{1,3},{3,1},{4,6},{6,4},{5,7},{7,5},{8,10},{10,8},{9,1... | collective-permute-start | bytes 688136 | tf_op jit(solution)/shard_map/ppermute | solution.py:24
  210.2 13.4 %collective-permute-start.41 = (bf16[128,896]{1,0:T(8,128)(2,1)S(1)}, bf16[128,896]{1,0:T(8,128)(2,1)S(1)}, u32[]{:S(2)}, u32[]{:S(2)}) collective-permute-start(bf16[128,896]{1,0:T(8,128)(2,1)S(1)} %slice_bitcast_fusion.4), channel_id=1, source_target_pairs={{0,16},{16,0},{1,17},{17,1},{2,18},{18,2},{3,19},{19,3},{4,20},{20... | collective-permute-start | bytes 688136 | tf_op jit(solution)/shard_map/ppermute | solution.py:24
  211.5 16.5 %collective-permute-start.44 = (bf16[2,128,896]{2,1,0:T(8,128)(2,1)S(1)}, bf16[2,128,896]{2,1,0:T(8,128)(2,1)S(1)}, u32[]{:S(2)}, u32[]{:S(2)}) collective-permute-start(bf16[2,128,896]{2,1,0:T(8,128)(2,1)S(1)} %constant_dynamic-slice_fusion.1), channel_id=1, source_target_pairs={{0,2},{2,0},{1,3},{3,1},{4,6},{6,4},{5,7},{7,5},{8,10},{10,8},{9,1... | collective-permute-start | bytes 1376264 | tf_op jit(solution)/shard_map/ppermute | solution.py:24
  216.6 24.6 %copy-start.15 = (bf16[128,896]{1,0:T(8,128)(2,1)S(1)}, bf16[128,896]{1,0:T(8,128)(2,1)}, u32[]{:S(2)}) copy-start(bf16[128,896]{1,0:T(8,128)(2,1)} %copy-done.14) | copy-start | bytes 688132
  216.7 19.7 %collective-permute-start.39 = (bf16[128,896]{1,0:T(8,128)(2,1)S(1)}, bf16[128,896]{1,0:T(8,128)(2,1)S(1)}, u32[]{:S(2)}, u32[]{:S(2)}) collective-permute-start(bf16[128,896]{1,0:T(8,128)(2,1)S(1)} %add_convert_fusion.6), channel_id=1, source_target_pairs={{0,8},{4,12},{8,0},{12,4},{1,9},{5,13},{9,1},{13,5},{2,10},{6,14},... | collective-permute-start | bytes 688136 | tf_op jit(solution)/shard_map/ppermute | solution.py:29
  223.7 12.6 %collective-permute-start.42 = (bf16[128,896]{1,0:T(8,128)(2,1)S(1)}, bf16[128,896]{1,0:T(8,128)(2,1)S(1)}, u32[]{:S(2)}, u32[]{:S(2)}) collective-permute-start(bf16[128,896]{1,0:T(8,128)(2,1)S(1)} %fusion.28), channel_id=1, source_target_pairs={{0,4},{4,8},{8,12},{12,0},{1,5},{5,9},{9,13},{13,1},{2,6},{6,10},{... | collective-permute-start | bytes 688136 | tf_op jit(solution)/shard_map/ppermute | solution.py:29
  228.2 6.1 %collective-permute-start.45 = (bf16[128,896]{1,0:T(8,128)(2,1)S(1)}, bf16[128,896]{1,0:T(8,128)(2,1)S(1)}, u32[]{:S(2)}, u32[]{:S(2)}) collective-permute-start(bf16[128,896]{1,0:T(8,128)(2,1)S(1)} %slice_bitcast_fusion.2), channel_id=1, source_target_pairs={{0,16},{16,0},{1,17},{17,1},{2,18},{18,2},{3,19},{19,3},{4,20},{20... | collective-permute-start | bytes 688136 | tf_op jit(solution)/shard_map/ppermute | solution.py:24
  230.0 13.9 %copy-start.1 = (bf16[32,64,576]{2,1,0:T(8,128)(2,1)S(1)}, bf16[32,64,576]{2,1,0:T(8,128)(2,1)}, u32[]{:S(2)}) copy-start(bf16[32,64,576]{2,1,0:T(8,128)(2,1)} %param.11) | copy-start | bytes 7077892
  230.1 6.6 %collective-permute-start.48 = (bf16[128,896]{1,0:T(8,128)(2,1)S(1)}, bf16[128,896]{1,0:T(8,128)(2,1)S(1)}, u32[]{:S(2)}, u32[]{:S(2)}) collective-permute-start(bf16[128,896]{1,0:T(8,128)(2,1)S(1)} %constant_dynamic-slice_fusion), channel_id=1, source_target_pairs={{0,2},{2,0},{1,3},{3,1},{4,6},{6,4},{5,7},{7,5},{8,10},{10,8},{9,1... | collective-permute-start | bytes 688136 | tf_op jit(solution)/shard_map/ppermute | solution.py:24
  234.3 6.9 %collective-permute-start.46 = (bf16[128,896]{1,0:T(8,128)(2,1)S(1)}, bf16[128,896]{1,0:T(8,128)(2,1)S(1)}, u32[]{:S(2)}, u32[]{:S(2)}) collective-permute-start(bf16[128,896]{1,0:T(8,128)(2,1)S(1)} %fusion.27), channel_id=1, source_target_pairs={{0,12},{4,0},{8,4},{12,8},{1,13},{5,1},{9,5},{13,9},{2,14},{6,2},{... | collective-permute-start | bytes 688136 | tf_op jit(solution)/shard_map/ppermute | solution.py:29
  241.5 1.4 collective-permute-start.49
  (11 other events, 13.3 us)

commit v2 on v1

--- a/solution.py
+++ b/solution.py
@@ -33,33 +33,66 @@
     return jnp.where(index == 0, value, jnp.flip(value, axis))
 
 
-def attend(queries, latent_cache, cache_len, value_up):
-    scores = (
-        jnp.einsum("rhk,rlk->rhl", queries, latent_cache, preferred_element_type=F32)
-        * SOFTMAX_SCALE
-    )
-    positions = jnp.arange(latent_cache.shape[1], dtype=jnp.int32)
-    in_range = positions[None, None, :] < cache_len[:, None, None]
-    masked = jnp.where(in_range, scores, MASK_VALUE)
-    row_max = jnp.max(masked, axis=2, keepdims=True)
-    exp_scores = jnp.where(in_range, jnp.exp(masked - row_max), 0.0)
-    probs = (exp_scores / jnp.sum(exp_scores, axis=2, keepdims=True)).astype(BF16)
-    latent_out = jnp.einsum(
-        "rhl,rlc->rhc", probs, latent_cache[:, :, :LAT], preferred_element_type=F32
-    ).astype(BF16)
-    heads_out = jnp.einsum("rhc,hcv->rhv", latent_out, value_up, preferred_element_type=F32)
-    return heads_out.astype(BF16).reshape(queries.shape[0], queries.shape[1] * VDIM)
-
-
 def in_hbm(value):
     return pltpu.with_memory_space_constraint(value, pltpu.HBM)
 
 
-def project_kernel(count, place_ref, own_ref, sibling_ref, *refs):
-    blocks, refs = refs[:-8], refs[-8:]
-    out_ref, rows_ref, own_rows, sibling_rows, own_total, sibling_total, total_ref, arrived = refs
-    size, depth = blocks[0].shape
-    tile = min(1024, depth)
+def attend_kernel(length_ref, query_ref, cache_ref, out_ref):
+    rows, depth = out_ref.shape[0], out_ref.shape[2]
+    scores = [
+        jnp.dot(query_ref[i], cache_ref[i], preferred_element_type=F32) for i in range(rows)
+    ]
+    positions = lax.broadcasted_iota(jnp.int32, scores[0].shape, 1)
+    probs = []
+    for i in range(rows):
+        in_range = positions < length_ref[pl.program_id(0) * rows + i]
+        masked = jnp.where(in_range, scores[i] * SOFTMAX_SCALE, MASK_VALUE)
+        row_max = jnp.max(masked, axis=1, keepdims=True)
+        exp_scores = jnp.where(in_range, jnp.exp(masked - row_max), 0.0)
+        probs.append((exp_scores / jnp.sum(exp_scores, axis=1, keepdims=True)).astype(BF16))
+    latent = [
+        lax.dot_general(
+            probs[i], cache_ref[i, :depth, :], (((1,), (1,)), ((), ())), preferred_element_type=F32
+        )
+        for i in range(rows)
+    ]
+    for i in range(rows):
+        out_ref[i] = latent[i].astype(BF16)
+
+
+def attend(queries, latent_cache, cache_len, value_up):
+    rows, heads, depth = queries.shape
+    positions = latent_cache.shape[1]
+    tile = 8
+    latent_out = pl.pallas_call(
+        attend_kernel,
+        grid_spec=pltpu.PrefetchScalarGridSpec(
+            num_scalar_prefetch=1,
+            grid=(rows // tile,),
+            in_specs=[
+                pl.BlockSpec((tile, heads, depth), lambda r, length: (r, 0, 0)),
+                pl.BlockSpec((tile, depth, positions), lambda r, length: (r, 0, 0)),
+            ],
+            out_specs=pl.BlockSpec((tile, heads, LAT), lambda r, length: (r, 0, 0)),
+        ),
+        out_shape=jax.ShapeDtypeStruct((rows, heads, LAT), BF16),
+        compiler_params=pltpu.CompilerParams(vmem_limit_bytes=16 * MIB),
+        cost_estimate=pl.CostEstimate(
+            flops=2 * rows * heads * positions * (depth + LAT),
+            bytes_accessed=2 * rows * (heads * (depth + LAT) + positions * depth),
+            transcendentals=rows * heads * positions,
+        ),
+    )(cache_len, in_hbm(queries), in_hbm(latent_cache.transpose(0, 2, 1)))
+    heads_out = jnp.einsum("rhc,hcv->rhv", latent_out, value_up, preferred_element_type=F32)
+    return heads_out.astype(BF16).reshape(rows, heads * VDIM)
+
+
+def project_kernel(slots, start, first, place_ref, own_ref, sibling_ref, *refs):
+    blocks, (out_ref, rows_ref, weight_ref, total_ref, arrived) = refs[:-5], refs[-5:]
+    if not first:
+        earlier_ref, *blocks = blocks
+    count, (size, depth), width = len(slots), blocks[0].shape, own_ref.shape[0]
+    tile = min(2048, depth)
     tiles = depth // tile
 
     def rows_copy(i, block):
@@ -68,68 +101,80 @@
 
     def weight_copy(half, k):
         columns = pl.ds(pl.multiple_of(k * tile, tile), tile)
-        source, target = ((own_ref, own_rows), (sibling_ref, sibling_rows))[half]
+        source, place = ((own_ref, place_ref[2 * count]), (sibling_ref, 1 - place_ref[2 * count]))[half]
         return pltpu.make_async_copy(
-            source.at[:, columns], target.at[:, columns], arrived.at[count + half * tiles + k]
+            source.at[:, pl.ds(pl.multiple_of(start + k * tile, tile), tile)],
+            weight_ref.at[pl.ds(pl.multiple_of(place * width, 16), width), columns],
+            arrived.at[count + half * tiles + k],
         )
 
-    for i in range(count):
-        for at, block in enumerate(blocks):
-
-            @pl.when(place_ref[2 * i] == at)
-            def _():
-                rows_copy(i, block).start()
+    for i, slot in enumerate(slots):
+        if len(slot) == 1:
+            rows_copy(i, blocks[slot[0]]).start()
+            continue
+        from_left = place_ref[2 * i] == 1
+
+        @pl.when(from_left)
+        def _():
+            rows_copy(i, blocks[slot[0]]).start()
+
+        @pl.when(jnp.logical_not(from_left))
+        def _():
+            rows_copy(i, blocks[slot[1]]).start()
 
     for k in range(tiles):
         for half in range(2):
             weight_copy(half, k).start()
-    own_total[...] = jnp.zeros_like(own_total)
-    sibling_total[...] = jnp.zeros_like(sibling_total)
+    total_ref[...] = jnp.zeros_like(total_ref)
     for i in range(count):
         rows_copy(i, blocks[0]).wait()
 
     def step(k, _):
         columns = pl.ds(pl.multiple_of(k * tile, tile), tile)
-        rows = rows_ref[:, columns]
-        for half, (weight_ref, sum_ref) in enumerate(
-            ((own_rows, own_total), (sibling_rows, sibling_total))
-        ):
+        for half in range(2):
             weight_copy(half, k).wait()
-            sum_ref[...] += lax.dot_general(
-                weight_ref[:, columns], rows, (((1,), (1,)), ((), ())), preferred_element_type=F32
-            )
+        total_ref[...] += lax.dot_general(
+            weight_ref[:, columns],
+            rows_ref[:, columns],
+            (((1,), (1,)), ((), ())),
+            preferred_element_type=F32,
+        )
         return 0
 
     lax.fori_loop(0, tiles, step, 0)
-    width, core = own_total.shape[0], place_ref[2 * count]
-    total_ref[pl.ds(pl.multiple_of(core * width, 8), width), :] = own_total[...]
-    total_ref[pl.ds(pl.multiple_of((1 - core) * width, 8), width), :] = sibling_total[...]
-    out_ref[...] = total_ref[...].T.astype(out_ref.dtype)
-
-
-def project(place, count, blocks, own, sibling, dtype):
-    size, depth = blocks[0].shape
+    total = total_ref[...].T
+    if not first:
+        total = total + earlier_ref[...]
+    out_ref[...] = total.astype(out_ref.dtype)
+
+
+def project(place, slots, blocks, own, sibling, start, earlier, dtype):
+    vmem = pl.BlockSpec(memory_space=pltpu.VMEM)
+    first = earlier is None
+    count, (size, depth) = len(slots), blocks[0].shape
     width = own.shape[0]
     anywhere = pl.BlockSpec(memory_space=pl.ANY)
     return pl.pallas_call(
-        functools.partial(project_kernel, count),
-        in_specs=[pl.BlockSpec(memory_space=pltpu.SMEM)] + [anywhere] * (2 + len(blocks)),
-        out_specs=pl.BlockSpec(memory_space=pltpu.VMEM),
+        functools.partial(project_kernel, slots, start, first),
+        in_specs=[pl.BlockSpec(memory_space=pltpu.SMEM)]
+        + [anywhere] * 2
+        + ([] if first else [vmem])
+        + [anywhere] * len(blocks),
+        out_specs=vmem,
         out_shape=jax.ShapeDtypeStruct((count * size, 2 * width), dtype),
-        scratch_shapes=[pltpu.VMEM((count * size, depth), BF16)]
-        + [pltpu.VMEM((width, depth), BF16)] * 2
-        + [pltpu.VMEM((width, count * size), F32)] * 2
-        + [
+        scratch_shapes=[
+            pltpu.VMEM((count * size, depth), BF16),
+            pltpu.VMEM((2 * width, depth), BF16),
             pltpu.VMEM((2 * width, count * size), F32),
-            pltpu.SemaphoreType.DMA((count + 2 * (depth // min(1024, depth)),)),
+            pltpu.SemaphoreType.DMA((count + 2 * (depth // min(2048, depth)),)),
         ],
-        compiler_params=pltpu.CompilerParams(vmem_limit_bytes=28 * MIB),
+        compiler_params=pltpu.CompilerParams(vmem_limit_bytes=16 * MIB),
         cost_estimate=pl.CostEstimate(
             flops=4 * count * size * depth * width,
             bytes_accessed=2 * depth * (2 * width + count * size),
             transcendentals=0,
         ),
-    )(place, in_hbm(own), in_hbm(sibling), *blocks)
+    )(place, in_hbm(own), in_hbm(sibling), *([] if first else [earlier]), *blocks)
 
 
 def hidden_kernel(layout, first, last, place_ref, *refs):
@@ -209,7 +254,7 @@
                 if last and matrix:
                     gate = sums[0][:, part]
                     hidden_ref[:, part] = (
-                        weight_ref[...] * (gate / (1.0 + jnp.exp(-gate))) * value
+                        weight_ref[:, :1] * (gate / (1.0 + jnp.exp(-gate))) * value
                     ).astype(hidden_ref.dtype)
                 else:
                     sums[matrix][:, part] = value
@@ -224,7 +269,7 @@
                 sum_copy(n, matrix, True).wait()
 
 
-def hidden_part(units, places, side, pieces, w_gate, w_up, sums=None, weight=None):
+def hidden_part(units, places, pieces, w_gate, w_up, sums=None, weight=None):
     first, last = sums is None, weight is not None
     size, width = pieces[0].shape[1:]
     rows, columns, depth = 4 * size, w_gate.shape[1], 2 * width
@@ -269,7 +314,7 @@
             bytes_accessed=4 * len(units) * depth * columns,
             transcendentals=rows * columns,
         ),
-    )(jnp.stack(places + [side]).astype(jnp.int32), *operands)
+    )(places, *operands)
 
 
 def add(one, other):
@@ -309,29 +354,59 @@
     ).reshape(-1, chip_width)
 
     heads = attend(queries, latent_cache, cache_len, value_up)
-    rights, lefts = [heads], [heads]
-    for k in shifts[1:]:
-        rights.append(
-            lax.ppermute(rights[-1], "line", [(i, i + 1) for i in range(k - 1, line - 1)])
-        )
-        lefts.append(lax.ppermute(lefts[-1], "line", [(i, i - 1) for i in range(1, line - k + 1)]))
-    near = [heads] + [value for pair in zip(rights[1:], lefts[1:]) for value in pair]
+    weight = jnp.sum(jnp.where(route_ids == lax.axis_index(GRP), route_weights, 0.0), axis=1)
+    weight = weight.reshape(2, line // 2, 2, 2, block).transpose(3, 0, 1, 2, 4)
+    weight = relative(relative(weight, 0, core), 1, sect).reshape(row_total, 1)
+    weight = jnp.broadcast_to(weight, (row_total, 128))
     holders = [range(line)] + [
         value for k in shifts[1:] for value in (range(k, line), range(line - k))
     ]
-    far = [
-        lax.ppermute(value, ("line", "side"), [(2 * i + y, 2 * i + 1 - y) for i in held for y in range(2)])
-        for value, held in zip(near, holders)
+    slots, place = [], []
+    for k in shifts:
+        slot = (2 * k - 1, 2 * (line - k)) if k else (0,)
+        for y in range(2):
+            slots.append(tuple(i + y * len(holders) for i in slot))
+            place += [at >= k, 2 * ((at - k) % line) + (side + y) % 2]
+    place = jnp.stack([jnp.asarray(value, jnp.int32) for value in place + [core]])
+    half, back = line // 2, line - 1
+    groups = ([0], [back], [1, half])
+    group_places = [
+        jnp.stack([(at - k) % line for k in group] + [side]).astype(jnp.int32) for group in groups
     ]
-    place = []
-    for k in shifts:
-        origin = jnp.where(at >= k, 2 * k - 1, 2 * (line - k)) if k else 0
-        for y in range(2):
-            place += [origin + y * len(near), 2 * ((at - k) % line) + (side + y) % 2]
-    place = jnp.stack([jnp.int32(value) for value in place] + [core]).astype(jnp.int32)
-    partial = project(
-        place, 2 * line, near + far, own_proj, sibling_proj, F32 if tp > 1 else BF16
-    )
+    length, partial, blocks = heads.shape[1] // 2, None, []
+    for part in range(2):
+        own = heads[:, part * length : (part + 1) * length]
+        if part:
+            own, weight, residual_rows, place, group_places = lax.optimization_barrier(
+                (own, weight, residual_rows, place, group_places)
+            )
+        rights, lefts = [own], [own]
+        for k in shifts[1:]:
+            if k == 3 and not part:
+                rights[-1], sibling_proj = lax.optimization_barrier((rights[-1], sibling_proj))
+            right = [(i, i + 1) for i in range(k - 1, line - 1)]
+            left = [(i, i - 1) for i in range(1, line - k + 1)]
+            rights.append(lax.ppermute(rights[-1], "line", right))
+            lefts.append(lax.ppermute(lefts[-1], "line", left))
+        near = [own] + [value for pair in zip(rights[1:], lefts[1:]) for value in pair]
+        far = [
+            lax.ppermute(
+                value, ("line", "side"), [(2 * i + y, 2 * i + 1 - y) for i in held for y in range(2)]
+            )
+            for value, held in zip(near, holders)
+        ]
+        blocks.append(near + far)
+    for part in range(2):
+        partial = project(
+            place,
+            slots,
+            blocks[part],
+            own_proj,
+            sibling_proj,
+            part * length,
+            partial,
+            BF16 if part and tp == 1 else F32,
+        )
     if tp > 1:
         partial = lax.psum(partial, "tp").astype(BF16)
     partial = partial.reshape(2, -1, chip_width)
@@ -340,15 +415,11 @@
     attention = kept.astype(F32) + swap(given, "sect").astype(F32)
     own_rows = (residual_rows.astype(F32) + attention).astype(BF16)
 
-    weight = jnp.sum(jnp.where(route_ids == lax.axis_index(GRP), route_weights, 0.0), axis=1)
-    weight = weight.reshape(2, line // 2, 2, 2, block).transpose(3, 0, 1, 2, 4)
-    weight = relative(relative(weight, 0, core), 1, sect).reshape(row_total, 1)
     got = {k: shift(own_rows, k) if k else own_rows for k in shifts if k != line // 2}
     right = lax.ppermute(got[1], "line", [(i, i + 1) for i in range(1, line - 1)])
     left = lax.ppermute(got[line - 1], "line", [(i, i - 1) for i in range(1, line - 1)])
     got[line // 2] = jnp.where(at >= line // 2, right, left)
     pairs, opposites = {}, {}
-    half, back = line // 2, line - 1
     for k in (0, back, 1, half):
         first, second = ("sect", "side") if k % 2 == 0 else ("side", "sect")
         pairs[k] = jnp.stack([got[k], swap(got[k], first)])
@@ -358,15 +429,13 @@
         for k in shifts
     ]
     sums = None
-    for group in ([0], [back], [1, half]):
+    for group, places in zip(groups, group_places):
         if group == [back]:
-            late = [opposites[k] for k in (back, 1, half)]
-            late, sums = lax.optimization_barrier((late, sums))
-            opposites.update(zip((back, 1, half), late))
+            for k in (back, 1, half):
+                opposites[k], _ = lax.optimization_barrier((opposites[k], sums))
         sums = hidden_part(
             [layout[k] for k in group],
-            [(at - k) % line for k in group],
-            side,
+            places,
             [
                 piece
                 for k in group

time: 245 us -> 242 us (0.988)
  matrix products: 24.3 us -> 10.8 us
  local copies, waits for them, and re-layouts: 15.2 us -> 24.1 us
  waiting for transfers between devices: 80.5 us -> 74 us
  starting transfers between devices: 72 us -> 77.1 us
  Pallas kernels: 43 us -> 47.5 us
    ppermute x30, waiting for transfers between devices: 33.2 us -> 48.3 us  [swap(): return lax.ppermute(value, axis, [(0, 1), (1, 0)])]
    ppermute x6 -> x12, waiting for transfers between devices: 24 us -> 11.9 us  [the longest x6 8.6 us: on_device(): lefts.append(lax.ppermute(lefts[-1], 'line', left))]
    dot_general x2 -> x0, matrix products: 10.1 us -> none  [the longest x1 6.54 us: attend(): jnp.einsum('rhl,rlc->rhc', probs, latent_cache[:, :, :LAT], preferred_ele...]
    ppermute x6 -> x12, starting transfers between devices: 11 us -> 20.2 us  [the longest x6 12.5 us: on_device(): rights.append(lax.ppermute(rights[-1], 'line', right))]
    unnamed x51 -> x73, local copies, waits for them, and re-layouts: 12.4 us -> 21.3 us
    ppermute x7 -> x14, starting transfers between devices: 15.4 us -> 24 us  [on_device(): lax.ppermute(value, ('line', 'side'), [(2 * i + y, 2 * i + 1 - y) for i i...]
    ppermute x7 -> x14, waiting for transfers between devices: 11 us -> 2.43 us  [on_device(): lax.ppermute(value, ('line', 'side'), [(2 * i + y, 2 * i + 1 - y) for i i...]
    ppermute x30, starting transfers between devices: 28.6 us -> 21.4 us  [swap(): return lax.ppermute(value, axis, [(0, 1), (1, 0)])]
  transfers between devices with their start and end apart: 50 -> 63, of which waited for: 22 -> 22; matrix products, arithmetic and copies ran while one was open for 12% -> 6% of each run, Pallas kernels for 7% -> 12%
where the time goes in v2:
time: 242 us; the launch traced here: 241 us
  starting transfers between devices  77.1 us (32%)
  waiting for transfers between devices  74 us (31%)
  Pallas kernels  47.5 us (20%)
  local copies, waits for them, and re-layouts  24.1 us (10%)
  matrix products  10.8 us (4%)
  other arithmetic  6.93 us (3%)
    ppermute x30, waiting for transfers between devices, swap(): return lax.ppermute(value, axis, [(0, 1), (1, 0)])  48.3 us
    pallas_call x3, Pallas kernels, hidden_part(): pl.pallas_call(functools.partial(hidden_kernel, layout, first, last), in_...  29.5 us
    ppermute x14, starting transfers between devices, on_device(): lax.ppermute(value, ('line', 'side'), [(2 * i + y, 2 * i + 1 - y) for i i...  24 us
    ppermute x30, starting transfers between devices, swap(): return lax.ppermute(value, axis, [(0, 1), (1, 0)])  21.4 us
    unnamed x73, local copies, waits for them, and re-layouts  21.3 us
    ppermute x6, starting transfers between devices, on_device(): rights.append(lax.ppermute(rights[-1], 'line', right))  12.5 us
    pallas_call x2, Pallas kernels, project(): pl.pallas_call(functools.partial(project_kernel, slots, start, first), in...  11.3 us
    ppermute x5, starting transfers between devices, shift(): lax.ppermute(value, 'line', [(i, (i + amount) % size) for i in range(size)])  9.38 us
  transfers between devices with their start and end apart: 63, of which 22 were waited for; matrix products, arithmetic and copies ran while one was open for 6% of the time, Pallas kernels for 12%

profile of v2, /device:TPU:0, one launch (start us, length us, event | category | flops | bytes accessed | tf_op | source)
XLA Modules:
  0.0 241.5 jit_solution(15687465471769746780)
XLA Ops:
  1.1 6.7 %shard_map.109 = bf16[32,64,512]{2,1,0:T(8,128)(2,1)S(1)} custom-call(s32[32]{0:T(128)S(1)} %copy-done.23, bf16[32,64,576]{2,1,0:T(8,128)(2,1)} %query_ref.1, bf16[32,576,128]{2,1,0:T(8,128)(2,1)} %bitcast.117), custom_call_target="tpu_custom_call" | custom-call | flops 570425344 | bytes 9175040 | tf_op jit(solution)/shard_map/pallas_call | solution.py:67
  7.9 2.0 fusion.19
  10.0 4.5 %collective-permute-start.1 = (bf16[32,4096]{1,0:T(8,128)(2,1)S(1)}, bf16[32,4096]{1,0:T(8,128)(2,1)S(1)}, u32[]{:S(2)}, u32[]{:S(2)}) collective-permute-start(bf16[32,4096]{1,0:T(8,128)(2,1)S(1)} %get-tuple-element.47.refs_0_), channel_id=1, source_target_pairs={{0,4},{4,8},{8,12},{1,5},{5,9},{9,13},{2,6},{6,10},{10,14},{3,7},{... | collective-permute-start | bytes 786440 | tf_op jit(solution)/shard_map/ppermute | solution.py:389
  14.5 1.3 collective-permute-start.4
  15.8 1.6 collective-permute-start.8
  20.8 4.5 %collective-permute-start.15 = (bf16[32,4096]{1,0:T(8,128)(2,1)S(1)}, bf16[32,4096]{1,0:T(8,128)(2,1)S(1)}, u32[]{:S(2)}, u32[]{:S(2)}) collective-permute-start(bf16[32,4096]{1,0:T(8,128)(2,1)S(1)} %get-tuple-element.26.refs_1_), channel_id=1, source_target_pairs={{0,4},{4,8},{8,12},{1,5},{5,9},{9,13},{2,6},{6,10},{10,14},{3,7},{... | collective-permute-start | bytes 786440 | tf_op jit(solution)/shard_map/ppermute | solution.py:389
  25.3 1.3 collective-permute-start.16
  27.9 3.3 %collective-permute-done.15.refs_2_ = bf16[32,4096]{1,0:T(8,128)(2,1)S(1)} collective-permute-done((bf16[32,4096]{1,0:T(8,128)(2,1)S(1)}, bf16[32,4096]{1,0:T(8,128)(2,1)S(1)}, u32[]{:S(2)}, u32[]{:S(2)}) %collective-permute-start.15) | collective-permute-done | bytes 262176 | tf_op jit(solution)/shard_map/ppermute | solution.py:389
  31.2 1.3 collective-permute-start.5
  32.5 2.9 %collective-permute-done.16.refs_3_ = bf16[32,4096]{1,0:T(8,128)(2,1)S(1)} collective-permute-done((bf16[32,4096]{1,0:T(8,128)(2,1)S(1)}, bf16[32,4096]{1,0:T(8,128)(2,1)S(1)}, u32[]{:S(2)}, u32[]{:S(2)}) %collective-permute-start.16) | collective-permute-done | bytes 262176 | tf_op jit(solution)/shard_map/ppermute | solution.py:390
  35.3 2.4 collective-permute-start.10
  39.1 1.3 collective-permute-start.18
  42.0 2.4 collective-permute-done.10.refs_9_
  45.1 1.3 collective-permute-start.7
  47.1 2.4 collective-permute-start.12
  50.2 3.8 %collective-permute-done.18.refs_5_ = bf16[32,4096]{1,0:T(8,128)(2,1)S(1)} collective-permute-done((bf16[32,4096]{1,0:T(8,128)(2,1)S(1)}, bf16[32,4096]{1,0:T(8,128)(2,1)S(1)}, u32[]{:S(2)}, u32[]{:S(2)}) %collective-permute-start.18) | collective-permute-done | bytes 262176 | tf_op jit(solution)/shard_map/ppermute | solution.py:390
  54.0 1.4 collective-permute-start.19
  56.1 1.3 collective-permute-start.20
  58.4 2.6 %collective-permute-start.14 = (bf16[32,4096]{1,0:T(8,128)(2,1)S(1)}, bf16[32,4096]{1,0:T(8,128)(2,1)S(1)}, u32[]{:S(2)}, u32[]{:S(2)}) collective-permute-start(bf16[32,4096]{1,0:T(8,128)(2,1)S(1)} %collective-permute-done.7.refs_6_), channel_id=1, source_target_pairs={{0,2},{2,0},{1,3},{3,1},{16,18},{18,16},{17,19},{19,17}} | collective-permute-start | bytes 786440 | tf_op jit(solution)/shard_map/ppermute | solution.py:393
  64.5 3.2 %collective-permute-start.23 = (bf16[32,4096]{1,0:T(8,128)(2,1)S(1)}, bf16[32,4096]{1,0:T(8,128)(2,1)}, u32[]{:S(2)}, u32[]{:S(2)}) collective-permute-start(bf16[32,4096]{1,0:T(8,128)(2,1)S(1)} %collective-permute-done.16.refs_3_), channel_id=1, source_target_pairs={{0,2},{2,0},{4,6},{6,4},{8,10},{10,8},{1,3},{3,1},{5,7},{7,5},{9,1... | collective-permute-start | bytes 786440 | tf_op jit(solution)/shard_map/ppermute | solution.py:393
  67.8 1.4 collective-permute-start.24
  69.9 2.6 %collective-permute-start.25 = (bf16[32,4096]{1,0:T(8,128)(2,1)S(1)}, bf16[32,4096]{1,0:T(8,128)(2,1)}, u32[]{:S(2)}, u32[]{:S(2)}) collective-permute-start(bf16[32,4096]{1,0:T(8,128)(2,1)S(1)} %collective-permute-done.18.refs_5_), channel_id=1, source_target_pairs={{0,2},{2,0},{4,6},{6,4},{1,3},{3,1},{5,7},{7,5},{16,18},{18,16},{2... | collective-permute-start | bytes 786440 | tf_op jit(solution)/shard_map/ppermute | solution.py:393
  73.2 1.4 collective-permute-start.26
  75.3 3.2 %collective-permute-start.27 = (bf16[32,4096]{1,0:T(8,128)(2,1)}, bf16[32,4096]{1,0:T(8,128)(2,1)}, u32[]{:S(2)}, u32[]{:S(2)}) collective-permute-start(bf16[32,4096]{1,0:T(8,128)(2,1)} %collective-permute-done.20.refs_7_), channel_id=1, source_target_pairs={{0,2},{2,0},{1,3},{3,1},{16,18},{18,16},{17,19},{19,17}} | collective-permute-start | bytes 786440 | tf_op jit(solution)/shard_map/ppermute | solution.py:393
  86.1 5.5 %shard_map.110.refs_0_ = f32[256,896]{1,0:T(8,128)S(1)} custom-call(s32[17]{0:T(128)S(1)} %stack.164.place_ref, bf16[448,8192]{1,0:T(8,128)(2,1)} %bitcast.115, bf16[448,8192]{1,0:T(8,128)(2,1)} %collective-permute-done.3.sibling_ref, bf16[32,4096]{1,0:T(8,128)(2,1)S(1)} %get-tuple-element.47.refs_0_, bf16[32,4096]{1,0:T(8,128)(2,1)S(1)} %collective-permute-done.1.refs_1_, ...), custom_call_target="tpu_custom_call" | custom-call | flops 1879048192 | bytes 9437184 | tf_op jit(solution)/shard_map/pallas_call | solution.py:157
  91.7 5.7 %shard_map.111 = bf16[256,896]{1,0:T(8,128)(2,1)S(1)} custom-call(s32[17]{0:T(128)S(1)} %stack.164.place_ref, bf16[448,8192]{1,0:T(8,128)(2,1)} %bitcast.116, bf16[448,8192]{1,0:T(8,128)(2,1)} %collective-permute-done.3.sibling_ref, f32[256,896]{1,0:T(8,128)S(1)} %shard_map.110.refs_0_, bf16[32,4096]{1,0:T(8,128)(2,1)S(1)} %get-tuple-element.26.refs_1_, ...), custom_call_target="tpu_custom_call" | custom-call | flops 1879048192 | bytes 9437184 | tf_op jit(solution)/shard_map/pallas_call | solution.py:157
  97.5 1.6 collective-permute-start.28
  99.1 5.2 %collective-permute-done.28 = bf16[128,896]{1,0:T(8,128)(2,1)S(1)} collective-permute-done((bf16[128,896]{1,0:T(8,128)(2,1)S(1)}, bf16[128,896]{1,0:T(8,128)(2,1)S(1)}, u32[]{:S(2)}, u32[]{:S(2)}) %collective-permute-start.28) | collective-permute-done | bytes 229408 | tf_op jit(solution)/shard_map/ppermute | solution.py:24
  104.4 1.6 collective-permute-start.32
  106.0 4.5 %collective-permute-done.32 = bf16[128,896]{1,0:T(8,128)(2,1)S(1)} collective-permute-done((bf16[128,896]{1,0:T(8,128)(2,1)S(1)}, bf16[128,896]{1,0:T(8,128)(2,1)S(1)}, u32[]{:S(2)}, u32[]{:S(2)}) %collective-permute-start.32) | collective-permute-done | bytes 229408 | tf_op jit(solution)/shard_map/ppermute | solution.py:24
  110.5 1.2 collective-permute-start.33
  111.8 3.4 %collective-permute-start.39 = (bf16[128,896]{1,0:T(8,128)(2,1)S(1)}, bf16[128,896]{1,0:T(8,128)(2,1)S(1)}, u32[]{:S(2)}, u32[]{:S(2)}) collective-permute-start(bf16[128,896]{1,0:T(8,128)(2,1)S(1)} %fusion.27), channel_id=1, source_target_pairs={{0,12},{4,0},{8,4},{12,8},{1,13},{5,1},{9,5},{13,9},{2,14},{6,2},{... | collective-permute-start | bytes 688136 | tf_op jit(solution)/shard_map/ppermute | solution.py:29
  115.9 3.1 %collective-permute-done.39 = bf16[128,896]{1,0:T(8,128)(2,1)S(1)} collective-permute-done((bf16[128,896]{1,0:T(8,128)(2,1)S(1)}, bf16[128,896]{1,0:T(8,128)(2,1)S(1)}, u32[]{:S(2)}, u32[]{:S(2)}) %collective-permute-start.39) | collective-permute-done | bytes 229408 | tf_op jit(solution)/shard_map/ppermute | solution.py:29
  119.0 1.5 collective-permute-start.40
  122.6 4.5 %collective-permute-done.40 = bf16[128,896]{1,0:T(8,128)(2,1)S(1)} collective-permute-done((bf16[128,896]{1,0:T(8,128)(2,1)S(1)}, bf16[128,896]{1,0:T(8,128)(2,1)S(1)}, u32[]{:S(2)}, u32[]{:S(2)}) %collective-permute-start.40) | collective-permute-done | bytes 229408 | tf_op jit(solution)/shard_map/ppermute | solution.py:420
  129.0 1.3 collective-permute-start.46
  130.4 3.1 %collective-permute-done.30 = bf16[128,896]{1,0:T(8,128)(2,1)S(1)} collective-permute-done((bf16[128,896]{1,0:T(8,128)(2,1)S(1)}, bf16[128,896]{1,0:T(8,128)(2,1)S(1)}, u32[]{:S(2)}, u32[]{:S(2)}) %collective-permute-start.30) | collective-permute-done | bytes 229408 | tf_op jit(solution)/shard_map/ppermute | solution.py:24
  133.5 2.0 collective-permute-done.41
  136.5 1.2 collective-permute-start.42
  137.7 7.7 %shard_map.112 = (f32[512,1024]{1,0:T(8,128)S(1)}, f32[512,1024]{1,0:T(8,128)S(1)}) custom-call(s32[2]{0:T(128)S(1)} %get-tuple-element.28.place_ref, bf16[2,128,896]{2,1,0:T(8,128)(2,1)S(1)} %pad_maximum_fusion.3.refs_0_, bf16[2,128,896]{2,1,0:T(8,128)(2,1)S(1)} %collective-permute-done.33.refs_1_, ...), custom_call_target="tpu_custom_call" | custom-call | flops 3758096384 | bytes 7340032 | tf_op jit(solution)/shard_map/pallas_call | solution.py:298
  145.4 1.3 copy-done
  147.8 5.2 %collective-permute-done.31.refs_1_ = bf16[2,128,896]{2,1,0:T(8,128)(2,1)} collective-permute-done((bf16[2,128,896]{2,1,0:T(8,128)(2,1)S(1)}, bf16[2,128,896]{2,1,0:T(8,128)(2,1)}, u32[]{:S(2)}, u32[]{:S(2)}) %collective-permute-start.31) | collective-permute-done | bytes 458784 | tf_op jit(solution)/shard_map/ppermute | solution.py:24
  154.3 1.6 copy-done.1
  156.9 8.8 %shard_map.113 = (f32[512,1024]{1,0:T(8,128)S(1)}, f32[512,1024]{1,0:T(8,128)S(1)}) custom-call(s32[2]{0:T(128)S(1)} %get-tuple-element.33.place_ref, bf16[2,128,896]{2,1,0:T(8,128)(2,1)S(1)} %pad_maximum_fusion.5.refs_0_, bf16[2,128,896]{2,1,0:T(8,128)(2,1)} %collective-permute-done.46.refs_1_, bf16[2,128,896]{2,1,0:T(8,128)(2,1)S(1)} %copy-done.4, ...), custom_call_target="tpu_custom_call" | custom-call | flops 3758096384 | bytes 7340032 | tf_op jit(solution)/shard_map/pallas_call | solution.py:298
  165.8 13.0 %shard_map.114 = bf16[512,1024]{1,0:T(8,128)(2,1)S(1)} custom-call(s32[3]{0:T(128)S(1)} %pad_add_fusion.2.place_ref, bf16[2,128,896]{2,1,0:T(8,128)(2,1)S(1)} %pad_maximum_fusion.2.refs_0_, bf16[2,128,896]{2,1,0:T(8,128)(2,1)} %collective-permute-done.31.refs_1_, bf16[2,128,896]{2,1,0:T(8,128)(2,1)} %collective-permute-done.36.refs_2_, ...), custom_call_target="tpu_custom_call" | custom-call | flops 7516192768 | bytes 14680064 | tf_op jit(solution)/shard_map/pallas_call | solution.py:298
  178.8 4.3 %fusion.7 = bf16[256,7168]{1,0:T(8,128)(2,1)S(1)} fusion(bf16[1,1024,7168]{2,1,0:T(8,128)(2,1)S(1)} %bitcast.139, bf16[512,1024]{1,0:T(8,128)(2,1)S(1)} %shard_map.114), kind=kOutput, calls=%fused_computation.5 | convolution fusion | flops 3759931392 | bytes 18874368 | tf_op jit(solution)/shard_map/dot_general | solution.py:461
  183.7 1.4 pad_maximum_fusion.1
  185.7 4.5 %fusion.4 = bf16[256,7168]{1,0:T(8,128)(2,1)S(1)} fusion(bf16[1,1024,7168]{2,1,0:T(8,128)(2,1)S(1)} %bitcast.139, bf16[512,1024]{1,0:T(8,128)(2,1)S(1)} %shard_map.114), kind=kOutput, calls=%fused_computation.4 | convolution fusion | flops 3759931392 | bytes 18874368 | tf_op jit(solution)/shard_map/dot_general | solution.py:461
  190.2 1.8 copy-done.25
  192.6 1.1 collective-permute-start.50
  193.7 1.2 collective-permute-start.53
  194.9 10.1 %collective-permute-done.50 = bf16[128,1792]{1,0:T(8,128)(2,1)S(1)} collective-permute-done((bf16[128,1792]{1,0:T(8,128)(2,1)S(1)}, bf16[128,1792]{1,0:T(8,128)(2,1)S(1)}, u32[]{:S(2)}, u32[]{:S(2)}) %collective-permute-start.50) | collective-permute-done | bytes 458784 | tf_op jit(solution)/shard_map/ppermute | solution.py:24
  205.2 2.4 %fusion.12 = (bf16[256,1792]{1,0:T(8,128)(2,1)S(1)}, bf16[256,1792]{1,0:T(8,128)(2,1)S(1)}) fusion(bf16[2,256,1792]{2,1,0:T(8,128)(2,1)} %collective-permute-done.56, bf16[256,7168]{1,0:T(8,128)(2,1)} %copy-done.25, s32[]{:T(128)S(6)} %select_n.217, s32[]{:T(128)S(6)} %select_n.216), kind=kLoop, calls=%fused_computation.11 | loop fusion | flops 3670016 | bytes 5505032 | tf_op jit(solution)/shard_map/convert_element_type | solution.py:321
  207.7 1.1 collective-permute-start.60
  208.8 1.2 collective-permute-start.51
  210.9 1.3 collective-permute-start.57
  212.2 5.2 %collective-permute-done.51 = bf16[128,896]{1,0:T(8,128)(2,1)S(1)} collective-permute-done((bf16[128,896]{1,0:T(8,128)(2,1)S(1)}, bf16[128,896]{1,0:T(8,128)(2,1)S(1)}, u32[]{:S(2)}, u32[]{:S(2)}) %collective-permute-start.51) | collective-permute-done | bytes 229408 | tf_op jit(solution)/shard_map/ppermute | solution.py:24
  217.5 1.6 collective-permute-start.52
  219.1 5.1 %collective-permute-done.54 = bf16[128,896]{1,0:T(8,128)(2,1)S(1)} collective-permute-done((bf16[128,896]{1,0:T(8,128)(2,1)S(1)}, bf16[128,896]{1,0:T(8,128)(2,1)S(1)}, u32[]{:S(2)}, u32[]{:S(2)}) %collective-permute-start.54) | collective-permute-done | bytes 229408 | tf_op jit(solution)/shard_map/ppermute | solution.py:24
  224.3 2.1 collective-permute-start.55
  228.3 4.4 %collective-permute-done.58 = bf16[128,896]{1,0:T(8,128)(2,1)S(1)} collective-permute-done((bf16[128,896]{1,0:T(8,128)(2,1)S(1)}, bf16[128,896]{1,0:T(8,128)(2,1)S(1)}, u32[]{:S(2)}, u32[]{:S(2)}) %collective-permute-start.58) | collective-permute-done | bytes 229408 | tf_op jit(solution)/shard_map/ppermute | solution.py:24
  232.7 2.2 collective-permute-start.59
  234.9 3.9 %collective-permute-done.59 = bf16[128,896]{1,0:T(8,128)(2,1)S(1)} collective-permute-done((bf16[128,896]{1,0:T(8,128)(2,1)S(1)}, bf16[128,896]{1,0:T(8,128)(2,1)S(1)}, u32[]{:S(2)}, u32[]{:S(2)}) %collective-permute-start.59) | collective-permute-done | bytes 229408 | tf_op jit(solution)/shard_map/ppermute | solution.py:29
  239.2 1.3 collective-permute-done.62
  (193 shorter events, 40.9 us)
Async XLA Ops:
  0.0 38.4 %collective-permute-start.3 = (bf16[448,8192]{1,0:T(8,128)(2,1)}, bf16[448,8192]{1,0:T(8,128)(2,1)}, u32[]{:S(2)}, u32[]{:S(2)}) collective-permute-start(bf16[448,8192]{1,0:T(8,128)(2,1)} %bitcast.114), channel_id=1, source_target_pairs={{0,1},{1,0},{2,3},{3,2},{4,5},{5,4},{6,7},{7,6},{8,9},{9,8},{10,11... | collective-permute-start | bytes 22020104 | tf_op jit(solution)/shard_map/ppermute | solution.py:24
  10.0 15.3 %collective-permute-start.1 = (bf16[32,4096]{1,0:T(8,128)(2,1)S(1)}, bf16[32,4096]{1,0:T(8,128)(2,1)S(1)}, u32[]{:S(2)}, u32[]{:S(2)}) collective-permute-start(bf16[32,4096]{1,0:T(8,128)(2,1)S(1)} %get-tuple-element.47.refs_0_), channel_id=1, source_target_pairs={{0,4},{4,8},{8,12},{1,5},{5,9},{9,13},{2,6},{6,10},{10,14},{3,7},{... | collective-permute-start | bytes 786440 | tf_op jit(solution)/shard_map/ppermute | solution.py:389
  14.5 12.1 %collective-permute-start.4 = (bf16[32,4096]{1,0:T(8,128)(2,1)S(1)}, bf16[32,4096]{1,0:T(8,128)(2,1)S(1)}, u32[]{:S(2)}, u32[]{:S(2)}) collective-permute-start(bf16[32,4096]{1,0:T(8,128)(2,1)S(1)} %get-tuple-element.47.refs_0_), channel_id=1, source_target_pairs={{4,0},{8,4},{12,8},{5,1},{9,5},{13,9},{6,2},{10,6},{14,10},{7,3},{... | collective-permute-start | bytes 786440 | tf_op jit(solution)/shard_map/ppermute | solution.py:390
  15.8 11.5 %collective-permute-start.8 = (bf16[32,4096]{1,0:T(8,128)(2,1)S(1)}, bf16[32,4096]{1,0:T(8,128)(2,1)S(1)}, u32[]{:S(2)}, u32[]{:S(2)}) collective-permute-start(bf16[32,4096]{1,0:T(8,128)(2,1)S(1)} %get-tuple-element.47.refs_0_), channel_id=1, source_target_pairs={{0,2},{2,0},{4,6},{6,4},{8,10},{10,8},{12,14},{14,12},{1,3},{3,1},... | collective-permute-start | bytes 786440 | tf_op jit(solution)/shard_map/ppermute | solution.py:393
  17.7 1.4 collective-permute-start
  20.8 10.4 %collective-permute-start.15 = (bf16[32,4096]{1,0:T(8,128)(2,1)S(1)}, bf16[32,4096]{1,0:T(8,128)(2,1)S(1)}, u32[]{:S(2)}, u32[]{:S(2)}) collective-permute-start(bf16[32,4096]{1,0:T(8,128)(2,1)S(1)} %get-tuple-element.26.refs_1_), channel_id=1, source_target_pairs={{0,4},{4,8},{8,12},{1,5},{5,9},{9,13},{2,6},{6,10},{10,14},{3,7},{... | collective-permute-start | bytes 786440 | tf_op jit(solution)/shard_map/ppermute | solution.py:389
  25.3 10.0 %collective-permute-start.16 = (bf16[32,4096]{1,0:T(8,128)(2,1)S(1)}, bf16[32,4096]{1,0:T(8,128)(2,1)S(1)}, u32[]{:S(2)}, u32[]{:S(2)}) collective-permute-start(bf16[32,4096]{1,0:T(8,128)(2,1)S(1)} %get-tuple-element.26.refs_1_), channel_id=1, source_target_pairs={{4,0},{8,4},{12,8},{5,1},{9,5},{13,9},{6,2},{10,6},{14,10},{7,3},{... | collective-permute-start | bytes 786440 | tf_op jit(solution)/shard_map/ppermute | solution.py:390
  26.7 11.1 %collective-permute-start.2 = (bf16[32,4096]{1,0:T(8,128)(2,1)S(1)}, bf16[32,4096]{1,0:T(8,128)(2,1)S(1)}, u32[]{:S(2)}, u32[]{:S(2)}) collective-permute-start(bf16[32,4096]{1,0:T(8,128)(2,1)S(1)} %collective-permute-done.1.refs_1_), channel_id=1, source_target_pairs={{4,8},{8,12},{5,9},{9,13},{6,10},{10,14},{7,11},{11,15},{20,24},{2... | collective-permute-start | bytes 786440 | tf_op jit(solution)/shard_map/ppermute | solution.py:389
  27.4 11.8 %collective-permute-start.21 = (bf16[32,4096]{1,0:T(8,128)(2,1)S(1)}, bf16[32,4096]{1,0:T(8,128)(2,1)S(1)}, u32[]{:S(2)}, u32[]{:S(2)}) collective-permute-start(bf16[32,4096]{1,0:T(8,128)(2,1)S(1)} %get-tuple-element.26.refs_1_), channel_id=1, source_target_pairs={{0,2},{2,0},{4,6},{6,4},{8,10},{10,8},{12,14},{14,12},{1,3},{3,1},... | collective-permute-start | bytes 786440 | tf_op jit(solution)/shard_map/ppermute | solution.py:393
  31.2 10.2 %collective-permute-start.5 = (bf16[32,4096]{1,0:T(8,128)(2,1)S(1)}, bf16[32,4096]{1,0:T(8,128)(2,1)S(1)}, u32[]{:S(2)}, u32[]{:S(2)}) collective-permute-start(bf16[32,4096]{1,0:T(8,128)(2,1)S(1)} %collective-permute-done.4.refs_2_), channel_id=1, source_target_pairs={{4,0},{8,4},{5,1},{9,5},{6,2},{10,6},{7,3},{11,7},{20,16},{24,20},... | collective-permute-start | bytes 786440 | tf_op jit(solution)/shard_map/ppermute | solution.py:390
  35.3 9.1 %collective-permute-start.10 = (bf16[32,4096]{1,0:T(8,128)(2,1)S(1)}, bf16[32,4096]{1,0:T(8,128)(2,1)S(1)}, u32[]{:S(2)}, u32[]{:S(2)}) collective-permute-start(bf16[32,4096]{1,0:T(8,128)(2,1)S(1)} %collective-permute-done.4.refs_2_), channel_id=1, source_target_pairs={{0,2},{2,0},{4,6},{6,4},{8,10},{10,8},{1,3},{3,1},{5,7},{7,5},{9,1... | collective-permute-start | bytes 786440 | tf_op jit(solution)/shard_map/ppermute | solution.py:393
  37.7 8.7 %collective-permute-start.9 = (bf16[32,4096]{1,0:T(8,128)(2,1)S(1)}, bf16[32,4096]{1,0:T(8,128)(2,1)S(1)}, u32[]{:S(2)}, u32[]{:S(2)}) collective-permute-start(bf16[32,4096]{1,0:T(8,128)(2,1)S(1)} %collective-permute-done.1.refs_1_), channel_id=1, source_target_pairs={{4,6},{6,4},{8,10},{10,8},{12,14},{14,12},{5,7},{7,5},{9,11},{11,9... | collective-permute-start | bytes 786440 | tf_op jit(solution)/shard_map/ppermute | solution.py:393
  38.4 11.1 %collective-permute-start.17 = (bf16[32,4096]{1,0:T(8,128)(2,1)S(1)}, bf16[32,4096]{1,0:T(8,128)(2,1)S(1)}, u32[]{:S(2)}, u32[]{:S(2)}) collective-permute-start(bf16[32,4096]{1,0:T(8,128)(2,1)S(1)} %collective-permute-done.15.refs_2_), channel_id=1, source_target_pairs={{4,8},{8,12},{5,9},{9,13},{6,10},{10,14},{7,11},{11,15},{20,24},{2... | collective-permute-start | bytes 786440 | tf_op jit(solution)/shard_map/ppermute | solution.py:389
  39.1 14.9 %collective-permute-start.18 = (bf16[32,4096]{1,0:T(8,128)(2,1)S(1)}, bf16[32,4096]{1,0:T(8,128)(2,1)S(1)}, u32[]{:S(2)}, u32[]{:S(2)}) collective-permute-start(bf16[32,4096]{1,0:T(8,128)(2,1)S(1)} %collective-permute-done.16.refs_3_), channel_id=1, source_target_pairs={{4,0},{8,4},{5,1},{9,5},{6,2},{10,6},{7,3},{11,7},{20,16},{24,20},... | collective-permute-start | bytes 786440 | tf_op jit(solution)/shard_map/ppermute | solution.py:390
  41.3 14.0 %collective-permute-start.22 = (bf16[32,4096]{1,0:T(8,128)(2,1)S(1)}, bf16[32,4096]{1,0:T(8,128)(2,1)S(1)}, u32[]{:S(2)}, u32[]{:S(2)}) collective-permute-start(bf16[32,4096]{1,0:T(8,128)(2,1)S(1)} %collective-permute-done.15.refs_2_), channel_id=1, source_target_pairs={{4,6},{6,4},{8,10},{10,8},{12,14},{14,12},{5,7},{7,5},{9,11},{11,9... | collective-permute-start | bytes 786440 | tf_op jit(solution)/shard_map/ppermute | solution.py:393
  45.1 13.3 %collective-permute-start.7 = (bf16[32,4096]{1,0:T(8,128)(2,1)S(1)}, bf16[32,4096]{1,0:T(8,128)(2,1)S(1)}, u32[]{:S(2)}, u32[]{:S(2)}) collective-permute-start(bf16[32,4096]{1,0:T(8,128)(2,1)S(1)} %collective-permute-done.5.refs_4_), channel_id=1, source_target_pairs={{4,0},{5,1},{6,2},{7,3},{20,16},{21,17},{22,18},{23,19}} | collective-permute-start | bytes 786440 | tf_op jit(solution)/shard_map/ppermute | solution.py:390
  47.1 14.6 %collective-permute-start.12 = (bf16[32,4096]{1,0:T(8,128)(2,1)S(1)}, bf16[32,4096]{1,0:T(8,128)(2,1)S(1)}, u32[]{:S(2)}, u32[]{:S(2)}) collective-permute-start(bf16[32,4096]{1,0:T(8,128)(2,1)S(1)} %collective-permute-done.5.refs_4_), channel_id=1, source_target_pairs={{0,2},{2,0},{4,6},{6,4},{1,3},{3,1},{5,7},{7,5},{16,18},{18,16},{2... | collective-permute-start | bytes 786440 | tf_op jit(solution)/shard_map/ppermute | solution.py:393
  49.5 13.6 %collective-permute-start.6 = (bf16[32,4096]{1,0:T(8,128)(2,1)S(1)}, bf16[32,4096]{1,0:T(8,128)(2,1)S(1)}, u32[]{:S(2)}, u32[]{:S(2)}) collective-permute-start(bf16[32,4096]{1,0:T(8,128)(2,1)S(1)} %collective-permute-done.2.refs_3_), channel_id=1, source_target_pairs={{8,12},{9,13},{10,14},{11,15},{24,28},{25,29},{26,30},{27,31}} | collective-permute-start | bytes 786440 | tf_op jit(solution)/shard_map/ppermute | solution.py:389
  54.0 10.5 %collective-permute-start.19 = (bf16[32,4096]{1,0:T(8,128)(2,1)S(1)}, bf16[32,4096]{1,0:T(8,128)(2,1)}, u32[]{:S(2)}, u32[]{:S(2)}) collective-permute-start(bf16[32,4096]{1,0:T(8,128)(2,1)S(1)} %collective-permute-done.17.refs_4_), channel_id=1, source_target_pairs={{8,12},{9,13},{10,14},{11,15},{24,28},{25,29},{26,30},{27,31}} | collective-permute-start | bytes 786440 | tf_op jit(solution)/shard_map/ppermute | solution.py:389
  56.1 11.7 %collective-permute-start.20 = (bf16[32,4096]{1,0:T(8,128)(2,1)S(1)}, bf16[32,4096]{1,0:T(8,128)(2,1)}, u32[]{:S(2)}, u32[]{:S(2)}) collective-permute-start(bf16[32,4096]{1,0:T(8,128)(2,1)S(1)} %collective-permute-done.18.refs_5_), channel_id=1, source_target_pairs={{4,0},{5,1},{6,2},{7,3},{20,16},{21,17},{22,18},{23,19}} | collective-permute-start | bytes 786440 | tf_op jit(solution)/shard_map/ppermute | solution.py:390
  58.4 10.7 %collective-permute-start.14 = (bf16[32,4096]{1,0:T(8,128)(2,1)S(1)}, bf16[32,4096]{1,0:T(8,128)(2,1)S(1)}, u32[]{:S(2)}, u32[]{:S(2)}) collective-permute-start(bf16[32,4096]{1,0:T(8,128)(2,1)S(1)} %collective-permute-done.7.refs_6_), channel_id=1, source_target_pairs={{0,2},{2,0},{1,3},{3,1},{16,18},{18,16},{17,19},{19,17}} | collective-permute-start | bytes 786440 | tf_op jit(solution)/shard_map/ppermute | solution.py:393
  62.4 10.0 %collective-permute-start.11 = (bf16[32,4096]{1,0:T(8,128)(2,1)S(1)}, bf16[32,4096]{1,0:T(8,128)(2,1)S(1)}, u32[]{:S(2)}, u32[]{:S(2)}) collective-permute-start(bf16[32,4096]{1,0:T(8,128)(2,1)S(1)} %collective-permute-done.2.refs_3_), channel_id=1, source_target_pairs={{8,10},{10,8},{12,14},{14,12},{9,11},{11,9},{13,15},{15,13},{24,26... | collective-permute-start | bytes 786440 | tf_op jit(solution)/shard_map/ppermute | solution.py:393
  63.1 11.4 %collective-permute-start.13 = (bf16[32,4096]{1,0:T(8,128)(2,1)S(1)}, bf16[32,4096]{1,0:T(8,128)(2,1)S(1)}, u32[]{:S(2)}, u32[]{:S(2)}) collective-permute-start(bf16[32,4096]{1,0:T(8,128)(2,1)S(1)} %collective-permute-done.6.refs_5_), channel_id=1, source_target_pairs={{12,14},{14,12},{13,15},{15,13},{28,30},{30,28},{29,31},{31,29}} | collective-permute-start | bytes 786440 | tf_op jit(solution)/shard_map/ppermute | solution.py:393
  64.5 27.1 %collective-permute-start.23 = (bf16[32,4096]{1,0:T(8,128)(2,1)S(1)}, bf16[32,4096]{1,0:T(8,128)(2,1)}, u32[]{:S(2)}, u32[]{:S(2)}) collective-permute-start(bf16[32,4096]{1,0:T(8,128)(2,1)S(1)} %collective-permute-done.16.refs_3_), channel_id=1, source_target_pairs={{0,2},{2,0},{4,6},{6,4},{8,10},{10,8},{1,3},{3,1},{5,7},{7,5},{9,1... | collective-permute-start | bytes 786440 | tf_op jit(solution)/shard_map/ppermute | solution.py:393
  67.8 23.9 %collective-permute-start.24 = (bf16[32,4096]{1,0:T(8,128)(2,1)S(1)}, bf16[32,4096]{1,0:T(8,128)(2,1)}, u32[]{:S(2)}, u32[]{:S(2)}) collective-permute-start(bf16[32,4096]{1,0:T(8,128)(2,1)S(1)} %collective-permute-done.17.refs_4_), channel_id=1, source_target_pairs={{8,10},{10,8},{12,14},{14,12},{9,11},{11,9},{13,15},{15,13},{24,26... | collective-permute-start | bytes 786440 | tf_op jit(solution)/shard_map/ppermute | solution.py:393
  69.9 21.8 %collective-permute-start.25 = (bf16[32,4096]{1,0:T(8,128)(2,1)S(1)}, bf16[32,4096]{1,0:T(8,128)(2,1)}, u32[]{:S(2)}, u32[]{:S(2)}) collective-permute-start(bf16[32,4096]{1,0:T(8,128)(2,1)S(1)} %collective-permute-done.18.refs_5_), channel_id=1, source_target_pairs={{0,2},{2,0},{4,6},{6,4},{1,3},{3,1},{5,7},{7,5},{16,18},{18,16},{2... | collective-permute-start | bytes 786440 | tf_op jit(solution)/shard_map/ppermute | solution.py:393
  73.2 18.5 %collective-permute-start.26 = (bf16[32,4096]{1,0:T(8,128)(2,1)}, bf16[32,4096]{1,0:T(8,128)(2,1)}, u32[]{:S(2)}, u32[]{:S(2)}) collective-permute-start(bf16[32,4096]{1,0:T(8,128)(2,1)} %collective-permute-done.19.refs_6_), channel_id=1, source_target_pairs={{12,14},{14,12},{13,15},{15,13},{28,30},{30,28},{29,31},{31,29}} | collective-permute-start | bytes 786440 | tf_op jit(solution)/shard_map/ppermute | solution.py:393
  75.3 16.4 %collective-permute-start.27 = (bf16[32,4096]{1,0:T(8,128)(2,1)}, bf16[32,4096]{1,0:T(8,128)(2,1)}, u32[]{:S(2)}, u32[]{:S(2)}) collective-permute-start(bf16[32,4096]{1,0:T(8,128)(2,1)} %collective-permute-done.20.refs_7_), channel_id=1, source_target_pairs={{0,2},{2,0},{1,3},{3,1},{16,18},{18,16},{17,19},{19,17}} | collective-permute-start | bytes 786440 | tf_op jit(solution)/shard_map/ppermute | solution.py:393
  97.5 6.8 %collective-permute-start.28 = (bf16[128,896]{1,0:T(8,128)(2,1)S(1)}, bf16[128,896]{1,0:T(8,128)(2,1)S(1)}, u32[]{:S(2)}, u32[]{:S(2)}) collective-permute-start(bf16[128,896]{1,0:T(8,128)(2,1)S(1)} %dynamic-slice_bitcast_fusion.4), channel_id=1, source_target_pairs={{0,16},{16,0},{1,17},{17,1},{2,18},{18,2},{3,19},{19,3},{4,20},{20... | collective-permute-start | bytes 688136 | tf_op jit(solution)/shard_map/ppermute | solution.py:24
  104.4 32.1 %copy-start.26 = (bf16[128,896]{1,0:T(8,128)(2,1)}, bf16[128,896]{1,0:T(8,128)(2,1)S(1)}, u32[]{:S(2)}) copy-start(bf16[128,896]{1,0:T(8,128)(2,1)S(1)} %fusion.27) | copy-start | bytes 688132
  104.4 6.1 %collective-permute-start.32 = (bf16[128,896]{1,0:T(8,128)(2,1)S(1)}, bf16[128,896]{1,0:T(8,128)(2,1)S(1)}, u32[]{:S(2)}, u32[]{:S(2)}) collective-permute-start(bf16[128,896]{1,0:T(8,128)(2,1)S(1)} %fusion.27), channel_id=1, source_target_pairs={{0,16},{16,0},{1,17},{17,1},{2,18},{18,2},{3,19},{19,3},{4,20},{20... | collective-permute-start | bytes 688136 | tf_op jit(solution)/shard_map/ppermute | solution.py:24
  106.0 9.3 %collective-permute-start.29 = (bf16[128,896]{1,0:T(8,128)(2,1)S(1)}, bf16[128,896]{1,0:T(8,128)(2,1)S(1)}, u32[]{:S(2)}, u32[]{:S(2)}) collective-permute-start(bf16[128,896]{1,0:T(8,128)(2,1)S(1)} %fusion.27), channel_id=1, source_target_pairs={{0,4},{4,8},{8,12},{12,0},{1,5},{5,9},{9,13},{13,1},{2,6},{6,10},{... | collective-permute-start | bytes 688136 | tf_op jit(solution)/shard_map/ppermute | solution.py:29
  110.5 12.1 %collective-permute-start.33 = (bf16[2,128,896]{2,1,0:T(8,128)(2,1)S(1)}, bf16[2,128,896]{2,1,0:T(8,128)(2,1)S(1)}, u32[]{:S(2)}, u32[]{:S(2)}) collective-permute-start(bf16[2,128,896]{2,1,0:T(8,128)(2,1)S(1)} %pad_maximum_fusion.3.refs_0_), channel_id=1, source_target_pairs={{0,2},{2,0},{1,3},{3,1},{4,6},{6,4},{5,7},{7,5},{8,10},{10,8},{9,1... | collective-permute-start | bytes 1376264 | tf_op jit(solution)/shard_map/ppermute | solution.py:24
  111.8 7.2 %collective-permute-start.39 = (bf16[128,896]{1,0:T(8,128)(2,1)S(1)}, bf16[128,896]{1,0:T(8,128)(2,1)S(1)}, u32[]{:S(2)}, u32[]{:S(2)}) collective-permute-start(bf16[128,896]{1,0:T(8,128)(2,1)S(1)} %fusion.27), channel_id=1, source_target_pairs={{0,12},{4,0},{8,4},{12,8},{1,13},{5,1},{9,5},{13,9},{2,14},{6,2},{... | collective-permute-start | bytes 688136 | tf_op jit(solution)/shard_map/ppermute | solution.py:29
  115.2 6.3 %collective-permute-start.38 = (bf16[128,896]{1,0:T(8,128)(2,1)S(1)}, bf16[128,896]{1,0:T(8,128)(2,1)S(1)}, u32[]{:S(2)}, u32[]{:S(2)}) collective-permute-start(bf16[128,896]{1,0:T(8,128)(2,1)S(1)} %collective-permute-done.29), channel_id=1, source_target_pairs={{4,8},{8,12},{5,9},{9,13},{6,10},{10,14},{7,11},{11,15},{20,24},{2... | collective-permute-start | bytes 688136 | tf_op jit(solution)/shard_map/ppermute | solution.py:419
  119.0 8.1 %collective-permute-start.40 = (bf16[128,896]{1,0:T(8,128)(2,1)S(1)}, bf16[128,896]{1,0:T(8,128)(2,1)S(1)}, u32[]{:S(2)}, u32[]{:S(2)}) collective-permute-start(bf16[128,896]{1,0:T(8,128)(2,1)S(1)} %collective-permute-done.39), channel_id=1, source_target_pairs={{4,0},{8,4},{5,1},{9,5},{6,2},{10,6},{7,3},{11,7},{20,16},{24,20},... | collective-permute-start | bytes 688136 | tf_op jit(solution)/shard_map/ppermute | solution.py:420
  120.4 16.1 %collective-permute-start.34 = (bf16[2,128,896]{2,1,0:T(8,128)(2,1)S(1)}, bf16[2,128,896]{2,1,0:T(8,128)(2,1)S(1)}, u32[]{:S(2)}, u32[]{:S(2)}) collective-permute-start(bf16[2,128,896]{2,1,0:T(8,128)(2,1)S(1)} %pad_maximum_fusion.3.refs_0_), channel_id=1, source_target_pairs={{0,1},{1,0},{2,3},{3,2},{4,5},{5,4},{6,7},{7,6},{8,9},{9,8},{10,11... | collective-permute-start | bytes 1376264 | tf_op jit(solution)/shard_map/ppermute | solution.py:24
  120.5 8.5 %collective-permute-start.45 = (bf16[128,896]{1,0:T(8,128)(2,1)S(1)}, bf16[128,896]{1,0:T(8,128)(2,1)S(1)}, u32[]{:S(2)}, u32[]{:S(2)}) collective-permute-start(bf16[128,896]{1,0:T(8,128)(2,1)S(1)} %collective-permute-done.39), channel_id=1, source_target_pairs={{0,2},{2,0},{1,3},{3,1},{4,6},{6,4},{5,7},{7,5},{8,10},{10,8},{9,1... | collective-permute-start | bytes 688136 | tf_op jit(solution)/shard_map/ppermute | solution.py:24
  121.5 11.9 %collective-permute-start.30 = (bf16[128,896]{1,0:T(8,128)(2,1)S(1)}, bf16[128,896]{1,0:T(8,128)(2,1)S(1)}, u32[]{:S(2)}, u32[]{:S(2)}) collective-permute-start(bf16[128,896]{1,0:T(8,128)(2,1)S(1)} %collective-permute-done.29), channel_id=1, source_target_pairs={{0,2},{2,0},{1,3},{3,1},{4,6},{6,4},{5,7},{7,5},{8,10},{10,8},{9,1... | collective-permute-start | bytes 688136 | tf_op jit(solution)/shard_map/ppermute | solution.py:24
  122.6 15.1 %collective-permute-start.35 = (bf16[2,128,896]{2,1,0:T(8,128)(2,1)S(1)}, bf16[2,128,896]{2,1,0:T(8,128)(2,1)S(1)}, u32[]{:S(2)}, u32[]{:S(2)}) collective-permute-start(bf16[2,128,896]{2,1,0:T(8,128)(2,1)S(1)} %collective-permute-done.33.refs_1_), channel_id=1, source_target_pairs={{0,1},{1,0},{2,3},{3,2},{4,5},{5,4},{6,7},{7,6},{8,9},{9,8},{10,11... | collective-permute-start | bytes 1376264 | tf_op jit(solution)/shard_map/ppermute | solution.py:24
  127.1 8.4 %collective-permute-start.41 = (bf16[128,896]{1,0:T(8,128)(2,1)S(1)}, bf16[128,896]{1,0:T(8,128)(2,1)S(1)}, u32[]{:S(2)}, u32[]{:S(2)}) collective-permute-start(bf16[128,896]{1,0:T(8,128)(2,1)S(1)} %broadcast_select_fusion), channel_id=1, source_target_pairs={{0,16},{16,0},{1,17},{17,1},{2,18},{18,2},{3,19},{19,3},{4,20},{20... | collective-permute-start | bytes 688136 | tf_op jit(solution)/shard_map/ppermute | solution.py:24
  129.0 17.7 %collective-permute-start.46 = (bf16[2,128,896]{2,1,0:T(8,128)(2,1)S(1)}, bf16[2,128,896]{2,1,0:T(8,128)(2,1)}, u32[]{:S(2)}, u32[]{:S(2)}) collective-permute-start(bf16[2,128,896]{2,1,0:T(8,128)(2,1)S(1)} %pad_maximum_fusion.5.refs_0_), channel_id=1, source_target_pairs={{0,16},{16,0},{1,17},{17,1},{2,18},{18,2},{3,19},{19,3},{4,20},{20... | collective-permute-start | bytes 1376264 | tf_op jit(solution)/shard_map/ppermute | solution.py:24
  133.5 19.5 %collective-permute-start.47 = (bf16[2,128,896]{2,1,0:T(8,128)(2,1)S(1)}, bf16[2,128,896]{2,1,0:T(8,128)(2,1)S(1)}, u32[]{:S(2)}, u32[]{:S(2)}) collective-permute-start(bf16[2,128,896]{2,1,0:T(8,128)(2,1)S(1)} %pad_maximum_fusion.5.refs_0_), channel_id=1, source_target_pairs={{0,1},{1,0},{2,3},{3,2},{4,5},{5,4},{6,7},{7,6},{8,9},{9,8},{10,11... | collective-permute-start | bytes 1376264 | tf_op jit(solution)/shard_map/ppermute | solution.py:24
  135.6 17.5 %collective-permute-start.31 = (bf16[2,128,896]{2,1,0:T(8,128)(2,1)S(1)}, bf16[2,128,896]{2,1,0:T(8,128)(2,1)}, u32[]{:S(2)}, u32[]{:S(2)}) collective-permute-start(bf16[2,128,896]{2,1,0:T(8,128)(2,1)S(1)} %pad_maximum_fusion.2.refs_0_), channel_id=1, source_target_pairs={{0,16},{16,0},{1,17},{17,1},{2,18},{18,2},{3,19},{19,3},{4,20},{20... | collective-permute-start | bytes 1376264 | tf_op jit(solution)/shard_map/ppermute | solution.py:24
  136.5 11.2 %collective-permute-start.42 = (bf16[2,128,896]{2,1,0:T(8,128)(2,1)S(1)}, bf16[2,128,896]{2,1,0:T(8,128)(2,1)}, u32[]{:S(2)}, u32[]{:S(2)}) collective-permute-start(bf16[2,128,896]{2,1,0:T(8,128)(2,1)S(1)} %pad_maximum_fusion.4.refs_4_), channel_id=1, source_target_pairs={{0,2},{2,0},{1,3},{3,1},{4,6},{6,4},{5,7},{7,5},{8,10},{10,8},{9,1... | collective-permute-start | bytes 1376264 | tf_op jit(solution)/shard_map/ppermute | solution.py:24
  146.8 7.5 %collective-permute-start.48 = (bf16[2,128,896]{2,1,0:T(8,128)(2,1)}, bf16[2,128,896]{2,1,0:T(8,128)(2,1)}, u32[]{:S(2)}, u32[]{:S(2)}) collective-permute-start(bf16[2,128,896]{2,1,0:T(8,128)(2,1)} %collective-permute-done.46.refs_1_), channel_id=1, source_target_pairs={{0,1},{1,0},{2,3},{3,2},{4,5},{5,4},{6,7},{7,6},{8,9},{9,8},{10,11... | collective-permute-start | bytes 1376264 | tf_op jit(solution)/shard_map/ppermute | solution.py:24
  146.8 18.9 %collective-permute-start.36 = (bf16[2,128,896]{2,1,0:T(8,128)(2,1)S(1)}, bf16[2,128,896]{2,1,0:T(8,128)(2,1)}, u32[]{:S(2)}, u32[]{:S(2)}) collective-permute-start(bf16[2,128,896]{2,1,0:T(8,128)(2,1)S(1)} %pad_maximum_fusion.2.refs_0_), channel_id=1, source_target_pairs={{0,1},{1,0},{2,3},{3,2},{4,5},{5,4},{6,7},{7,6},{8,9},{9,8},{10,11... | collective-permute-start | bytes 1376264 | tf_op jit(solution)/shard_map/ppermute | solution.py:24
  147.8 18.0 %collective-permute-start.43 = (bf16[2,128,896]{2,1,0:T(8,128)(2,1)S(1)}, bf16[2,128,896]{2,1,0:T(8,128)(2,1)}, u32[]{:S(2)}, u32[]{:S(2)}) collective-permute-start(bf16[2,128,896]{2,1,0:T(8,128)(2,1)S(1)} %pad_maximum_fusion.4.refs_4_), channel_id=1, source_target_pairs={{0,1},{1,0},{2,3},{3,2},{4,5},{5,4},{6,7},{7,6},{8,9},{9,8},{10,11... | collective-permute-start | bytes 1376264 | tf_op jit(solution)/shard_map/ppermute | solution.py:24
  153.0 12.7 %collective-permute-start.44 = (bf16[2,128,896]{2,1,0:T(8,128)(2,1)}, bf16[2,128,896]{2,1,0:T(8,128)(2,1)}, u32[]{:S(2)}, u32[]{:S(2)}) collective-permute-start(bf16[2,128,896]{2,1,0:T(8,128)(2,1)} %collective-permute-done.42.refs_5_), channel_id=1, source_target_pairs={{0,1},{1,0},{2,3},{3,2},{4,5},{5,4},{6,7},{7,6},{8,9},{9,8},{10,11... | collective-permute-start | bytes 1376264 | tf_op jit(solution)/shard_map/ppermute | solution.py:24
  153.8 12.0 %collective-permute-start.37 = (bf16[2,128,896]{2,1,0:T(8,128)(2,1)}, bf16[2,128,896]{2,1,0:T(8,128)(2,1)}, u32[]{:S(2)}, u32[]{:S(2)}) collective-permute-start(bf16[2,128,896]{2,1,0:T(8,128)(2,1)} %collective-permute-done.31.refs_1_), channel_id=1, source_target_pairs={{0,1},{1,0},{2,3},{3,2},{4,5},{5,4},{6,7},{7,6},{8,9},{9,8},{10,11... | collective-permute-start | bytes 1376264 | tf_op jit(solution)/shard_map/ppermute | solution.py:24
  183.7 6.5 %collective-permute-start.49 = (bf16[2,256,1792]{2,1,0:T(8,128)(2,1)S(1)}, bf16[2,256,1792]{2,1,0:T(8,128)(2,1)S(1)}, u32[]{:S(2)}, u32[]{:S(2)}) collective-permute-start(bf16[2,256,1792]{2,1,0:T(8,128)(2,1)S(1)} %pad_maximum_fusion), channel_id=1, source_target_pairs={{0,1},{1,0},{2,3},{3,2},{4,5},{5,4},{6,7},{7,6},{8,9},{9,8},{10,11... | collective-permute-start | bytes 5505032 | tf_op jit(solution)/shard_map/ppermute | solution.py:24
  185.2 20.0 %collective-permute-start.56 = (bf16[2,256,1792]{2,1,0:T(8,128)(2,1)}, bf16[2,256,1792]{2,1,0:T(8,128)(2,1)}, u32[]{:S(2)}, u32[]{:S(2)}) collective-permute-start(bf16[2,256,1792]{2,1,0:T(8,128)(2,1)} %pad_maximum_fusion.1), channel_id=1, source_target_pairs={{0,1},{1,0},{2,3},{3,2},{4,5},{5,4},{6,7},{7,6},{8,9},{9,8},{10,11... | collective-permute-start | bytes 5505032 | tf_op jit(solution)/shard_map/ppermute | solution.py:24
  192.6 12.5 %collective-permute-start.50 = (bf16[128,1792]{1,0:T(8,128)(2,1)S(1)}, bf16[128,1792]{1,0:T(8,128)(2,1)S(1)}, u32[]{:S(2)}, u32[]{:S(2)}) collective-permute-start(bf16[128,1792]{1,0:T(8,128)(2,1)S(1)} %slice.67), channel_id=1, source_target_pairs={{0,16},{16,0},{1,17},{17,1},{2,18},{18,2},{3,19},{19,3},{4,20},{20... | collective-permute-start | bytes 1376264 | tf_op jit(solution)/shard_map/ppermute | solution.py:24
  193.7 16.3 %collective-permute-start.53 = (bf16[2,128,896]{2,1,0:T(8,128)(2,1)S(1)}, bf16[2,128,896]{2,1,0:T(8,128)(2,1)S(1)}, u32[]{:S(2)}, u32[]{:S(2)}) collective-permute-start(bf16[2,128,896]{2,1,0:T(8,128)(2,1)S(1)} %constant_dynamic-slice_fusion.2), channel_id=1, source_target_pairs={{0,2},{2,0},{1,3},{3,1},{4,6},{6,4},{5,7},{7,5},{8,10},{10,8},{9,1... | collective-permute-start | bytes 1376264 | tf_op jit(solution)/shard_map/ppermute | solution.py:24
  207.7 19.6 %collective-permute-start.60 = (bf16[128,1792]{1,0:T(8,128)(2,1)S(1)}, bf16[128,1792]{1,0:T(8,128)(2,1)S(1)}, u32[]{:S(2)}, u32[]{:S(2)}) collective-permute-start(bf16[128,1792]{1,0:T(8,128)(2,1)S(1)} %slice.73), channel_id=1, source_target_pairs={{0,16},{16,0},{1,17},{17,1},{2,18},{18,2},{3,19},{19,3},{4,20},{20... | collective-permute-start | bytes 1376264 | tf_op jit(solution)/shard_map/ppermute | solution.py:24
  208.8 8.6 %collective-permute-start.51 = (bf16[128,896]{1,0:T(8,128)(2,1)S(1)}, bf16[128,896]{1,0:T(8,128)(2,1)S(1)}, u32[]{:S(2)}, u32[]{:S(2)}) collective-permute-start(bf16[128,896]{1,0:T(8,128)(2,1)S(1)} %constant_dynamic-slice_fusion.3), channel_id=1, source_target_pairs={{0,2},{2,0},{1,3},{3,1},{4,6},{6,4},{5,7},{7,5},{8,10},{10,8},{9,1... | collective-permute-start | bytes 688136 | tf_op jit(solution)/shard_map/ppermute | solution.py:24
  210.2 14.1 %collective-permute-start.54 = (bf16[128,896]{1,0:T(8,128)(2,1)S(1)}, bf16[128,896]{1,0:T(8,128)(2,1)S(1)}, u32[]{:S(2)}, u32[]{:S(2)}) collective-permute-start(bf16[128,896]{1,0:T(8,128)(2,1)S(1)} %slice_bitcast_fusion.4), channel_id=1, source_target_pairs={{0,16},{16,0},{1,17},{17,1},{2,18},{18,2},{3,19},{19,3},{4,20},{20... | collective-permute-start | bytes 688136 | tf_op jit(solution)/shard_map/ppermute | solution.py:24
  210.9 15.5 %collective-permute-start.57 = (bf16[2,128,896]{2,1,0:T(8,128)(2,1)S(1)}, bf16[2,128,896]{2,1,0:T(8,128)(2,1)S(1)}, u32[]{:S(2)}, u32[]{:S(2)}) collective-permute-start(bf16[2,128,896]{2,1,0:T(8,128)(2,1)S(1)} %constant_dynamic-slice_fusion.1), channel_id=1, source_target_pairs={{0,2},{2,0},{1,3},{3,1},{4,6},{6,4},{5,7},{7,5},{8,10},{10,8},{9,1... | collective-permute-start | bytes 1376264 | tf_op jit(solution)/shard_map/ppermute | solution.py:24
  217.5 17.5 %collective-permute-start.52 = (bf16[128,896]{1,0:T(8,128)(2,1)S(1)}, bf16[128,896]{1,0:T(8,128)(2,1)S(1)}, u32[]{:S(2)}, u32[]{:S(2)}) collective-permute-start(bf16[128,896]{1,0:T(8,128)(2,1)S(1)} %add_convert_fusion.6), channel_id=1, source_target_pairs={{0,8},{4,12},{8,0},{12,4},{1,9},{5,13},{9,1},{13,5},{2,10},{6,14},... | collective-permute-start | bytes 688136 | tf_op jit(solution)/shard_map/ppermute | solution.py:29
  224.3 10.6 %collective-permute-start.55 = (bf16[128,896]{1,0:T(8,128)(2,1)S(1)}, bf16[128,896]{1,0:T(8,128)(2,1)S(1)}, u32[]{:S(2)}, u32[]{:S(2)}) collective-permute-start(bf16[128,896]{1,0:T(8,128)(2,1)S(1)} %fusion.25), channel_id=1, source_target_pairs={{0,4},{4,8},{8,12},{12,0},{1,5},{5,9},{9,13},{13,1},{2,6},{6,10},{... | collective-permute-start | bytes 688136 | tf_op jit(solution)/shard_map/ppermute | solution.py:29
  226.6 6.1 %collective-permute-start.58 = (bf16[128,896]{1,0:T(8,128)(2,1)S(1)}, bf16[128,896]{1,0:T(8,128)(2,1)S(1)}, u32[]{:S(2)}, u32[]{:S(2)}) collective-permute-start(bf16[128,896]{1,0:T(8,128)(2,1)S(1)} %slice_bitcast_fusion.2), channel_id=1, source_target_pairs={{0,16},{16,0},{1,17},{17,1},{2,18},{18,2},{3,19},{19,3},{4,20},{20... | collective-permute-start | bytes 688136 | tf_op jit(solution)/shard_map/ppermute | solution.py:24
  227.4 7.5 %collective-permute-start.61 = (bf16[128,896]{1,0:T(8,128)(2,1)S(1)}, bf16[128,896]{1,0:T(8,128)(2,1)S(1)}, u32[]{:S(2)}, u32[]{:S(2)}) collective-permute-start(bf16[128,896]{1,0:T(8,128)(2,1)S(1)} %constant_dynamic-slice_fusion), channel_id=1, source_target_pairs={{0,2},{2,0},{1,3},{3,1},{4,6},{6,4},{5,7},{7,5},{8,10},{10,8},{9,1... | collective-permute-start | bytes 688136 | tf_op jit(solution)/shard_map/ppermute | solution.py:24
  232.7 6.1 %collective-permute-start.59 = (bf16[128,896]{1,0:T(8,128)(2,1)S(1)}, bf16[128,896]{1,0:T(8,128)(2,1)S(1)}, u32[]{:S(2)}, u32[]{:S(2)}) collective-permute-start(bf16[128,896]{1,0:T(8,128)(2,1)S(1)} %fusion.24), channel_id=1, source_target_pairs={{0,12},{4,0},{8,4},{12,8},{1,13},{5,1},{9,5},{13,9},{2,14},{6,2},{... | collective-permute-start | bytes 688136 | tf_op jit(solution)/shard_map/ppermute | solution.py:29
  239.1 1.4 collective-permute-start.62
  (35 other events, 162.9 us)

commit v3 on v2

--- a/solution.py
+++ b/solution.py
@@ -27,6 +27,10 @@
 def shift(value, amount):
     size = lax.axis_size("line")
     return lax.ppermute(value, "line", [(i, (i + amount) % size) for i in range(size)])
+
+
+def part_of(value, start, size, axis):
+    return lax.dynamic_slice_in_dim(value, start, size, axis, allow_negative_indices=False)
 
 
 def relative(value, axis, index):
@@ -373,12 +377,22 @@
     group_places = [
         jnp.stack([(at - k) % line for k in group] + [side]).astype(jnp.int32) for group in groups
     ]
+    index = dict(
+        own_sect=sect,
+        other_sect=1 - sect,
+        own_side=side * chip_width,
+        other_side=(1 - side) * chip_width,
+        upper=at >= half,
+        near_core=core == 0,
+        share=lax.axis_index("tp"),
+        columns=[(at + k) % line * 2 * chip_width for k in shifts],
+    )
     length, partial, blocks = heads.shape[1] // 2, None, []
     for part in range(2):
         own = heads[:, part * length : (part + 1) * length]
         if part:
-            own, weight, residual_rows, place, group_places = lax.optimization_barrier(
-                (own, weight, residual_rows, place, group_places)
+            own, weight, residual_rows, place, group_places, index = lax.optimization_barrier(
+                (own, weight, residual_rows, place, group_places, index)
             )
         rights, lefts = [own], [own]
         for k in shifts[1:]:
@@ -410,15 +424,15 @@
     if tp > 1:
         partial = lax.psum(partial, "tp").astype(BF16)
     partial = partial.reshape(2, -1, chip_width)
-    kept = lax.dynamic_index_in_dim(partial, sect, 0, keepdims=False)
-    given = lax.dynamic_index_in_dim(partial, 1 - sect, 0, keepdims=False)
+    kept = part_of(partial, index["own_sect"], 1, 0)[0]
+    given = part_of(partial, index["other_sect"], 1, 0)[0]
     attention = kept.astype(F32) + swap(given, "sect").astype(F32)
     own_rows = (residual_rows.astype(F32) + attention).astype(BF16)
 
     got = {k: shift(own_rows, k) if k else own_rows for k in shifts if k != line // 2}
     right = lax.ppermute(got[1], "line", [(i, i + 1) for i in range(1, line - 1)])
     left = lax.ppermute(got[line - 1], "line", [(i, i - 1) for i in range(1, line - 1)])
-    got[line // 2] = jnp.where(at >= line // 2, right, left)
+    got[line // 2] = jnp.where(index["upper"], right, left)
     pairs, opposites = {}, {}
     for k in (0, back, 1, half):
         first, second = ("sect", "side") if k % 2 == 0 else ("side", "sect")
@@ -451,10 +465,10 @@
     hidden = sums
 
     def own_side(value):
-        return lax.dynamic_slice_in_dim(value, side * chip_width, chip_width, value.ndim - 1)
+        return part_of(value, index["own_side"], chip_width, value.ndim - 1)
 
     def other_side(value):
-        return lax.dynamic_slice_in_dim(value, (1 - side) * chip_width, chip_width, value.ndim - 1)
+        return part_of(value, index["other_side"], chip_width, value.ndim - 1)
 
     count = row_total // 2
     send, keep = (
@@ -465,7 +479,7 @@
     send, keep = send.astype(BF16), keep.astype(BF16)
 
     def columns_to(value, k):
-        return lax.dynamic_slice_in_dim(value, (at + k) % line * 2 * chip_width, 2 * chip_width, 1)
+        return part_of(value, index["columns"][k], 2 * chip_width, 1)
 
     total, held = own_rows.astype(F32), None
     for group in ((half, 1), (back, 0)):
@@ -484,12 +498,12 @@
             total = total + (shift(part, k) if k else part).astype(F32)
     total = total.astype(BF16)
 
-    mine = jnp.where(core == 0, total[:, :width], total[:, width:])
-    other = swap(jnp.where(core == 0, total[:, width:], total[:, :width]), "core")
-    out = relative(jnp.stack([mine, other]), 0, core).reshape(2, -1, block, width)
-    out = out.transpose(1, 0, 2, 3).reshape(-1, width)
+    mine = jnp.where(index["near_core"], total[:, :width], total[:, width:])
+    other = swap(jnp.where(index["near_core"], total[:, width:], total[:, :width]), "core")
+    out = jnp.where(index["near_core"], jnp.stack([mine, other]), jnp.stack([other, mine]))
+    out = out.reshape(2, -1, block, width).transpose(1, 0, 2, 3).reshape(-1, width)
     share = out.shape[0] // tp
-    return lax.dynamic_slice_in_dim(out, lax.axis_index("tp") * share, share, 0)
+    return part_of(out, index["share"] * share, share, 0) if tp > 1 else out
 
 
 def solution(mesh):

time: 242 us -> 235 us (0.971)
  local copies, waits for them, and re-layouts: 24.1 us -> 5.28 us
  waiting for transfers between devices: 74 us -> 84.2 us
  matrix products: 10.8 us -> 21 us
  starting transfers between devices: 77.1 us -> 71.8 us
    unnamed x73 -> x11, local copies, waits for them, and re-layouts: 21.3 us -> 0.88 us
    dot_general x2, matrix products: 8.79 us -> 19 us  [on_device(): jnp.dot(rows, w_down[0], preferred_element_type=F32)]
    ppermute x5, starting transfers between devices: 9.38 us -> 3.41 us  [shift(): lax.ppermute(value, 'line', [(i, (i + amount) % size) for i in range(size)])]
    ppermute x14, waiting for transfers between devices: 2.43 us -> 7.41 us  [on_device(): lax.ppermute(value, ('line', 'side'), [(2 * i + y, 2 * i + 1 - y) for i i...]
    ppermute x6, waiting for transfers between devices: 8.6 us -> 12.4 us  [on_device(): lefts.append(lax.ppermute(lefts[-1], 'line', left))]
  transfers between devices with their start and end apart: 63 -> 63, of which waited for: 22 -> 26; matrix products, arithmetic and copies ran while one was open for 6% -> 7% of each run, Pallas kernels for 12% -> 12%
where the time goes in v3:
time: 235 us; the launch traced here: 234 us
  waiting for transfers between devices  84.2 us (36%)
  starting transfers between devices  71.8 us (31%)
  Pallas kernels  46 us (20%)
  matrix products  21 us (9%)
  local copies, waits for them, and re-layouts  5.28 us (2%)
  other arithmetic  4.93 us (2%)
    ppermute x30, waiting for transfers between devices, swap(): return lax.ppermute(value, axis, [(0, 1), (1, 0)])  48.6 us
    pallas_call x3, Pallas kernels, hidden_part(): pl.pallas_call(functools.partial(hidden_kernel, layout, first, last), in_...  28.2 us
    ppermute x30, starting transfers between devices, swap(): return lax.ppermute(value, axis, [(0, 1), (1, 0)])  23.5 us
    ppermute x14, starting transfers between devices, on_device(): lax.ppermute(value, ('line', 'side'), [(2 * i + y, 2 * i + 1 - y) for i i...  23.3 us
    dot_general x2, matrix products, on_device(): jnp.dot(rows, w_down[0], preferred_element_type=F32)  19 us
    ppermute x6, waiting for transfers between devices, on_device(): lefts.append(lax.ppermute(lefts[-1], 'line', left))  12.4 us
    ppermute x6, starting transfers between devices, on_device(): rights.append(lax.ppermute(rights[-1], 'line', right))  11.8 us
    pallas_call x2, Pallas kernels, project(): pl.pallas_call(functools.partial(project_kernel, slots, start, first), in...  11.2 us
  transfers between devices with their start and end apart: 63, of which 26 were waited for; matrix products, arithmetic and copies ran while one was open for 7% of the time, Pallas kernels for 12%

profile of v3, /device:TPU:0, one launch (start us, length us, event | category | flops | bytes accessed | tf_op | source)
XLA Modules:
  0.0 234.3 jit_solution(15210598908897397807)
XLA Ops:
  1.1 6.7 %shard_map.109 = bf16[32,64,512]{2,1,0:T(8,128)(2,1)S(1)} custom-call(s32[32]{0:T(128)S(1)} %copy-done, bf16[32,64,576]{2,1,0:T(8,128)(2,1)} %query_ref.1, bf16[32,576,128]{2,1,0:T(8,128)(2,1)} %bitcast.121), custom_call_target="tpu_custom_call" | custom-call | flops 570425344 | bytes 9175040 | tf_op jit(solution)/shard_map/pallas_call | solution.py:71
  7.9 2.0 fusion.19
  10.0 4.5 %collective-permute-start.1 = (bf16[32,4096]{1,0:T(8,128)(2,1)S(1)}, bf16[32,4096]{1,0:T(8,128)(2,1)S(1)}, u32[]{:S(2)}, u32[]{:S(2)}) collective-permute-start(bf16[32,4096]{1,0:T(8,128)(2,1)S(1)} %get-tuple-element.67.refs_0_), channel_id=1, source_target_pairs={{0,4},{4,8},{8,12},{1,5},{5,9},{9,13},{2,6},{6,10},{10,14},{3,7},{... | collective-permute-start | bytes 786440 | tf_op jit(solution)/shard_map/ppermute | solution.py:403
  14.5 1.3 collective-permute-start.4
  15.8 1.6 collective-permute-start.8
  19.4 4.6 %collective-permute-start.15 = (bf16[32,4096]{1,0:T(8,128)(2,1)S(1)}, bf16[32,4096]{1,0:T(8,128)(2,1)S(1)}, u32[]{:S(2)}, u32[]{:S(2)}) collective-permute-start(bf16[32,4096]{1,0:T(8,128)(2,1)S(1)} %get-tuple-element.37.refs_1_), channel_id=1, source_target_pairs={{0,4},{4,8},{8,12},{1,5},{5,9},{9,13},{2,6},{6,10},{10,14},{3,7},{... | collective-permute-start | bytes 786440 | tf_op jit(solution)/shard_map/ppermute | solution.py:403
  24.0 1.3 collective-permute-start.16
  26.0 1.2 collective-permute-start.21
  27.1 2.7 %collective-permute-done.15.refs_2_ = bf16[32,4096]{1,0:T(8,128)(2,1)S(1)} collective-permute-done((bf16[32,4096]{1,0:T(8,128)(2,1)S(1)}, bf16[32,4096]{1,0:T(8,128)(2,1)S(1)}, u32[]{:S(2)}, u32[]{:S(2)}) %collective-permute-start.15) | collective-permute-done | bytes 262176 | tf_op jit(solution)/shard_map/ppermute | solution.py:403
  29.8 1.3 collective-permute-start.5
  31.1 2.9 %collective-permute-done.16.refs_3_ = bf16[32,4096]{1,0:T(8,128)(2,1)S(1)} collective-permute-done((bf16[32,4096]{1,0:T(8,128)(2,1)S(1)}, bf16[32,4096]{1,0:T(8,128)(2,1)S(1)}, u32[]{:S(2)}, u32[]{:S(2)}) %collective-permute-start.16) | collective-permute-done | bytes 262176 | tf_op jit(solution)/shard_map/ppermute | solution.py:404
  33.9 2.4 %collective-permute-start.10 = (bf16[32,4096]{1,0:T(8,128)(2,1)S(1)}, bf16[32,4096]{1,0:T(8,128)(2,1)S(1)}, u32[]{:S(2)}, u32[]{:S(2)}) collective-permute-start(bf16[32,4096]{1,0:T(8,128)(2,1)S(1)} %collective-permute-done.4.refs_2_), channel_id=1, source_target_pairs={{0,2},{2,0},{4,6},{6,4},{8,10},{10,8},{1,3},{3,1},{5,7},{7,5},{9,1... | collective-permute-start | bytes 786440 | tf_op jit(solution)/shard_map/ppermute | solution.py:407
  37.8 1.3 collective-permute-start.18
  40.6 2.4 %collective-permute-done.10.refs_9_ = bf16[32,4096]{1,0:T(8,128)(2,1)S(1)} collective-permute-done((bf16[32,4096]{1,0:T(8,128)(2,1)S(1)}, bf16[32,4096]{1,0:T(8,128)(2,1)S(1)}, u32[]{:S(2)}, u32[]{:S(2)}) %collective-permute-start.10) | collective-permute-done | bytes 262176 | tf_op jit(solution)/shard_map/ppermute | solution.py:407
  43.0 1.3 collective-permute-start.7
  44.3 2.4 %collective-permute-start.12 = (bf16[32,4096]{1,0:T(8,128)(2,1)S(1)}, bf16[32,4096]{1,0:T(8,128)(2,1)S(1)}, u32[]{:S(2)}, u32[]{:S(2)}) collective-permute-start(bf16[32,4096]{1,0:T(8,128)(2,1)S(1)} %collective-permute-done.5.refs_4_), channel_id=1, source_target_pairs={{0,2},{2,0},{4,6},{6,4},{1,3},{3,1},{5,7},{7,5},{16,18},{18,16},{2... | collective-permute-start | bytes 786440 | tf_op jit(solution)/shard_map/ppermute | solution.py:407
  47.5 5.9 %collective-permute-done.18.refs_5_ = bf16[32,4096]{1,0:T(8,128)(2,1)S(1)} collective-permute-done((bf16[32,4096]{1,0:T(8,128)(2,1)S(1)}, bf16[32,4096]{1,0:T(8,128)(2,1)S(1)}, u32[]{:S(2)}, u32[]{:S(2)}) %collective-permute-start.18) | collective-permute-done | bytes 262176 | tf_op jit(solution)/shard_map/ppermute | solution.py:404
  54.0 1.3 collective-permute-start.20
  55.3 2.7 %collective-permute-done.7.refs_6_ = bf16[32,4096]{1,0:T(8,128)(2,1)S(1)} collective-permute-done((bf16[32,4096]{1,0:T(8,128)(2,1)S(1)}, bf16[32,4096]{1,0:T(8,128)(2,1)S(1)}, u32[]{:S(2)}, u32[]{:S(2)}) %collective-permute-start.7) | collective-permute-done | bytes 262176 | tf_op jit(solution)/shard_map/ppermute | solution.py:404
  58.1 2.8 %collective-permute-start.14 = (bf16[32,4096]{1,0:T(8,128)(2,1)S(1)}, bf16[32,4096]{1,0:T(8,128)(2,1)S(1)}, u32[]{:S(2)}, u32[]{:S(2)}) collective-permute-start(bf16[32,4096]{1,0:T(8,128)(2,1)S(1)} %collective-permute-done.7.refs_6_), channel_id=1, source_target_pairs={{0,2},{2,0},{1,3},{3,1},{16,18},{18,16},{17,19},{19,17}} | collective-permute-start | bytes 786440 | tf_op jit(solution)/shard_map/ppermute | solution.py:407
  62.3 3.0 %collective-permute-start.23 = (bf16[32,4096]{1,0:T(8,128)(2,1)S(1)}, bf16[32,4096]{1,0:T(8,128)(2,1)S(1)}, u32[]{:S(2)}, u32[]{:S(2)}) collective-permute-start(bf16[32,4096]{1,0:T(8,128)(2,1)S(1)} %collective-permute-done.16.refs_3_), channel_id=1, source_target_pairs={{0,2},{2,0},{4,6},{6,4},{8,10},{10,8},{1,3},{3,1},{5,7},{7,5},{9,1... | collective-permute-start | bytes 786440 | tf_op jit(solution)/shard_map/ppermute | solution.py:407
  66.0 2.9 %collective-permute-done.14.refs_13_ = bf16[32,4096]{1,0:T(8,128)(2,1)S(1)} collective-permute-done((bf16[32,4096]{1,0:T(8,128)(2,1)S(1)}, bf16[32,4096]{1,0:T(8,128)(2,1)S(1)}, u32[]{:S(2)}, u32[]{:S(2)}) %collective-permute-start.14) | collective-permute-done | bytes 262176 | tf_op jit(solution)/shard_map/ppermute | solution.py:407
  68.9 2.8 %collective-permute-start.25 = (bf16[32,4096]{1,0:T(8,128)(2,1)S(1)}, bf16[32,4096]{1,0:T(8,128)(2,1)S(1)}, u32[]{:S(2)}, u32[]{:S(2)}) collective-permute-start(bf16[32,4096]{1,0:T(8,128)(2,1)S(1)} %collective-permute-done.18.refs_5_), channel_id=1, source_target_pairs={{0,2},{2,0},{4,6},{6,4},{1,3},{3,1},{5,7},{7,5},{16,18},{18,16},{2... | collective-permute-start | bytes 786440 | tf_op jit(solution)/shard_map/ppermute | solution.py:407
  72.4 3.0 %collective-permute-start.27 = (bf16[32,4096]{1,0:T(8,128)(2,1)S(1)}, bf16[32,4096]{1,0:T(8,128)(2,1)S(1)}, u32[]{:S(2)}, u32[]{:S(2)}) collective-permute-start(bf16[32,4096]{1,0:T(8,128)(2,1)S(1)} %collective-permute-done.20.refs_7_), channel_id=1, source_target_pairs={{0,2},{2,0},{1,3},{3,1},{16,18},{18,16},{17,19},{19,17}} | collective-permute-start | bytes 786440 | tf_op jit(solution)/shard_map/ppermute | solution.py:407
  75.4 5.6 %shard_map.110.refs_0_ = f32[256,896]{1,0:T(8,128)S(1)} custom-call(s32[17]{0:T(128)S(1)} %stack.169.place_ref, bf16[448,8192]{1,0:T(8,128)(2,1)} %bitcast.119, bf16[448,8192]{1,0:T(8,128)(2,1)} %collective-permute-done.3.sibling_ref, bf16[32,4096]{1,0:T(8,128)(2,1)S(1)} %get-tuple-element.67.refs_0_, bf16[32,4096]{1,0:T(8,128)(2,1)S(1)} %collective-permute-done.1.refs_1_, ...), custom_call_target="tpu_custom_call" | custom-call | flops 1879048192 | bytes 9437184 | tf_op jit(solution)/shard_map/pallas_call | solution.py:161
  81.0 2.1 collective-permute-done.27.refs_14_
  83.2 5.6 %shard_map.111 = bf16[256,896]{1,0:T(8,128)(2,1)S(1)} custom-call(s32[17]{0:T(128)S(1)} %stack.169.place_ref, bf16[448,8192]{1,0:T(8,128)(2,1)} %bitcast.120, bf16[448,8192]{1,0:T(8,128)(2,1)} %collective-permute-done.3.sibling_ref, f32[256,896]{1,0:T(8,128)S(1)} %shard_map.110.refs_0_, bf16[32,4096]{1,0:T(8,128)(2,1)S(1)} %get-tuple-element.37.refs_1_, ...), custom_call_target="tpu_custom_call" | custom-call | flops 1879048192 | bytes 9437184 | tf_op jit(solution)/shard_map/pallas_call | solution.py:161
  88.8 1.6 collective-permute-start.28
  90.3 5.3 %collective-permute-done.28 = bf16[128,896]{1,0:T(8,128)(2,1)S(1)} collective-permute-done((bf16[128,896]{1,0:T(8,128)(2,1)S(1)}, bf16[128,896]{1,0:T(8,128)(2,1)S(1)}, u32[]{:S(2)}, u32[]{:S(2)}) %collective-permute-start.28) | collective-permute-done | bytes 229408 | tf_op jit(solution)/shard_map/ppermute | solution.py:24
  95.7 1.5 collective-permute-start.32
  97.3 4.5 %collective-permute-done.32 = bf16[128,896]{1,0:T(8,128)(2,1)S(1)} collective-permute-done((bf16[128,896]{1,0:T(8,128)(2,1)S(1)}, bf16[128,896]{1,0:T(8,128)(2,1)S(1)}, u32[]{:S(2)}, u32[]{:S(2)}) %collective-permute-start.32) | collective-permute-done | bytes 229408 | tf_op jit(solution)/shard_map/ppermute | solution.py:24
  102.8 2.4 %collective-permute-done.29 = bf16[128,896]{1,0:T(8,128)(2,1)S(1)} collective-permute-done((bf16[128,896]{1,0:T(8,128)(2,1)S(1)}, bf16[128,896]{1,0:T(8,128)(2,1)S(1)}, u32[]{:S(2)}, u32[]{:S(2)}) %collective-permute-start.29) | collective-permute-done | bytes 229408 | tf_op jit(solution)/shard_map/ppermute | solution.py:29
  105.9 3.0 %collective-permute-done.39 = bf16[128,896]{1,0:T(8,128)(2,1)S(1)} collective-permute-done((bf16[128,896]{1,0:T(8,128)(2,1)S(1)}, bf16[128,896]{1,0:T(8,128)(2,1)S(1)}, u32[]{:S(2)}, u32[]{:S(2)}) %collective-permute-start.39) | collective-permute-done | bytes 229408 | tf_op jit(solution)/shard_map/ppermute | solution.py:29
  108.9 1.5 collective-permute-start.40
  110.4 1.2 collective-permute-start.45
  112.5 4.3 %collective-permute-done.40 = bf16[128,896]{1,0:T(8,128)(2,1)S(1)} collective-permute-done((bf16[128,896]{1,0:T(8,128)(2,1)S(1)}, bf16[128,896]{1,0:T(8,128)(2,1)S(1)}, u32[]{:S(2)}, u32[]{:S(2)}) %collective-permute-start.40) | collective-permute-done | bytes 229408 | tf_op jit(solution)/shard_map/ppermute | solution.py:434
  116.8 1.6 collective-permute-start.41
  118.9 1.6 collective-permute-start.46
  120.5 2.8 %collective-permute-done.30 = bf16[128,896]{1,0:T(8,128)(2,1)S(1)} collective-permute-done((bf16[128,896]{1,0:T(8,128)(2,1)S(1)}, bf16[128,896]{1,0:T(8,128)(2,1)S(1)}, u32[]{:S(2)}, u32[]{:S(2)}) %collective-permute-start.30) | collective-permute-done | bytes 229408 | tf_op jit(solution)/shard_map/ppermute | solution.py:24
  123.4 1.6 collective-permute-done.41
  125.1 1.5 collective-permute-start.31
  126.6 1.2 collective-permute-start.42
  127.8 7.7 %shard_map.112 = (f32[512,1024]{1,0:T(8,128)S(1)}, f32[512,1024]{1,0:T(8,128)S(1)}) custom-call(s32[2]{0:T(128)S(1)} %get-tuple-element.41.place_ref, bf16[2,128,896]{2,1,0:T(8,128)(2,1)S(1)} %pad_maximum_fusion.3.refs_0_, bf16[2,128,896]{2,1,0:T(8,128)(2,1)S(1)} %collective-permute-done.33.refs_1_, ...), custom_call_target="tpu_custom_call" | custom-call | flops 3758096384 | bytes 7340032 | tf_op jit(solution)/shard_map/pallas_call | solution.py:302
  136.1 1.7 collective-permute-done.42.refs_5_
  137.8 4.8 %collective-permute-done.31.refs_1_ = bf16[2,128,896]{2,1,0:T(8,128)(2,1)S(1)} collective-permute-done((bf16[2,128,896]{2,1,0:T(8,128)(2,1)S(1)}, bf16[2,128,896]{2,1,0:T(8,128)(2,1)S(1)}, u32[]{:S(2)}, u32[]{:S(2)}) %collective-permute-start.31) | collective-permute-done | bytes 458784 | tf_op jit(solution)/shard_map/ppermute | solution.py:24
  143.1 8.2 %shard_map.113 = (f32[512,1024]{1,0:T(8,128)S(1)}, f32[512,1024]{1,0:T(8,128)S(1)}) custom-call(s32[2]{0:T(128)S(1)} %get-tuple-element.47.place_ref, bf16[2,128,896]{2,1,0:T(8,128)(2,1)S(1)} %pad_maximum_fusion.5.refs_0_, bf16[2,128,896]{2,1,0:T(8,128)(2,1)S(1)} %collective-permute-done.46.refs_1_, ...), custom_call_target="tpu_custom_call" | custom-call | flops 3758096384 | bytes 7340032 | tf_op jit(solution)/shard_map/pallas_call | solution.py:302
  151.4 12.2 %shard_map.114 = bf16[512,1024]{1,0:T(8,128)(2,1)S(1)} custom-call(s32[3]{0:T(128)S(1)} %pad_add_fusion.2.place_ref, bf16[2,128,896]{2,1,0:T(8,128)(2,1)S(1)} %pad_maximum_fusion.2.refs_0_, bf16[2,128,896]{2,1,0:T(8,128)(2,1)S(1)} %collective-permute-done.31.refs_1_, bf16[2,128,896]{2,1,0:T(8,128)(2,1)S(1)} %collective-permute-done.36.refs_2_, ...), custom_call_target="tpu_custom_call" | custom-call | flops 7516192768 | bytes 14680064 | tf_op jit(solution)/shard_map/pallas_call | solution.py:302
  163.6 9.6 %fusion.7 = bf16[256,7168]{1,0:T(8,128)(2,1)S(1)} fusion(bf16[1,1024,7168]{2,1,0:T(8,128)(2,1)} %param.19, bf16[512,1024]{1,0:T(8,128)(2,1)S(1)} %shard_map.114), kind=kOutput, calls=%fused_computation.5 | convolution fusion | flops 3759931392 | bytes 18874368 | tf_op jit(solution)/shard_map/dot_general | solution.py:475
  173.2 2.2 dynamic-slice_bitcast_fusion.3
  176.4 9.4 %fusion.4 = bf16[256,7168]{1,0:T(8,128)(2,1)S(1)} fusion(bf16[1,1024,7168]{2,1,0:T(8,128)(2,1)} %param.19, bf16[512,1024]{1,0:T(8,128)(2,1)S(1)} %shard_map.114), kind=kOutput, calls=%fused_computation.4 | convolution fusion | flops 3759931392 | bytes 18874368 | tf_op jit(solution)/shard_map/dot_general | solution.py:475
  185.8 1.3 fusion.14
  187.1 1.6 collective-permute-start.50
  188.9 1.2 collective-permute-start.53
  190.1 9.6 %collective-permute-done.50 = bf16[128,1792]{1,0:T(8,128)(2,1)S(1)} collective-permute-done((bf16[128,1792]{1,0:T(8,128)(2,1)S(1)}, bf16[128,1792]{1,0:T(8,128)(2,1)S(1)}, u32[]{:S(2)}, u32[]{:S(2)}) %collective-permute-start.50) | collective-permute-done | bytes 458784 | tf_op jit(solution)/shard_map/ppermute | solution.py:24
  199.8 1.3 fusion.12
  201.1 1.6 collective-permute-start.60
  202.8 1.2 collective-permute-start.51
  206.1 5.4 %collective-permute-done.51 = bf16[128,896]{1,0:T(8,128)(2,1)S(1)} collective-permute-done((bf16[128,896]{1,0:T(8,128)(2,1)S(1)}, bf16[128,896]{1,0:T(8,128)(2,1)S(1)}, u32[]{:S(2)}, u32[]{:S(2)}) %collective-permute-start.51) | collective-permute-done | bytes 229408 | tf_op jit(solution)/shard_map/ppermute | solution.py:24
  211.7 6.0 %collective-permute-done.54 = bf16[128,896]{1,0:T(8,128)(2,1)S(1)} collective-permute-done((bf16[128,896]{1,0:T(8,128)(2,1)S(1)}, bf16[128,896]{1,0:T(8,128)(2,1)S(1)}, u32[]{:S(2)}, u32[]{:S(2)}) %collective-permute-start.54) | collective-permute-done | bytes 229408 | tf_op jit(solution)/shard_map/ppermute | solution.py:24
  220.7 1.2 collective-permute-start.61
  221.8 3.7 %collective-permute-done.58 = bf16[128,896]{1,0:T(8,128)(2,1)S(1)} collective-permute-done((bf16[128,896]{1,0:T(8,128)(2,1)S(1)}, bf16[128,896]{1,0:T(8,128)(2,1)S(1)}, u32[]{:S(2)}, u32[]{:S(2)}) %collective-permute-start.58) | collective-permute-done | bytes 229408 | tf_op jit(solution)/shard_map/ppermute | solution.py:24
  225.6 2.6 %collective-permute-start.59 = (bf16[128,896]{1,0:T(8,128)(2,1)S(1)}, bf16[128,896]{1,0:T(8,128)(2,1)S(1)}, u32[]{:S(2)}, u32[]{:S(2)}) collective-permute-start(bf16[128,896]{1,0:T(8,128)(2,1)S(1)} %fusion.24), channel_id=1, source_target_pairs={{0,12},{4,0},{8,4},{12,8},{1,13},{5,1},{9,5},{13,9},{2,14},{6,2},{... | collective-permute-start | bytes 688136 | tf_op jit(solution)/shard_map/ppermute | solution.py:29
  228.1 3.5 %collective-permute-done.59 = bf16[128,896]{1,0:T(8,128)(2,1)S(1)} collective-permute-done((bf16[128,896]{1,0:T(8,128)(2,1)S(1)}, bf16[128,896]{1,0:T(8,128)(2,1)S(1)}, u32[]{:S(2)}, u32[]{:S(2)}) %collective-permute-start.59) | collective-permute-done | bytes 229408 | tf_op jit(solution)/shard_map/ppermute | solution.py:29
  232.1 1.3 collective-permute-done.62
  (128 shorter events, 23.3 us)
Async XLA Ops:
  0.0 37.1 %collective-permute-start.3 = (bf16[448,8192]{1,0:T(8,128)(2,1)}, bf16[448,8192]{1,0:T(8,128)(2,1)}, u32[]{:S(2)}, u32[]{:S(2)}) collective-permute-start(bf16[448,8192]{1,0:T(8,128)(2,1)} %bitcast.118), channel_id=1, source_target_pairs={{0,1},{1,0},{2,3},{3,2},{4,5},{5,4},{6,7},{7,6},{8,9},{9,8},{10,11... | collective-permute-start | bytes 22020104 | tf_op jit(solution)/shard_map/ppermute | solution.py:24
  9.9 7.9 %copy-start.3 = (f32[512,8]{0,1:T(8,128)S(1)}, f32[512,8]{0,1:T(8,128)}, u32[]{:S(2)}) copy-start(f32[512,8]{0,1:T(8,128)} %param.21) | copy-start | bytes 49156
  10.0 13.9 %collective-permute-start.1 = (bf16[32,4096]{1,0:T(8,128)(2,1)S(1)}, bf16[32,4096]{1,0:T(8,128)(2,1)S(1)}, u32[]{:S(2)}, u32[]{:S(2)}) collective-permute-start(bf16[32,4096]{1,0:T(8,128)(2,1)S(1)} %get-tuple-element.67.refs_0_), channel_id=1, source_target_pairs={{0,4},{4,8},{8,12},{1,5},{5,9},{9,13},{2,6},{6,10},{10,14},{3,7},{... | collective-permute-start | bytes 786440 | tf_op jit(solution)/shard_map/ppermute | solution.py:403
  14.5 10.7 %collective-permute-start.4 = (bf16[32,4096]{1,0:T(8,128)(2,1)S(1)}, bf16[32,4096]{1,0:T(8,128)(2,1)S(1)}, u32[]{:S(2)}, u32[]{:S(2)}) collective-permute-start(bf16[32,4096]{1,0:T(8,128)(2,1)S(1)} %get-tuple-element.67.refs_0_), channel_id=1, source_target_pairs={{4,0},{8,4},{12,8},{5,1},{9,5},{13,9},{6,2},{10,6},{14,10},{7,3},{... | collective-permute-start | bytes 786440 | tf_op jit(solution)/shard_map/ppermute | solution.py:404
  15.8 10.1 %collective-permute-start.8 = (bf16[32,4096]{1,0:T(8,128)(2,1)S(1)}, bf16[32,4096]{1,0:T(8,128)(2,1)S(1)}, u32[]{:S(2)}, u32[]{:S(2)}) collective-permute-start(bf16[32,4096]{1,0:T(8,128)(2,1)S(1)} %get-tuple-element.67.refs_0_), channel_id=1, source_target_pairs={{0,2},{2,0},{4,6},{6,4},{8,10},{10,8},{12,14},{14,12},{1,3},{3,1},... | collective-permute-start | bytes 786440 | tf_op jit(solution)/shard_map/ppermute | solution.py:407
  17.7 1.4 collective-permute-start
  19.4 10.4 %collective-permute-start.15 = (bf16[32,4096]{1,0:T(8,128)(2,1)S(1)}, bf16[32,4096]{1,0:T(8,128)(2,1)S(1)}, u32[]{:S(2)}, u32[]{:S(2)}) collective-permute-start(bf16[32,4096]{1,0:T(8,128)(2,1)S(1)} %get-tuple-element.37.refs_1_), channel_id=1, source_target_pairs={{0,4},{4,8},{8,12},{1,5},{5,9},{9,13},{2,6},{6,10},{10,14},{3,7},{... | collective-permute-start | bytes 786440 | tf_op jit(solution)/shard_map/ppermute | solution.py:403
  24.0 10.0 %collective-permute-start.16 = (bf16[32,4096]{1,0:T(8,128)(2,1)S(1)}, bf16[32,4096]{1,0:T(8,128)(2,1)S(1)}, u32[]{:S(2)}, u32[]{:S(2)}) collective-permute-start(bf16[32,4096]{1,0:T(8,128)(2,1)S(1)} %get-tuple-element.37.refs_1_), channel_id=1, source_target_pairs={{4,0},{8,4},{12,8},{5,1},{9,5},{13,9},{6,2},{10,6},{14,10},{7,3},{... | collective-permute-start | bytes 786440 | tf_op jit(solution)/shard_map/ppermute | solution.py:404
  25.3 11.1 %collective-permute-start.2 = (bf16[32,4096]{1,0:T(8,128)(2,1)S(1)}, bf16[32,4096]{1,0:T(8,128)(2,1)S(1)}, u32[]{:S(2)}, u32[]{:S(2)}) collective-permute-start(bf16[32,4096]{1,0:T(8,128)(2,1)S(1)} %collective-permute-done.1.refs_1_), channel_id=1, source_target_pairs={{4,8},{8,12},{5,9},{9,13},{6,10},{10,14},{7,11},{11,15},{20,24},{2... | collective-permute-start | bytes 786440 | tf_op jit(solution)/shard_map/ppermute | solution.py:403
  26.0 11.8 %collective-permute-start.21 = (bf16[32,4096]{1,0:T(8,128)(2,1)S(1)}, bf16[32,4096]{1,0:T(8,128)(2,1)S(1)}, u32[]{:S(2)}, u32[]{:S(2)}) collective-permute-start(bf16[32,4096]{1,0:T(8,128)(2,1)S(1)} %get-tuple-element.37.refs_1_), channel_id=1, source_target_pairs={{0,2},{2,0},{4,6},{6,4},{8,10},{10,8},{12,14},{14,12},{1,3},{3,1},... | collective-permute-start | bytes 786440 | tf_op jit(solution)/shard_map/ppermute | solution.py:407
  29.8 10.2 %collective-permute-start.5 = (bf16[32,4096]{1,0:T(8,128)(2,1)S(1)}, bf16[32,4096]{1,0:T(8,128)(2,1)S(1)}, u32[]{:S(2)}, u32[]{:S(2)}) collective-permute-start(bf16[32,4096]{1,0:T(8,128)(2,1)S(1)} %collective-permute-done.4.refs_2_), channel_id=1, source_target_pairs={{4,0},{8,4},{5,1},{9,5},{6,2},{10,6},{7,3},{11,7},{20,16},{24,20},... | collective-permute-start | bytes 786440 | tf_op jit(solution)/shard_map/ppermute | solution.py:404
  33.9 9.1 %collective-permute-start.10 = (bf16[32,4096]{1,0:T(8,128)(2,1)S(1)}, bf16[32,4096]{1,0:T(8,128)(2,1)S(1)}, u32[]{:S(2)}, u32[]{:S(2)}) collective-permute-start(bf16[32,4096]{1,0:T(8,128)(2,1)S(1)} %collective-permute-done.4.refs_2_), channel_id=1, source_target_pairs={{0,2},{2,0},{4,6},{6,4},{8,10},{10,8},{1,3},{3,1},{5,7},{7,5},{9,1... | collective-permute-start | bytes 786440 | tf_op jit(solution)/shard_map/ppermute | solution.py:407
  36.4 8.0 %collective-permute-start.9 = (bf16[32,4096]{1,0:T(8,128)(2,1)S(1)}, bf16[32,4096]{1,0:T(8,128)(2,1)S(1)}, u32[]{:S(2)}, u32[]{:S(2)}) collective-permute-start(bf16[32,4096]{1,0:T(8,128)(2,1)S(1)} %collective-permute-done.1.refs_1_), channel_id=1, source_target_pairs={{4,6},{6,4},{8,10},{10,8},{12,14},{14,12},{5,7},{7,5},{9,11},{11,9... | collective-permute-start | bytes 786440 | tf_op jit(solution)/shard_map/ppermute | solution.py:407
  37.1 9.7 %collective-permute-start.17 = (bf16[32,4096]{1,0:T(8,128)(2,1)S(1)}, bf16[32,4096]{1,0:T(8,128)(2,1)S(1)}, u32[]{:S(2)}, u32[]{:S(2)}) collective-permute-start(bf16[32,4096]{1,0:T(8,128)(2,1)S(1)} %collective-permute-done.15.refs_2_), channel_id=1, source_target_pairs={{4,8},{8,12},{5,9},{9,13},{6,10},{10,14},{7,11},{11,15},{20,24},{2... | collective-permute-start | bytes 786440 | tf_op jit(solution)/shard_map/ppermute | solution.py:403
  37.8 15.6 %collective-permute-start.18 = (bf16[32,4096]{1,0:T(8,128)(2,1)S(1)}, bf16[32,4096]{1,0:T(8,128)(2,1)S(1)}, u32[]{:S(2)}, u32[]{:S(2)}) collective-permute-start(bf16[32,4096]{1,0:T(8,128)(2,1)S(1)} %collective-permute-done.16.refs_3_), channel_id=1, source_target_pairs={{4,0},{8,4},{5,1},{9,5},{6,2},{10,6},{7,3},{11,7},{20,16},{24,20},... | collective-permute-start | bytes 786440 | tf_op jit(solution)/shard_map/ppermute | solution.py:404
  40.0 14.1 %collective-permute-start.22 = (bf16[32,4096]{1,0:T(8,128)(2,1)S(1)}, bf16[32,4096]{1,0:T(8,128)(2,1)S(1)}, u32[]{:S(2)}, u32[]{:S(2)}) collective-permute-start(bf16[32,4096]{1,0:T(8,128)(2,1)S(1)} %collective-permute-done.15.refs_2_), channel_id=1, source_target_pairs={{4,6},{6,4},{8,10},{10,8},{12,14},{14,12},{5,7},{7,5},{9,11},{11,9... | collective-permute-start | bytes 786440 | tf_op jit(solution)/shard_map/ppermute | solution.py:407
  43.0 15.0 %collective-permute-start.7 = (bf16[32,4096]{1,0:T(8,128)(2,1)S(1)}, bf16[32,4096]{1,0:T(8,128)(2,1)S(1)}, u32[]{:S(2)}, u32[]{:S(2)}) collective-permute-start(bf16[32,4096]{1,0:T(8,128)(2,1)S(1)} %collective-permute-done.5.refs_4_), channel_id=1, source_target_pairs={{4,0},{5,1},{6,2},{7,3},{20,16},{21,17},{22,18},{23,19}} | collective-permute-start | bytes 786440 | tf_op jit(solution)/shard_map/ppermute | solution.py:404
  44.3 16.5 %collective-permute-start.12 = (bf16[32,4096]{1,0:T(8,128)(2,1)S(1)}, bf16[32,4096]{1,0:T(8,128)(2,1)S(1)}, u32[]{:S(2)}, u32[]{:S(2)}) collective-permute-start(bf16[32,4096]{1,0:T(8,128)(2,1)S(1)} %collective-permute-done.5.refs_4_), channel_id=1, source_target_pairs={{0,2},{2,0},{4,6},{6,4},{1,3},{3,1},{5,7},{7,5},{16,18},{18,16},{2... | collective-permute-start | bytes 786440 | tf_op jit(solution)/shard_map/ppermute | solution.py:407
  46.8 14.8 %collective-permute-start.6 = (bf16[32,4096]{1,0:T(8,128)(2,1)S(1)}, bf16[32,4096]{1,0:T(8,128)(2,1)S(1)}, u32[]{:S(2)}, u32[]{:S(2)}) collective-permute-start(bf16[32,4096]{1,0:T(8,128)(2,1)S(1)} %collective-permute-done.2.refs_3_), channel_id=1, source_target_pairs={{8,12},{9,13},{10,14},{11,15},{24,28},{25,29},{26,30},{27,31}} | collective-permute-start | bytes 786440 | tf_op jit(solution)/shard_map/ppermute | solution.py:403
  53.4 8.9 %collective-permute-start.19 = (bf16[32,4096]{1,0:T(8,128)(2,1)S(1)}, bf16[32,4096]{1,0:T(8,128)(2,1)S(1)}, u32[]{:S(2)}, u32[]{:S(2)}) collective-permute-start(bf16[32,4096]{1,0:T(8,128)(2,1)S(1)} %collective-permute-done.17.refs_4_), channel_id=1, source_target_pairs={{8,12},{9,13},{10,14},{11,15},{24,28},{25,29},{26,30},{27,31}} | collective-permute-start | bytes 786440 | tf_op jit(solution)/shard_map/ppermute | solution.py:403
  54.0 11.3 %collective-permute-start.20 = (bf16[32,4096]{1,0:T(8,128)(2,1)S(1)}, bf16[32,4096]{1,0:T(8,128)(2,1)S(1)}, u32[]{:S(2)}, u32[]{:S(2)}) collective-permute-start(bf16[32,4096]{1,0:T(8,128)(2,1)S(1)} %collective-permute-done.18.refs_5_), channel_id=1, source_target_pairs={{4,0},{5,1},{6,2},{7,3},{20,16},{21,17},{22,18},{23,19}} | collective-permute-start | bytes 786440 | tf_op jit(solution)/shard_map/ppermute | solution.py:404
  58.1 10.8 %collective-permute-start.14 = (bf16[32,4096]{1,0:T(8,128)(2,1)S(1)}, bf16[32,4096]{1,0:T(8,128)(2,1)S(1)}, u32[]{:S(2)}, u32[]{:S(2)}) collective-permute-start(bf16[32,4096]{1,0:T(8,128)(2,1)S(1)} %collective-permute-done.7.refs_6_), channel_id=1, source_target_pairs={{0,2},{2,0},{1,3},{3,1},{16,18},{18,16},{17,19},{19,17}} | collective-permute-start | bytes 786440 | tf_op jit(solution)/shard_map/ppermute | solution.py:407
  60.9 10.8 %collective-permute-start.11 = (bf16[32,4096]{1,0:T(8,128)(2,1)S(1)}, bf16[32,4096]{1,0:T(8,128)(2,1)S(1)}, u32[]{:S(2)}, u32[]{:S(2)}) collective-permute-start(bf16[32,4096]{1,0:T(8,128)(2,1)S(1)} %collective-permute-done.2.refs_3_), channel_id=1, source_target_pairs={{8,10},{10,8},{12,14},{14,12},{9,11},{11,9},{13,15},{15,13},{24,26... | collective-permute-start | bytes 786440 | tf_op jit(solution)/shard_map/ppermute | solution.py:407
  61.6 10.8 %collective-permute-start.13 = (bf16[32,4096]{1,0:T(8,128)(2,1)S(1)}, bf16[32,4096]{1,0:T(8,128)(2,1)S(1)}, u32[]{:S(2)}, u32[]{:S(2)}) collective-permute-start(bf16[32,4096]{1,0:T(8,128)(2,1)S(1)} %collective-permute-done.6.refs_5_), channel_id=1, source_target_pairs={{12,14},{14,12},{13,15},{15,13},{28,30},{30,28},{29,31},{31,29}} | collective-permute-start | bytes 786440 | tf_op jit(solution)/shard_map/ppermute | solution.py:407
  62.3 18.7 %collective-permute-start.23 = (bf16[32,4096]{1,0:T(8,128)(2,1)S(1)}, bf16[32,4096]{1,0:T(8,128)(2,1)S(1)}, u32[]{:S(2)}, u32[]{:S(2)}) collective-permute-start(bf16[32,4096]{1,0:T(8,128)(2,1)S(1)} %collective-permute-done.16.refs_3_), channel_id=1, source_target_pairs={{0,2},{2,0},{4,6},{6,4},{8,10},{10,8},{1,3},{3,1},{5,7},{7,5},{9,1... | collective-permute-start | bytes 786440 | tf_op jit(solution)/shard_map/ppermute | solution.py:407
  65.3 15.7 %collective-permute-start.24 = (bf16[32,4096]{1,0:T(8,128)(2,1)S(1)}, bf16[32,4096]{1,0:T(8,128)(2,1)S(1)}, u32[]{:S(2)}, u32[]{:S(2)}) collective-permute-start(bf16[32,4096]{1,0:T(8,128)(2,1)S(1)} %collective-permute-done.17.refs_4_), channel_id=1, source_target_pairs={{8,10},{10,8},{12,14},{14,12},{9,11},{11,9},{13,15},{15,13},{24,26... | collective-permute-start | bytes 786440 | tf_op jit(solution)/shard_map/ppermute | solution.py:407
  68.9 12.2 %collective-permute-start.25 = (bf16[32,4096]{1,0:T(8,128)(2,1)S(1)}, bf16[32,4096]{1,0:T(8,128)(2,1)S(1)}, u32[]{:S(2)}, u32[]{:S(2)}) collective-permute-start(bf16[32,4096]{1,0:T(8,128)(2,1)S(1)} %collective-permute-done.18.refs_5_), channel_id=1, source_target_pairs={{0,2},{2,0},{4,6},{6,4},{1,3},{3,1},{5,7},{7,5},{16,18},{18,16},{2... | collective-permute-start | bytes 786440 | tf_op jit(solution)/shard_map/ppermute | solution.py:407
  71.7 9.4 %collective-permute-start.26 = (bf16[32,4096]{1,0:T(8,128)(2,1)S(1)}, bf16[32,4096]{1,0:T(8,128)(2,1)S(1)}, u32[]{:S(2)}, u32[]{:S(2)}) collective-permute-start(bf16[32,4096]{1,0:T(8,128)(2,1)S(1)} %collective-permute-done.19.refs_6_), channel_id=1, source_target_pairs={{12,14},{14,12},{13,15},{15,13},{28,30},{30,28},{29,31},{31,29}} | collective-permute-start | bytes 786440 | tf_op jit(solution)/shard_map/ppermute | solution.py:407
  72.4 10.8 %collective-permute-start.27 = (bf16[32,4096]{1,0:T(8,128)(2,1)S(1)}, bf16[32,4096]{1,0:T(8,128)(2,1)S(1)}, u32[]{:S(2)}, u32[]{:S(2)}) collective-permute-start(bf16[32,4096]{1,0:T(8,128)(2,1)S(1)} %collective-permute-done.20.refs_7_), channel_id=1, source_target_pairs={{0,2},{2,0},{1,3},{3,1},{16,18},{18,16},{17,19},{19,17}} | collective-permute-start | bytes 786440 | tf_op jit(solution)/shard_map/ppermute | solution.py:407
  88.8 6.8 %collective-permute-start.28 = (bf16[128,896]{1,0:T(8,128)(2,1)S(1)}, bf16[128,896]{1,0:T(8,128)(2,1)S(1)}, u32[]{:S(2)}, u32[]{:S(2)}) collective-permute-start(bf16[128,896]{1,0:T(8,128)(2,1)S(1)} %dynamic-slice_bitcast_fusion.4), channel_id=1, source_target_pairs={{0,16},{16,0},{1,17},{17,1},{2,18},{18,2},{3,19},{19,3},{4,20},{20... | collective-permute-start | bytes 688136 | tf_op jit(solution)/shard_map/ppermute | solution.py:24
  95.7 6.1 %collective-permute-start.32 = (bf16[128,896]{1,0:T(8,128)(2,1)S(1)}, bf16[128,896]{1,0:T(8,128)(2,1)S(1)}, u32[]{:S(2)}, u32[]{:S(2)}) collective-permute-start(bf16[128,896]{1,0:T(8,128)(2,1)S(1)} %fusion.27), channel_id=1, source_target_pairs={{0,16},{16,0},{1,17},{17,1},{2,18},{18,2},{3,19},{19,3},{4,20},{20... | collective-permute-start | bytes 688136 | tf_op jit(solution)/shard_map/ppermute | solution.py:24
  97.3 7.9 %collective-permute-start.29 = (bf16[128,896]{1,0:T(8,128)(2,1)S(1)}, bf16[128,896]{1,0:T(8,128)(2,1)S(1)}, u32[]{:S(2)}, u32[]{:S(2)}) collective-permute-start(bf16[128,896]{1,0:T(8,128)(2,1)S(1)} %fusion.27), channel_id=1, source_target_pairs={{0,4},{4,8},{8,12},{12,0},{1,5},{5,9},{9,13},{13,1},{2,6},{6,10},{... | collective-permute-start | bytes 688136 | tf_op jit(solution)/shard_map/ppermute | solution.py:29
  101.9 10.6 %collective-permute-start.33 = (bf16[2,128,896]{2,1,0:T(8,128)(2,1)S(1)}, bf16[2,128,896]{2,1,0:T(8,128)(2,1)S(1)}, u32[]{:S(2)}, u32[]{:S(2)}) collective-permute-start(bf16[2,128,896]{2,1,0:T(8,128)(2,1)S(1)} %pad_maximum_fusion.3.refs_0_), channel_id=1, source_target_pairs={{0,2},{2,0},{1,3},{3,1},{4,6},{6,4},{5,7},{7,5},{8,10},{10,8},{9,1... | collective-permute-start | bytes 1376264 | tf_op jit(solution)/shard_map/ppermute | solution.py:24
  102.8 6.0 %collective-permute-start.39 = (bf16[128,896]{1,0:T(8,128)(2,1)S(1)}, bf16[128,896]{1,0:T(8,128)(2,1)S(1)}, u32[]{:S(2)}, u32[]{:S(2)}) collective-permute-start(bf16[128,896]{1,0:T(8,128)(2,1)S(1)} %fusion.27), channel_id=1, source_target_pairs={{0,12},{4,0},{8,4},{12,8},{1,13},{5,1},{9,5},{13,9},{2,14},{6,2},{... | collective-permute-start | bytes 688136 | tf_op jit(solution)/shard_map/ppermute | solution.py:29
  105.2 6.4 %collective-permute-start.38 = (bf16[128,896]{1,0:T(8,128)(2,1)S(1)}, bf16[128,896]{1,0:T(8,128)(2,1)S(1)}, u32[]{:S(2)}, u32[]{:S(2)}) collective-permute-start(bf16[128,896]{1,0:T(8,128)(2,1)S(1)} %collective-permute-done.29), channel_id=1, source_target_pairs={{4,8},{8,12},{5,9},{9,13},{6,10},{10,14},{7,11},{11,15},{20,24},{2... | collective-permute-start | bytes 688136 | tf_op jit(solution)/shard_map/ppermute | solution.py:433
  108.9 7.9 %collective-permute-start.40 = (bf16[128,896]{1,0:T(8,128)(2,1)S(1)}, bf16[128,896]{1,0:T(8,128)(2,1)S(1)}, u32[]{:S(2)}, u32[]{:S(2)}) collective-permute-start(bf16[128,896]{1,0:T(8,128)(2,1)S(1)} %collective-permute-done.39), channel_id=1, source_target_pairs={{4,0},{8,4},{5,1},{9,5},{6,2},{10,6},{7,3},{11,7},{20,16},{24,20},... | collective-permute-start | bytes 688136 | tf_op jit(solution)/shard_map/ppermute | solution.py:434
  110.3 16.3 %collective-permute-start.34 = (bf16[2,128,896]{2,1,0:T(8,128)(2,1)S(1)}, bf16[2,128,896]{2,1,0:T(8,128)(2,1)S(1)}, u32[]{:S(2)}, u32[]{:S(2)}) collective-permute-start(bf16[2,128,896]{2,1,0:T(8,128)(2,1)S(1)} %pad_maximum_fusion.3.refs_0_), channel_id=1, source_target_pairs={{0,1},{1,0},{2,3},{3,2},{4,5},{5,4},{6,7},{7,6},{8,9},{9,8},{10,11... | collective-permute-start | bytes 1376264 | tf_op jit(solution)/shard_map/ppermute | solution.py:24
  110.4 8.5 %collective-permute-start.45 = (bf16[128,896]{1,0:T(8,128)(2,1)S(1)}, bf16[128,896]{1,0:T(8,128)(2,1)S(1)}, u32[]{:S(2)}, u32[]{:S(2)}) collective-permute-start(bf16[128,896]{1,0:T(8,128)(2,1)S(1)} %collective-permute-done.39), channel_id=1, source_target_pairs={{0,2},{2,0},{1,3},{3,1},{4,6},{6,4},{5,7},{7,5},{8,10},{10,8},{9,1... | collective-permute-start | bytes 688136 | tf_op jit(solution)/shard_map/ppermute | solution.py:24
  111.6 11.7 %collective-permute-start.30 = (bf16[128,896]{1,0:T(8,128)(2,1)S(1)}, bf16[128,896]{1,0:T(8,128)(2,1)S(1)}, u32[]{:S(2)}, u32[]{:S(2)}) collective-permute-start(bf16[128,896]{1,0:T(8,128)(2,1)S(1)} %collective-permute-done.29), channel_id=1, source_target_pairs={{0,2},{2,0},{1,3},{3,1},{4,6},{6,4},{5,7},{7,5},{8,10},{10,8},{9,1... | collective-permute-start | bytes 688136 | tf_op jit(solution)/shard_map/ppermute | solution.py:24
  112.5 15.3 %collective-permute-start.35 = (bf16[2,128,896]{2,1,0:T(8,128)(2,1)S(1)}, bf16[2,128,896]{2,1,0:T(8,128)(2,1)S(1)}, u32[]{:S(2)}, u32[]{:S(2)}) collective-permute-start(bf16[2,128,896]{2,1,0:T(8,128)(2,1)S(1)} %collective-permute-done.33.refs_1_), channel_id=1, source_target_pairs={{0,1},{1,0},{2,3},{3,2},{4,5},{5,4},{6,7},{7,6},{8,9},{9,8},{10,11... | collective-permute-start | bytes 1376264 | tf_op jit(solution)/shard_map/ppermute | solution.py:24
  116.8 8.3 %collective-permute-start.41 = (bf16[128,896]{1,0:T(8,128)(2,1)S(1)}, bf16[128,896]{1,0:T(8,128)(2,1)S(1)}, u32[]{:S(2)}, u32[]{:S(2)}) collective-permute-start(bf16[128,896]{1,0:T(8,128)(2,1)S(1)} %broadcast_select_fusion), channel_id=1, source_target_pairs={{0,16},{16,0},{1,17},{17,1},{2,18},{18,2},{3,19},{19,3},{4,20},{20... | collective-permute-start | bytes 688136 | tf_op jit(solution)/shard_map/ppermute | solution.py:24
  118.9 16.6 %collective-permute-start.46 = (bf16[2,128,896]{2,1,0:T(8,128)(2,1)S(1)}, bf16[2,128,896]{2,1,0:T(8,128)(2,1)S(1)}, u32[]{:S(2)}, u32[]{:S(2)}) collective-permute-start(bf16[2,128,896]{2,1,0:T(8,128)(2,1)S(1)} %pad_maximum_fusion.5.refs_0_), channel_id=1, source_target_pairs={{0,16},{16,0},{1,17},{17,1},{2,18},{18,2},{3,19},{19,3},{4,20},{20... | collective-permute-start | bytes 1376264 | tf_op jit(solution)/shard_map/ppermute | solution.py:24
  123.3 19.2 %collective-permute-start.47 = (bf16[2,128,896]{2,1,0:T(8,128)(2,1)S(1)}, bf16[2,128,896]{2,1,0:T(8,128)(2,1)S(1)}, u32[]{:S(2)}, u32[]{:S(2)}) collective-permute-start(bf16[2,128,896]{2,1,0:T(8,128)(2,1)S(1)} %pad_maximum_fusion.5.refs_0_), channel_id=1, source_target_pairs={{0,1},{1,0},{2,3},{3,2},{4,5},{5,4},{6,7},{7,6},{8,9},{9,8},{10,11... | collective-permute-start | bytes 1376264 | tf_op jit(solution)/shard_map/ppermute | solution.py:24
  125.1 17.5 %collective-permute-start.31 = (bf16[2,128,896]{2,1,0:T(8,128)(2,1)S(1)}, bf16[2,128,896]{2,1,0:T(8,128)(2,1)S(1)}, u32[]{:S(2)}, u32[]{:S(2)}) collective-permute-start(bf16[2,128,896]{2,1,0:T(8,128)(2,1)S(1)} %pad_maximum_fusion.2.refs_0_), channel_id=1, source_target_pairs={{0,16},{16,0},{1,17},{17,1},{2,18},{18,2},{3,19},{19,3},{4,20},{20... | collective-permute-start | bytes 1376264 | tf_op jit(solution)/shard_map/ppermute | solution.py:24
  126.6 11.1 %collective-permute-start.42 = (bf16[2,128,896]{2,1,0:T(8,128)(2,1)S(1)}, bf16[2,128,896]{2,1,0:T(8,128)(2,1)S(1)}, u32[]{:S(2)}, u32[]{:S(2)}) collective-permute-start(bf16[2,128,896]{2,1,0:T(8,128)(2,1)S(1)} %pad_maximum_fusion.4.refs_4_), channel_id=1, source_target_pairs={{0,2},{2,0},{1,3},{3,1},{4,6},{6,4},{5,7},{7,5},{8,10},{10,8},{9,1... | collective-permute-start | bytes 1376264 | tf_op jit(solution)/shard_map/ppermute | solution.py:24
  135.5 7.6 %collective-permute-start.48 = (bf16[2,128,896]{2,1,0:T(8,128)(2,1)S(1)}, bf16[2,128,896]{2,1,0:T(8,128)(2,1)S(1)}, u32[]{:S(2)}, u32[]{:S(2)}) collective-permute-start(bf16[2,128,896]{2,1,0:T(8,128)(2,1)S(1)} %collective-permute-done.46.refs_1_), channel_id=1, source_target_pairs={{0,1},{1,0},{2,3},{3,2},{4,5},{5,4},{6,7},{7,6},{8,9},{9,8},{10,11... | collective-permute-start | bytes 1376264 | tf_op jit(solution)/shard_map/ppermute | solution.py:24
  135.6 15.7 %collective-permute-start.36 = (bf16[2,128,896]{2,1,0:T(8,128)(2,1)S(1)}, bf16[2,128,896]{2,1,0:T(8,128)(2,1)S(1)}, u32[]{:S(2)}, u32[]{:S(2)}) collective-permute-start(bf16[2,128,896]{2,1,0:T(8,128)(2,1)S(1)} %pad_maximum_fusion.2.refs_0_), channel_id=1, source_target_pairs={{0,1},{1,0},{2,3},{3,2},{4,5},{5,4},{6,7},{7,6},{8,9},{9,8},{10,11... | collective-permute-start | bytes 1376264 | tf_op jit(solution)/shard_map/ppermute | solution.py:24
  137.8 13.6 %collective-permute-start.43 = (bf16[2,128,896]{2,1,0:T(8,128)(2,1)S(1)}, bf16[2,128,896]{2,1,0:T(8,128)(2,1)S(1)}, u32[]{:S(2)}, u32[]{:S(2)}) collective-permute-start(bf16[2,128,896]{2,1,0:T(8,128)(2,1)S(1)} %pad_maximum_fusion.4.refs_4_), channel_id=1, source_target_pairs={{0,1},{1,0},{2,3},{3,2},{4,5},{5,4},{6,7},{7,6},{8,9},{9,8},{10,11... | collective-permute-start | bytes 1376264 | tf_op jit(solution)/shard_map/ppermute | solution.py:24
  142.6 8.8 %collective-permute-start.44 = (bf16[2,128,896]{2,1,0:T(8,128)(2,1)S(1)}, bf16[2,128,896]{2,1,0:T(8,128)(2,1)S(1)}, u32[]{:S(2)}, u32[]{:S(2)}) collective-permute-start(bf16[2,128,896]{2,1,0:T(8,128)(2,1)S(1)} %collective-permute-done.42.refs_5_), channel_id=1, source_target_pairs={{0,1},{1,0},{2,3},{3,2},{4,5},{5,4},{6,7},{7,6},{8,9},{9,8},{10,11... | collective-permute-start | bytes 1376264 | tf_op jit(solution)/shard_map/ppermute | solution.py:24
  142.6 8.8 %collective-permute-start.37 = (bf16[2,128,896]{2,1,0:T(8,128)(2,1)S(1)}, bf16[2,128,896]{2,1,0:T(8,128)(2,1)S(1)}, u32[]{:S(2)}, u32[]{:S(2)}) collective-permute-start(bf16[2,128,896]{2,1,0:T(8,128)(2,1)S(1)} %collective-permute-done.31.refs_1_), channel_id=1, source_target_pairs={{0,1},{1,0},{2,3},{3,2},{4,5},{5,4},{6,7},{7,6},{8,9},{9,8},{10,11... | collective-permute-start | bytes 1376264 | tf_op jit(solution)/shard_map/ppermute | solution.py:24
  175.6 10.2 %collective-permute-start.49 = (bf16[2,256,1792]{2,1,0:T(8,128)(2,1)S(1)}, bf16[2,256,1792]{2,1,0:T(8,128)(2,1)S(1)}, u32[]{:S(2)}, u32[]{:S(2)}) collective-permute-start(bf16[2,256,1792]{2,1,0:T(8,128)(2,1)S(1)} %pad_maximum_fusion), channel_id=1, source_target_pairs={{0,1},{1,0},{2,3},{3,2},{4,5},{5,4},{6,7},{7,6},{8,9},{9,8},{10,11... | collective-permute-start | bytes 5505032 | tf_op jit(solution)/shard_map/ppermute | solution.py:24
  175.9 23.9 %collective-permute-start.56 = (bf16[2,256,1792]{2,1,0:T(8,128)(2,1)S(1)}, bf16[2,256,1792]{2,1,0:T(8,128)(2,1)S(1)}, u32[]{:S(2)}, u32[]{:S(2)}) collective-permute-start(bf16[2,256,1792]{2,1,0:T(8,128)(2,1)S(1)} %pad_maximum_fusion.1), channel_id=1, source_target_pairs={{0,1},{1,0},{2,3},{3,2},{4,5},{5,4},{6,7},{7,6},{8,9},{9,8},{10,11... | collective-permute-start | bytes 5505032 | tf_op jit(solution)/shard_map/ppermute | solution.py:24
  187.1 12.5 %collective-permute-start.50 = (bf16[128,1792]{1,0:T(8,128)(2,1)S(1)}, bf16[128,1792]{1,0:T(8,128)(2,1)S(1)}, u32[]{:S(2)}, u32[]{:S(2)}) collective-permute-start(bf16[128,1792]{1,0:T(8,128)(2,1)S(1)} %slice.67), channel_id=1, source_target_pairs={{0,16},{16,0},{1,17},{17,1},{2,18},{18,2},{3,19},{19,3},{4,20},{20... | collective-permute-start | bytes 1376264 | tf_op jit(solution)/shard_map/ppermute | solution.py:24
  188.9 15.1 %collective-permute-start.53 = (bf16[2,128,896]{2,1,0:T(8,128)(2,1)S(1)}, bf16[2,128,896]{2,1,0:T(8,128)(2,1)S(1)}, u32[]{:S(2)}, u32[]{:S(2)}) collective-permute-start(bf16[2,128,896]{2,1,0:T(8,128)(2,1)S(1)} %constant_dynamic-slice_fusion.2), channel_id=1, source_target_pairs={{0,2},{2,0},{1,3},{3,1},{4,6},{6,4},{5,7},{7,5},{8,10},{10,8},{9,1... | collective-permute-start | bytes 1376264 | tf_op jit(solution)/shard_map/ppermute | solution.py:24
  201.1 19.3 %collective-permute-start.60 = (bf16[128,1792]{1,0:T(8,128)(2,1)S(1)}, bf16[128,1792]{1,0:T(8,128)(2,1)S(1)}, u32[]{:S(2)}, u32[]{:S(2)}) collective-permute-start(bf16[128,1792]{1,0:T(8,128)(2,1)S(1)} %slice.73), channel_id=1, source_target_pairs={{0,16},{16,0},{1,17},{17,1},{2,18},{18,2},{3,19},{19,3},{4,20},{20... | collective-permute-start | bytes 1376264 | tf_op jit(solution)/shard_map/ppermute | solution.py:24
  202.8 8.6 %collective-permute-start.51 = (bf16[128,896]{1,0:T(8,128)(2,1)S(1)}, bf16[128,896]{1,0:T(8,128)(2,1)S(1)}, u32[]{:S(2)}, u32[]{:S(2)}) collective-permute-start(bf16[128,896]{1,0:T(8,128)(2,1)S(1)} %constant_dynamic-slice_fusion.3), channel_id=1, source_target_pairs={{0,2},{2,0},{1,3},{3,1},{4,6},{6,4},{5,7},{7,5},{8,10},{10,8},{9,1... | collective-permute-start | bytes 688136 | tf_op jit(solution)/shard_map/ppermute | solution.py:24
  204.3 13.4 %collective-permute-start.54 = (bf16[128,896]{1,0:T(8,128)(2,1)S(1)}, bf16[128,896]{1,0:T(8,128)(2,1)S(1)}, u32[]{:S(2)}, u32[]{:S(2)}) collective-permute-start(bf16[128,896]{1,0:T(8,128)(2,1)S(1)} %slice_bitcast_fusion.4), channel_id=1, source_target_pairs={{0,16},{16,0},{1,17},{17,1},{2,18},{18,2},{3,19},{19,3},{4,20},{20... | collective-permute-start | bytes 688136 | tf_op jit(solution)/shard_map/ppermute | solution.py:24
  205.1 14.1 %collective-permute-start.57 = (bf16[2,128,896]{2,1,0:T(8,128)(2,1)S(1)}, bf16[2,128,896]{2,1,0:T(8,128)(2,1)S(1)}, u32[]{:S(2)}, u32[]{:S(2)}) collective-permute-start(bf16[2,128,896]{2,1,0:T(8,128)(2,1)S(1)} %constant_dynamic-slice_fusion.1), channel_id=1, source_target_pairs={{0,2},{2,0},{1,3},{3,1},{4,6},{6,4},{5,7},{7,5},{8,10},{10,8},{9,1... | collective-permute-start | bytes 1376264 | tf_op jit(solution)/shard_map/ppermute | solution.py:24
  211.6 16.5 %collective-permute-start.52 = (bf16[128,896]{1,0:T(8,128)(2,1)S(1)}, bf16[128,896]{1,0:T(8,128)(2,1)S(1)}, u32[]{:S(2)}, u32[]{:S(2)}) collective-permute-start(bf16[128,896]{1,0:T(8,128)(2,1)S(1)} %add_convert_fusion.6), channel_id=1, source_target_pairs={{0,8},{4,12},{8,0},{12,4},{1,9},{5,13},{9,1},{13,5},{2,10},{6,14},... | collective-permute-start | bytes 688136 | tf_op jit(solution)/shard_map/ppermute | solution.py:29
  217.8 10.4 %collective-permute-start.55 = (bf16[128,896]{1,0:T(8,128)(2,1)S(1)}, bf16[128,896]{1,0:T(8,128)(2,1)S(1)}, u32[]{:S(2)}, u32[]{:S(2)}) collective-permute-start(bf16[128,896]{1,0:T(8,128)(2,1)S(1)} %fusion.25), channel_id=1, source_target_pairs={{0,4},{4,8},{8,12},{12,0},{1,5},{5,9},{9,13},{13,1},{2,6},{6,10},{... | collective-permute-start | bytes 688136 | tf_op jit(solution)/shard_map/ppermute | solution.py:29
  219.4 6.1 %collective-permute-start.58 = (bf16[128,896]{1,0:T(8,128)(2,1)S(1)}, bf16[128,896]{1,0:T(8,128)(2,1)S(1)}, u32[]{:S(2)}, u32[]{:S(2)}) collective-permute-start(bf16[128,896]{1,0:T(8,128)(2,1)S(1)} %slice_bitcast_fusion.2), channel_id=1, source_target_pairs={{0,16},{16,0},{1,17},{17,1},{2,18},{18,2},{3,19},{19,3},{4,20},{20... | collective-permute-start | bytes 688136 | tf_op jit(solution)/shard_map/ppermute | solution.py:24
  220.7 7.4 %collective-permute-start.61 = (bf16[128,896]{1,0:T(8,128)(2,1)S(1)}, bf16[128,896]{1,0:T(8,128)(2,1)S(1)}, u32[]{:S(2)}, u32[]{:S(2)}) collective-permute-start(bf16[128,896]{1,0:T(8,128)(2,1)S(1)} %constant_dynamic-slice_fusion), channel_id=1, source_target_pairs={{0,2},{2,0},{1,3},{3,1},{4,6},{6,4},{5,7},{7,5},{8,10},{10,8},{9,1... | collective-permute-start | bytes 688136 | tf_op jit(solution)/shard_map/ppermute | solution.py:24
  225.6 6.1 %collective-permute-start.59 = (bf16[128,896]{1,0:T(8,128)(2,1)S(1)}, bf16[128,896]{1,0:T(8,128)(2,1)S(1)}, u32[]{:S(2)}, u32[]{:S(2)}) collective-permute-start(bf16[128,896]{1,0:T(8,128)(2,1)S(1)} %fusion.24), channel_id=1, source_target_pairs={{0,12},{4,0},{8,4},{12,8},{1,13},{5,1},{9,5},{13,9},{2,14},{6,2},{... | collective-permute-start | bytes 688136 | tf_op jit(solution)/shard_map/ppermute | solution.py:29
  232.0 1.4 collective-permute-start.62
  (4 other events, 22.9 us)

commit v4 on v3

--- a/solution.py
+++ b/solution.py
@@ -187,11 +187,10 @@
     if not first:
         gate_in, up_in, *rest = rest
     if last:
-        weight_ref, hidden_ref, *rest = rest
+        weight_ref, down_ref, hidden_ref, send_ref, *rest, down_rows, down_fetched = rest
     else:
         gate_out, up_out, *rest = rest
-    rows_ref, gate_rows, up_rows, *rest, arrived, fetched, summed = rest
-    sums = rest
+    rows_ref, gate_rows, up_rows, *sums, arrived, fetched, summed = rest
     size, width = pieces[0].shape[1:]
     depth, columns = 2 * width, gate_ref.shape[1]
     tile = min(512, columns)
@@ -238,6 +237,10 @@
                 copy.start()
             if not first:
                 sum_copy(n, matrix, False).start()
+    if last:
+        down = down_copies(place_ref, count + 1, send_ref.shape[0], down_ref, down_rows, down_fetched)
+        for copy in down:
+            copy.start()
     for copy in copies:
         copy.wait()
 
@@ -267,13 +270,84 @@
         return 0
 
     lax.fori_loop(0, steps, step, 0)
-    if not last:
+    if last:
+        for copy in down:
+            copy.wait()
+        rows = send_ref.shape[1]
+        for i in range(send_ref.shape[0]):
+            down_products(hidden_ref[rows:], down_rows, i, send_ref)
+    else:
         for n in range(steps):
             for matrix in range(2):
                 sum_copy(n, matrix, True).wait()
 
 
-def hidden_part(units, places, pieces, w_gate, w_up, sums=None, weight=None):
+def down_copies(place_ref, start, count, source_ref, target_ref, arrived):
+    depth, width = source_ref.shape[0], target_ref.shape[1] // count
+    half = depth // 2
+    return [
+        pltpu.make_async_copy(
+            source_ref.at[
+                pl.ds(j * half, half),
+                pl.ds(pl.multiple_of(place_ref[start + i] * width, 128), width),
+            ],
+            target_ref.at[pl.ds(j * half, half), pl.ds(i * width, width)],
+            arrived.at[2 * i + j],
+        )
+        for i in range(count)
+        for j in range(2)
+    ]
+
+
+def down_products(rows, weight_ref, i, out_ref):
+    width, tile = out_ref.shape[2], 256
+
+    def step(n, _):
+        columns = pl.ds(pl.multiple_of(i * width + n * tile, tile), tile)
+        out_ref[i, :, pl.ds(pl.multiple_of(n * tile, tile), tile)] = jnp.dot(
+            rows, weight_ref[:, columns], preferred_element_type=F32
+        ).astype(out_ref.dtype)
+        return 0
+
+    lax.fori_loop(0, width // tile, step, 0)
+
+
+def down_kernel(halves, place_ref, hidden_ref, weight_ref, *refs):
+    outs, (weight_rows, arrived) = refs[:-2], refs[-2:]
+    amount, rows, _ = outs[0].shape
+    copies = down_copies(place_ref, 0, amount, weight_ref, weight_rows, arrived)
+    for copy in copies:
+        copy.start()
+    for i in range(amount):
+        for copy in copies[2 * i : 2 * i + 2]:
+            copy.wait()
+        for half, out_ref in zip(halves, outs):
+            down_products(hidden_ref[half * rows : (half + 1) * rows], weight_rows, i, out_ref)
+
+
+def down_part(places, halves, hidden, w_down, width):
+    rows, units = hidden.shape[0] // 2, hidden.shape[1]
+    vmem = pl.BlockSpec(memory_space=pltpu.VMEM)
+    return pl.pallas_call(
+        functools.partial(down_kernel, halves),
+        in_specs=[
+            pl.BlockSpec(memory_space=pltpu.SMEM),
+            vmem,
+            pl.BlockSpec(memory_space=pl.ANY),
+        ],
+        out_specs=[vmem] * len(halves),
+        out_shape=[jax.ShapeDtypeStruct((2, rows, width), BF16)] * len(halves),
+        scratch_shapes=[pltpu.VMEM((units, 2 * width), BF16), pltpu.SemaphoreType.DMA((4,))],
+        compiler_params=pltpu.CompilerParams(vmem_limit_bytes=18 * MIB),
+        cost_estimate=pl.CostEstimate(
+            flops=4 * len(halves) * rows * units * width,
+            bytes_accessed=4 * units * width,
+            transcendentals=0,
+        ),
+    )(places, hidden, in_hbm(w_down))
+
+
+def hidden_part(units, places, pieces, w_gate, w_up, sums=None, weight=None, w_down=None):
     first, last = sums is None, weight is not None
     size, width = pieces[0].shape[1:]
     rows, columns, depth = 4 * size, w_gate.shape[1], 2 * width
@@ -291,10 +365,16 @@
     if not first:
         in_specs += [anywhere] * 2
         operands += list(sums)
+    scratch = []
     if last:
-        in_specs += [vmem]
-        operands += [weight]
-        out_shape, out_specs = jax.ShapeDtypeStruct((rows, columns), BF16), vmem
+        in_specs += [vmem, anywhere]
+        operands += [weight, in_hbm(w_down)]
+        out_shape = [
+            jax.ShapeDtypeStruct((rows, columns), BF16),
+            jax.ShapeDtypeStruct((2, rows // 2, depth), BF16),
+        ]
+        out_specs = [vmem] * 2
+        scratch = [pltpu.VMEM((columns, 2 * depth), BF16), pltpu.SemaphoreType.DMA((4,))]
     else:
         out_shape = [jax.ShapeDtypeStruct((rows, columns), F32)] * 2
         out_specs = [anywhere] * 2
@@ -311,8 +391,11 @@
             pltpu.SemaphoreType.DMA((sum(len(unit) for unit in layout),)),
             pltpu.SemaphoreType.DMA((steps, 2, len(units), 2)),
             pltpu.SemaphoreType.DMA((steps, 2, 2)),
-        ],
-        compiler_params=pltpu.CompilerParams(vmem_limit_bytes=(12 + 10 * len(units)) * MIB),
+        ]
+        + scratch,
+        compiler_params=pltpu.CompilerParams(
+            vmem_limit_bytes=(12 + 10 * len(units) + 10 * last) * MIB
+        ),
         cost_estimate=pl.CostEstimate(
             flops=4 * rows * len(units) * depth * columns,
             bytes_accessed=4 * len(units) * depth * columns,
@@ -375,7 +458,16 @@
     half, back = line // 2, line - 1
     groups = ([0], [back], [1, half])
     group_places = [
-        jnp.stack([(at - k) % line for k in group] + [side]).astype(jnp.int32) for group in groups
+        jnp.stack(
+            [(at - k) % line for k in group]
+            + [side]
+            + ([(at + k) % line for k in (half, 1)] if half in group else [])
+        ).astype(jnp.int32)
+        for group in groups
+    ]
+    down_places = [
+        jnp.stack([(at + k) % line for k in group]).astype(jnp.int32)
+        for group in ((half, 1), (back, 0))
     ]
     index = dict(
         own_sect=sect,
@@ -385,14 +477,15 @@
         upper=at >= half,
         near_core=core == 0,
         share=lax.axis_index("tp"),
-        columns=[(at + k) % line * 2 * chip_width for k in shifts],
     )
     length, partial, blocks = heads.shape[1] // 2, None, []
     for part in range(2):
         own = heads[:, part * length : (part + 1) * length]
         if part:
-            own, weight, residual_rows, place, group_places, index = lax.optimization_barrier(
-                (own, weight, residual_rows, place, group_places, index)
+            own, weight, residual_rows, place, group_places, down_places, index = (
+                lax.optimization_barrier(
+                    (own, weight, residual_rows, place, group_places, down_places, index)
+                )
             )
         rights, lefts = [own], [own]
         for k in shifts[1:]:
@@ -461,8 +554,9 @@
             w_up[0],
             sums,
             weight if half in group else None,
+            w_down[0] if half in group else None,
         )
-    hidden = sums
+    hidden, send = sums
 
     def own_side(value):
         return part_of(value, index["own_side"], chip_width, value.ndim - 1)
@@ -470,24 +564,19 @@
     def other_side(value):
         return part_of(value, index["other_side"], chip_width, value.ndim - 1)
 
-    count = row_total // 2
-    send, keep = (
-        jnp.dot(rows, w_down[0], preferred_element_type=F32) for rows in (hidden[count:], hidden[:count])
-    )
-    if tp > 1:
-        send, keep = (lax.psum(v, "tp") for v in (send, keep))
-    send, keep = send.astype(BF16), keep.astype(BF16)
-
-    def columns_to(value, k):
-        return part_of(value, index["columns"][k], 2 * chip_width, 1)
+    def summed(value):
+        return lax.psum(value.astype(F32), "tp").astype(BF16) if tp > 1 else value
 
     total, held = own_rows.astype(F32), None
-    for group in ((half, 1), (back, 0)):
-        arrived = swap(jnp.stack([columns_to(send, k) for k in group]), "core")
-        if held is not None:
-            arrived, held = lax.optimization_barrier((arrived, held))
-        for k, arrival in zip(group, arrived):
-            part = add(columns_to(keep, k), arrival).reshape(2, -1, 2 * chip_width)
+    for group, places in zip(((half, 1), (back, 0)), down_places):
+        if held is None:
+            arrived = swap(summed(send), "core")
+            (keep,) = down_part(places, [0], hidden, w_down[0], 2 * chip_width)
+        else:
+            keep, send = down_part(places, [0, 1], hidden, w_down[0], 2 * chip_width)
+            arrived, held = lax.optimization_barrier((swap(summed(send), "core"), held))
+        for k, part in zip(group, add(summed(keep), arrived)):
+            part = part.reshape(2, -1, 2 * chip_width)
             if k % 2 == 0:
                 part = add(part[0], swap(part[1], "sect"))
                 held = part

time: 235 us -> 234 us (level)
  Pallas kernels: 46 us -> 68.8 us
  matrix products: 21 us -> 1.98 us
    dot_general x2 -> x0, matrix products: 19 us -> none  [on_device(): jnp.dot(rows, w_down[0], preferred_element_type=F32)]
    pallas_call x0 -> x2, Pallas kernels: none -> 18.4 us  [down_part(): pl.pallas_call(functools.partial(down_kernel, halves), in_specs=[pl.Block...]
    pallas_call x3, Pallas kernels: 28.2 us -> 32.6 us  [hidden_part(): pl.pallas_call(functools.partial(hidden_kernel, layout, first, last), in_...]
  transfers between devices with their start and end apart: 63 -> 63, of which waited for: 26 -> 26; matrix products, arithmetic and copies ran while one was open for 7% -> 3% of each run, Pallas kernels for 12% -> 20%
where the time goes in v4:
time: 234 us
  waiting for transfers between devices  84.4 us (36%)
  starting transfers between devices  71.4 us (31%)
  Pallas kernels  68.8 us (29%)
  local copies, waits for them, and re-layouts  3.3 us (1%)
  other arithmetic  2.83 us (1%)
    ppermute x30, waiting for transfers between devices, swap(): return lax.ppermute(value, axis, [(0, 1), (1, 0)])  48.6 us
    pallas_call x3, Pallas kernels, hidden_part(): pl.pallas_call(functools.partial(hidden_kernel, layout, first, last), in_...  32.6 us
    ppermute x30, starting transfers between devices, swap(): return lax.ppermute(value, axis, [(0, 1), (1, 0)])  23.4 us
    ppermute x14, starting transfers between devices, on_device(): lax.ppermute(value, ('line', 'side'), [(2 * i + y, 2 * i + 1 - y) for i i...  23.3 us
    pallas_call x2, Pallas kernels, down_part(): pl.pallas_call(functools.partial(down_kernel, halves), in_specs=[pl.Block...  18.4 us
    ppermute x6, waiting for transfers between devices, on_device(): lefts.append(lax.ppermute(lefts[-1], 'line', left))  12.4 us
    ppermute x6, starting transfers between devices, on_device(): rights.append(lax.ppermute(rights[-1], 'line', right))  11.8 us
    pallas_call x2, Pallas kernels, project(): pl.pallas_call(functools.partial(project_kernel, slots, start, first), in...  11.1 us
  transfers between devices with their start and end apart: 63, of which 26 were waited for; matrix products, arithmetic and copies ran while one was open for 3% of the time, Pallas kernels for 20%

profile of v4, /device:TPU:0, one launch (start us, length us, event | category | flops | bytes accessed | tf_op | source)
XLA Modules:
  0.0 233.6 jit_solution(4715769091124750711)
XLA Ops:
  1.1 6.7 %shard_map.109 = bf16[32,64,512]{2,1,0:T(8,128)(2,1)S(1)} custom-call(s32[32]{0:T(128)S(1)} %copy-done, bf16[32,64,576]{2,1,0:T(8,128)(2,1)} %query_ref.1, bf16[32,576,128]{2,1,0:T(8,128)(2,1)} %bitcast.109), custom_call_target="tpu_custom_call" | custom-call | flops 570425344 | bytes 9175040 | tf_op jit(solution)/shard_map/pallas_call | solution.py:71
  7.9 2.0 fusion.5
  10.0 4.5 %collective-permute-start.1 = (bf16[32,4096]{1,0:T(8,128)(2,1)S(1)}, bf16[32,4096]{1,0:T(8,128)(2,1)S(1)}, u32[]{:S(2)}, u32[]{:S(2)}) collective-permute-start(bf16[32,4096]{1,0:T(8,128)(2,1)S(1)} %get-tuple-element.63.refs_0_), channel_id=1, source_target_pairs={{0,4},{4,8},{8,12},{1,5},{5,9},{9,13},{2,6},{6,10},{10,14},{3,7},{... | collective-permute-start | bytes 786440 | tf_op jit(solution)/shard_map/ppermute | solution.py:496
  14.5 1.3 collective-permute-start.4
  15.8 1.6 collective-permute-start.8
  19.4 4.6 %collective-permute-start.15 = (bf16[32,4096]{1,0:T(8,128)(2,1)S(1)}, bf16[32,4096]{1,0:T(8,128)(2,1)S(1)}, u32[]{:S(2)}, u32[]{:S(2)}) collective-permute-start(bf16[32,4096]{1,0:T(8,128)(2,1)S(1)} %get-tuple-element.39.refs_1_), channel_id=1, source_target_pairs={{0,4},{4,8},{8,12},{1,5},{5,9},{9,13},{2,6},{6,10},{10,14},{3,7},{... | collective-permute-start | bytes 786440 | tf_op jit(solution)/shard_map/ppermute | solution.py:496
  24.0 1.3 collective-permute-start.16
  26.0 1.2 collective-permute-start.21
  27.1 2.7 %collective-permute-done.15.refs_2_ = bf16[32,4096]{1,0:T(8,128)(2,1)S(1)} collective-permute-done((bf16[32,4096]{1,0:T(8,128)(2,1)S(1)}, bf16[32,4096]{1,0:T(8,128)(2,1)S(1)}, u32[]{:S(2)}, u32[]{:S(2)}) %collective-permute-start.15) | collective-permute-done | bytes 262176 | tf_op jit(solution)/shard_map/ppermute | solution.py:496
  29.8 1.3 collective-permute-start.5
  31.1 2.9 %collective-permute-done.16.refs_3_ = bf16[32,4096]{1,0:T(8,128)(2,1)S(1)} collective-permute-done((bf16[32,4096]{1,0:T(8,128)(2,1)S(1)}, bf16[32,4096]{1,0:T(8,128)(2,1)S(1)}, u32[]{:S(2)}, u32[]{:S(2)}) %collective-permute-start.16) | collective-permute-done | bytes 262176 | tf_op jit(solution)/shard_map/ppermute | solution.py:497
  33.9 2.4 %collective-permute-start.10 = (bf16[32,4096]{1,0:T(8,128)(2,1)S(1)}, bf16[32,4096]{1,0:T(8,128)(2,1)S(1)}, u32[]{:S(2)}, u32[]{:S(2)}) collective-permute-start(bf16[32,4096]{1,0:T(8,128)(2,1)S(1)} %collective-permute-done.4.refs_2_), channel_id=1, source_target_pairs={{0,2},{2,0},{4,6},{6,4},{8,10},{10,8},{1,3},{3,1},{5,7},{7,5},{9,1... | collective-permute-start | bytes 786440 | tf_op jit(solution)/shard_map/ppermute | solution.py:500
  37.8 1.3 collective-permute-start.18
  39.1 0.9 collective-permute-done.5.refs_4_
  40.6 2.4 %collective-permute-done.10.refs_9_ = bf16[32,4096]{1,0:T(8,128)(2,1)S(1)} collective-permute-done((bf16[32,4096]{1,0:T(8,128)(2,1)S(1)}, bf16[32,4096]{1,0:T(8,128)(2,1)S(1)}, u32[]{:S(2)}, u32[]{:S(2)}) %collective-permute-start.10) | collective-permute-done | bytes 262176 | tf_op jit(solution)/shard_map/ppermute | solution.py:500
  43.0 1.3 collective-permute-start.7
  44.3 2.4 %collective-permute-start.12 = (bf16[32,4096]{1,0:T(8,128)(2,1)S(1)}, bf16[32,4096]{1,0:T(8,128)(2,1)S(1)}, u32[]{:S(2)}, u32[]{:S(2)}) collective-permute-start(bf16[32,4096]{1,0:T(8,128)(2,1)S(1)} %collective-permute-done.5.refs_4_), channel_id=1, source_target_pairs={{0,2},{2,0},{4,6},{6,4},{1,3},{3,1},{5,7},{7,5},{16,18},{18,16},{2... | collective-permute-start | bytes 786440 | tf_op jit(solution)/shard_map/ppermute | solution.py:500
  47.5 5.9 %collective-permute-done.18.refs_5_ = bf16[32,4096]{1,0:T(8,128)(2,1)S(1)} collective-permute-done((bf16[32,4096]{1,0:T(8,128)(2,1)S(1)}, bf16[32,4096]{1,0:T(8,128)(2,1)S(1)}, u32[]{:S(2)}, u32[]{:S(2)}) %collective-permute-start.18) | collective-permute-done | bytes 262176 | tf_op jit(solution)/shard_map/ppermute | solution.py:497
  54.0 1.3 collective-permute-start.20
  55.3 2.7 %collective-permute-done.7.refs_6_ = bf16[32,4096]{1,0:T(8,128)(2,1)S(1)} collective-permute-done((bf16[32,4096]{1,0:T(8,128)(2,1)S(1)}, bf16[32,4096]{1,0:T(8,128)(2,1)S(1)}, u32[]{:S(2)}, u32[]{:S(2)}) %collective-permute-start.7) | collective-permute-done | bytes 262176 | tf_op jit(solution)/shard_map/ppermute | solution.py:497
  58.1 2.8 %collective-permute-start.14 = (bf16[32,4096]{1,0:T(8,128)(2,1)S(1)}, bf16[32,4096]{1,0:T(8,128)(2,1)S(1)}, u32[]{:S(2)}, u32[]{:S(2)}) collective-permute-start(bf16[32,4096]{1,0:T(8,128)(2,1)S(1)} %collective-permute-done.7.refs_6_), channel_id=1, source_target_pairs={{0,2},{2,0},{1,3},{3,1},{16,18},{18,16},{17,19},{19,17}} | collective-permute-start | bytes 786440 | tf_op jit(solution)/shard_map/ppermute | solution.py:500
  62.3 3.0 %collective-permute-start.23 = (bf16[32,4096]{1,0:T(8,128)(2,1)S(1)}, bf16[32,4096]{1,0:T(8,128)(2,1)S(1)}, u32[]{:S(2)}, u32[]{:S(2)}) collective-permute-start(bf16[32,4096]{1,0:T(8,128)(2,1)S(1)} %collective-permute-done.16.refs_3_), channel_id=1, source_target_pairs={{0,2},{2,0},{4,6},{6,4},{8,10},{10,8},{1,3},{3,1},{5,7},{7,5},{9,1... | collective-permute-start | bytes 786440 | tf_op jit(solution)/shard_map/ppermute | solution.py:500
  66.0 2.9 %collective-permute-done.14.refs_13_ = bf16[32,4096]{1,0:T(8,128)(2,1)S(1)} collective-permute-done((bf16[32,4096]{1,0:T(8,128)(2,1)S(1)}, bf16[32,4096]{1,0:T(8,128)(2,1)S(1)}, u32[]{:S(2)}, u32[]{:S(2)}) %collective-permute-start.14) | collective-permute-done | bytes 262176 | tf_op jit(solution)/shard_map/ppermute | solution.py:500
  68.9 2.8 %collective-permute-start.25 = (bf16[32,4096]{1,0:T(8,128)(2,1)S(1)}, bf16[32,4096]{1,0:T(8,128)(2,1)S(1)}, u32[]{:S(2)}, u32[]{:S(2)}) collective-permute-start(bf16[32,4096]{1,0:T(8,128)(2,1)S(1)} %collective-permute-done.18.refs_5_), channel_id=1, source_target_pairs={{0,2},{2,0},{4,6},{6,4},{1,3},{3,1},{5,7},{7,5},{16,18},{18,16},{2... | collective-permute-start | bytes 786440 | tf_op jit(solution)/shard_map/ppermute | solution.py:500
  72.4 3.0 %collective-permute-start.27 = (bf16[32,4096]{1,0:T(8,128)(2,1)S(1)}, bf16[32,4096]{1,0:T(8,128)(2,1)S(1)}, u32[]{:S(2)}, u32[]{:S(2)}) collective-permute-start(bf16[32,4096]{1,0:T(8,128)(2,1)S(1)} %collective-permute-done.20.refs_7_), channel_id=1, source_target_pairs={{0,2},{2,0},{1,3},{3,1},{16,18},{18,16},{17,19},{19,17}} | collective-permute-start | bytes 786440 | tf_op jit(solution)/shard_map/ppermute | solution.py:500
  75.4 5.6 %shard_map.110.refs_0_ = f32[256,896]{1,0:T(8,128)S(1)} custom-call(s32[17]{0:T(128)S(1)} %stack.169.place_ref, bf16[448,8192]{1,0:T(8,128)(2,1)} %bitcast.107, bf16[448,8192]{1,0:T(8,128)(2,1)} %collective-permute-done.3.sibling_ref, bf16[32,4096]{1,0:T(8,128)(2,1)S(1)} %get-tuple-element.63.refs_0_, bf16[32,4096]{1,0:T(8,128)(2,1)S(1)} %collective-permute-done.1.refs_1_, ...), custom_call_target="tpu_custom_call" | custom-call | flops 1879048192 | bytes 9437184 | tf_op jit(solution)/shard_map/pallas_call | solution.py:161
  81.0 2.1 collective-permute-done.27.refs_14_
  83.2 5.6 %shard_map.111 = bf16[256,896]{1,0:T(8,128)(2,1)S(1)} custom-call(s32[17]{0:T(128)S(1)} %stack.169.place_ref, bf16[448,8192]{1,0:T(8,128)(2,1)} %bitcast.108, bf16[448,8192]{1,0:T(8,128)(2,1)} %collective-permute-done.3.sibling_ref, f32[256,896]{1,0:T(8,128)S(1)} %shard_map.110.refs_0_, bf16[32,4096]{1,0:T(8,128)(2,1)S(1)} %get-tuple-element.39.refs_1_, ...), custom_call_target="tpu_custom_call" | custom-call | flops 1879048192 | bytes 9437184 | tf_op jit(solution)/shard_map/pallas_call | solution.py:161
  88.8 1.6 collective-permute-start.28
  90.3 5.3 %collective-permute-done.28 = bf16[128,896]{1,0:T(8,128)(2,1)S(1)} collective-permute-done((bf16[128,896]{1,0:T(8,128)(2,1)S(1)}, bf16[128,896]{1,0:T(8,128)(2,1)S(1)}, u32[]{:S(2)}, u32[]{:S(2)}) %collective-permute-start.28) | collective-permute-done | bytes 229408 | tf_op jit(solution)/shard_map/ppermute | solution.py:24
  95.7 1.6 collective-permute-start.32
  97.3 4.5 %collective-permute-done.32 = bf16[128,896]{1,0:T(8,128)(2,1)S(1)} collective-permute-done((bf16[128,896]{1,0:T(8,128)(2,1)S(1)}, bf16[128,896]{1,0:T(8,128)(2,1)S(1)}, u32[]{:S(2)}, u32[]{:S(2)}) %collective-permute-start.32) | collective-permute-done | bytes 229408 | tf_op jit(solution)/shard_map/ppermute | solution.py:24
  101.9 1.0 collective-permute-start.33
  102.8 2.4 %collective-permute-done.29 = bf16[128,896]{1,0:T(8,128)(2,1)S(1)} collective-permute-done((bf16[128,896]{1,0:T(8,128)(2,1)S(1)}, bf16[128,896]{1,0:T(8,128)(2,1)S(1)}, u32[]{:S(2)}, u32[]{:S(2)}) %collective-permute-start.29) | collective-permute-done | bytes 229408 | tf_op jit(solution)/shard_map/ppermute | solution.py:29
  105.9 3.0 %collective-permute-done.39 = bf16[128,896]{1,0:T(8,128)(2,1)S(1)} collective-permute-done((bf16[128,896]{1,0:T(8,128)(2,1)S(1)}, bf16[128,896]{1,0:T(8,128)(2,1)S(1)}, u32[]{:S(2)}, u32[]{:S(2)}) %collective-permute-start.39) | collective-permute-done | bytes 229408 | tf_op jit(solution)/shard_map/ppermute | solution.py:29
  108.8 1.3 collective-permute-start.40
  110.2 1.2 collective-permute-start.45
  112.3 4.4 %collective-permute-done.40 = bf16[128,896]{1,0:T(8,128)(2,1)S(1)} collective-permute-done((bf16[128,896]{1,0:T(8,128)(2,1)S(1)}, bf16[128,896]{1,0:T(8,128)(2,1)S(1)}, u32[]{:S(2)}, u32[]{:S(2)}) %collective-permute-start.40) | collective-permute-done | bytes 229408 | tf_op jit(solution)/shard_map/ppermute | solution.py:527
  116.8 1.6 collective-permute-start.41
  118.7 1.6 collective-permute-start.46
  120.3 2.8 %collective-permute-done.30 = bf16[128,896]{1,0:T(8,128)(2,1)S(1)} collective-permute-done((bf16[128,896]{1,0:T(8,128)(2,1)S(1)}, bf16[128,896]{1,0:T(8,128)(2,1)S(1)}, u32[]{:S(2)}, u32[]{:S(2)}) %collective-permute-start.30) | collective-permute-done | bytes 229408 | tf_op jit(solution)/shard_map/ppermute | solution.py:24
  123.2 1.9 collective-permute-done.41
  125.1 1.5 collective-permute-start.31
  126.7 1.2 collective-permute-start.42
  127.9 7.9 %shard_map.112 = (f32[512,1024]{1,0:T(8,128)S(1)}, f32[512,1024]{1,0:T(8,128)S(1)}) custom-call(s32[2]{0:T(128)S(1)} %get-tuple-element.44.place_ref, bf16[2,128,896]{2,1,0:T(8,128)(2,1)S(1)} %pad_maximum_fusion.1.refs_0_, bf16[2,128,896]{2,1,0:T(8,128)(2,1)S(1)} %collective-permute-done.33.refs_1_, ...), custom_call_target="tpu_custom_call" | custom-call | flops 3758096384 | bytes 7340032 | tf_op jit(solution)/shard_map/pallas_call | solution.py:382
  136.3 1.2 collective-permute-done.42.refs_5_
  137.6 4.9 %collective-permute-done.31.refs_1_ = bf16[2,128,896]{2,1,0:T(8,128)(2,1)S(1)} collective-permute-done((bf16[2,128,896]{2,1,0:T(8,128)(2,1)S(1)}, bf16[2,128,896]{2,1,0:T(8,128)(2,1)S(1)}, u32[]{:S(2)}, u32[]{:S(2)}) %collective-permute-start.31) | collective-permute-done | bytes 458784 | tf_op jit(solution)/shard_map/ppermute | solution.py:24
  143.0 8.2 %shard_map.113 = (f32[512,1024]{1,0:T(8,128)S(1)}, f32[512,1024]{1,0:T(8,128)S(1)}) custom-call(s32[2]{0:T(128)S(1)} %get-tuple-element.50.place_ref, bf16[2,128,896]{2,1,0:T(8,128)(2,1)S(1)} %pad_maximum_fusion.3.refs_0_, bf16[2,128,896]{2,1,0:T(8,128)(2,1)S(1)} %collective-permute-done.46.refs_1_, ...), custom_call_target="tpu_custom_call" | custom-call | flops 3758096384 | bytes 7340032 | tf_op jit(solution)/shard_map/pallas_call | solution.py:382
  151.3 16.4 %shard_map.114 = (bf16[512,1024]{1,0:T(8,128)(2,1)S(1)}, bf16[2,256,1792]{2,1,0:T(8,128)(2,1)S(1)}) custom-call(s32[5]{0:T(128)S(1)} %stack.179.place_ref, bf16[2,128,896]{2,1,0:T(8,128)(2,1)S(1)} %pad_maximum_fusion.refs_0_, bf16[2,128,896]{2,1,0:T(8,128)(2,1)S(1)} %collective-permute-done.31.refs_1_, ...), custom_call_target="tpu_custom_call" | custom-call | flops 7516192768 | bytes 14680064 | tf_op jit(solution)/shard_map/pallas_call | solution.py:382
  167.9 11.4 %shard_map.116 = (bf16[2,256,1792]{2,1,0:T(8,128)(2,1)S(1)}, bf16[2,256,1792]{2,1,0:T(8,128)(2,1)S(1)}) custom-call(s32[2]{0:T(128)S(1)} %get-tuple-element.59.place_ref, bf16[512,1024]{1,0:T(8,128)(2,1)S(1)} %get-tuple-element.55.hidden_ref, bf16[1024,7168]{1,0:T(8,128)(2,1)} %bitcast.98), custom_call_target="tpu_custom_call" | custom-call | flops 3758096384 | bytes 7340032 | tf_op jit(solution)/shard_map/pallas_call | solution.py:331
  179.8 7.0 %shard_map.115 = bf16[2,256,1792]{2,1,0:T(8,128)(2,1)S(1)} custom-call(s32[2]{0:T(128)S(1)} %get-tuple-element.42.place_ref, bf16[512,1024]{1,0:T(8,128)(2,1)S(1)} %get-tuple-element.55.hidden_ref, bf16[1024,7168]{1,0:T(8,128)(2,1)} %bitcast.99), custom_call_target="tpu_custom_call" | custom-call | flops 1879048192 | bytes 7340032 | tf_op jit(solution)/shard_map/pallas_call | solution.py:331
  187.3 1.6 collective-permute-start.50
  189.2 1.2 collective-permute-start.53
  190.4 9.5 %collective-permute-done.50 = bf16[128,1792]{1,0:T(8,128)(2,1)S(1)} collective-permute-done((bf16[128,1792]{1,0:T(8,128)(2,1)S(1)}, bf16[128,1792]{1,0:T(8,128)(2,1)S(1)}, u32[]{:S(2)}, u32[]{:S(2)}) %collective-permute-start.50) | collective-permute-done | bytes 458784 | tf_op jit(solution)/shard_map/ppermute | solution.py:24
  200.5 1.6 collective-permute-start.60
  202.2 1.2 collective-permute-start.51
  204.5 1.0 collective-permute-start.57
  205.4 5.4 %collective-permute-done.51 = bf16[128,896]{1,0:T(8,128)(2,1)S(1)} collective-permute-done((bf16[128,896]{1,0:T(8,128)(2,1)S(1)}, bf16[128,896]{1,0:T(8,128)(2,1)S(1)}, u32[]{:S(2)}, u32[]{:S(2)}) %collective-permute-start.51) | collective-permute-done | bytes 229408 | tf_op jit(solution)/shard_map/ppermute | solution.py:24
  211.0 6.0 %collective-permute-done.54 = bf16[128,896]{1,0:T(8,128)(2,1)S(1)} collective-permute-done((bf16[128,896]{1,0:T(8,128)(2,1)S(1)}, bf16[128,896]{1,0:T(8,128)(2,1)S(1)}, u32[]{:S(2)}, u32[]{:S(2)}) %collective-permute-start.54) | collective-permute-done | bytes 229408 | tf_op jit(solution)/shard_map/ppermute | solution.py:24
  219.9 1.2 collective-permute-start.61
  221.0 3.9 %collective-permute-done.58 = bf16[128,896]{1,0:T(8,128)(2,1)S(1)} collective-permute-done((bf16[128,896]{1,0:T(8,128)(2,1)S(1)}, bf16[128,896]{1,0:T(8,128)(2,1)S(1)}, u32[]{:S(2)}, u32[]{:S(2)}) %collective-permute-start.58) | collective-permute-done | bytes 229408 | tf_op jit(solution)/shard_map/ppermute | solution.py:24
  224.9 2.6 %collective-permute-start.59 = (bf16[128,896]{1,0:T(8,128)(2,1)S(1)}, bf16[128,896]{1,0:T(8,128)(2,1)S(1)}, u32[]{:S(2)}, u32[]{:S(2)}) collective-permute-start(bf16[128,896]{1,0:T(8,128)(2,1)S(1)} %fusion.10), channel_id=1, source_target_pairs={{0,12},{4,0},{8,4},{12,8},{1,13},{5,1},{9,5},{13,9},{2,14},{6,2},{... | collective-permute-start | bytes 688136 | tf_op jit(solution)/shard_map/ppermute | solution.py:29
  227.5 3.5 %collective-permute-done.59 = bf16[128,896]{1,0:T(8,128)(2,1)S(1)} collective-permute-done((bf16[128,896]{1,0:T(8,128)(2,1)S(1)}, bf16[128,896]{1,0:T(8,128)(2,1)S(1)}, u32[]{:S(2)}, u32[]{:S(2)}) %collective-permute-start.59) | collective-permute-done | bytes 229408 | tf_op jit(solution)/shard_map/ppermute | solution.py:29
  231.4 1.3 collective-permute-done.62
  (128 shorter events, 20.7 us)
Async XLA Ops:
  0.0 37.1 %collective-permute-start.3 = (bf16[448,8192]{1,0:T(8,128)(2,1)}, bf16[448,8192]{1,0:T(8,128)(2,1)}, u32[]{:S(2)}, u32[]{:S(2)}) collective-permute-start(bf16[448,8192]{1,0:T(8,128)(2,1)} %bitcast.106), channel_id=1, source_target_pairs={{0,1},{1,0},{2,3},{3,2},{4,5},{5,4},{6,7},{7,6},{8,9},{9,8},{10,11... | collective-permute-start | bytes 22020104 | tf_op jit(solution)/shard_map/ppermute | solution.py:24
  9.9 7.9 %copy-start.3 = (f32[512,8]{0,1:T(8,128)S(1)}, f32[512,8]{0,1:T(8,128)}, u32[]{:S(2)}) copy-start(f32[512,8]{0,1:T(8,128)} %param.21) | copy-start | bytes 49156
  10.0 13.9 %collective-permute-start.1 = (bf16[32,4096]{1,0:T(8,128)(2,1)S(1)}, bf16[32,4096]{1,0:T(8,128)(2,1)S(1)}, u32[]{:S(2)}, u32[]{:S(2)}) collective-permute-start(bf16[32,4096]{1,0:T(8,128)(2,1)S(1)} %get-tuple-element.63.refs_0_), channel_id=1, source_target_pairs={{0,4},{4,8},{8,12},{1,5},{5,9},{9,13},{2,6},{6,10},{10,14},{3,7},{... | collective-permute-start | bytes 786440 | tf_op jit(solution)/shard_map/ppermute | solution.py:496
  14.5 10.7 %collective-permute-start.4 = (bf16[32,4096]{1,0:T(8,128)(2,1)S(1)}, bf16[32,4096]{1,0:T(8,128)(2,1)S(1)}, u32[]{:S(2)}, u32[]{:S(2)}) collective-permute-start(bf16[32,4096]{1,0:T(8,128)(2,1)S(1)} %get-tuple-element.63.refs_0_), channel_id=1, source_target_pairs={{4,0},{8,4},{12,8},{5,1},{9,5},{13,9},{6,2},{10,6},{14,10},{7,3},{... | collective-permute-start | bytes 786440 | tf_op jit(solution)/shard_map/ppermute | solution.py:497
  15.8 10.1 %collective-permute-start.8 = (bf16[32,4096]{1,0:T(8,128)(2,1)S(1)}, bf16[32,4096]{1,0:T(8,128)(2,1)S(1)}, u32[]{:S(2)}, u32[]{:S(2)}) collective-permute-start(bf16[32,4096]{1,0:T(8,128)(2,1)S(1)} %get-tuple-element.63.refs_0_), channel_id=1, source_target_pairs={{0,2},{2,0},{4,6},{6,4},{8,10},{10,8},{12,14},{14,12},{1,3},{3,1},... | collective-permute-start | bytes 786440 | tf_op jit(solution)/shard_map/ppermute | solution.py:500
  17.7 1.4 collective-permute-start
  19.4 10.4 %collective-permute-start.15 = (bf16[32,4096]{1,0:T(8,128)(2,1)S(1)}, bf16[32,4096]{1,0:T(8,128)(2,1)S(1)}, u32[]{:S(2)}, u32[]{:S(2)}) collective-permute-start(bf16[32,4096]{1,0:T(8,128)(2,1)S(1)} %get-tuple-element.39.refs_1_), channel_id=1, source_target_pairs={{0,4},{4,8},{8,12},{1,5},{5,9},{9,13},{2,6},{6,10},{10,14},{3,7},{... | collective-permute-start | bytes 786440 | tf_op jit(solution)/shard_map/ppermute | solution.py:496
  24.0 10.0 %collective-permute-start.16 = (bf16[32,4096]{1,0:T(8,128)(2,1)S(1)}, bf16[32,4096]{1,0:T(8,128)(2,1)S(1)}, u32[]{:S(2)}, u32[]{:S(2)}) collective-permute-start(bf16[32,4096]{1,0:T(8,128)(2,1)S(1)} %get-tuple-element.39.refs_1_), channel_id=1, source_target_pairs={{4,0},{8,4},{12,8},{5,1},{9,5},{13,9},{6,2},{10,6},{14,10},{7,3},{... | collective-permute-start | bytes 786440 | tf_op jit(solution)/shard_map/ppermute | solution.py:497
  25.3 11.1 %collective-permute-start.2 = (bf16[32,4096]{1,0:T(8,128)(2,1)S(1)}, bf16[32,4096]{1,0:T(8,128)(2,1)S(1)}, u32[]{:S(2)}, u32[]{:S(2)}) collective-permute-start(bf16[32,4096]{1,0:T(8,128)(2,1)S(1)} %collective-permute-done.1.refs_1_), channel_id=1, source_target_pairs={{4,8},{8,12},{5,9},{9,13},{6,10},{10,14},{7,11},{11,15},{20,24},{2... | collective-permute-start | bytes 786440 | tf_op jit(solution)/shard_map/ppermute | solution.py:496
  26.0 11.8 %collective-permute-start.21 = (bf16[32,4096]{1,0:T(8,128)(2,1)S(1)}, bf16[32,4096]{1,0:T(8,128)(2,1)S(1)}, u32[]{:S(2)}, u32[]{:S(2)}) collective-permute-start(bf16[32,4096]{1,0:T(8,128)(2,1)S(1)} %get-tuple-element.39.refs_1_), channel_id=1, source_target_pairs={{0,2},{2,0},{4,6},{6,4},{8,10},{10,8},{12,14},{14,12},{1,3},{3,1},... | collective-permute-start | bytes 786440 | tf_op jit(solution)/shard_map/ppermute | solution.py:500
  29.8 10.2 %collective-permute-start.5 = (bf16[32,4096]{1,0:T(8,128)(2,1)S(1)}, bf16[32,4096]{1,0:T(8,128)(2,1)S(1)}, u32[]{:S(2)}, u32[]{:S(2)}) collective-permute-start(bf16[32,4096]{1,0:T(8,128)(2,1)S(1)} %collective-permute-done.4.refs_2_), channel_id=1, source_target_pairs={{4,0},{8,4},{5,1},{9,5},{6,2},{10,6},{7,3},{11,7},{20,16},{24,20},... | collective-permute-start | bytes 786440 | tf_op jit(solution)/shard_map/ppermute | solution.py:497
  33.9 9.1 %collective-permute-start.10 = (bf16[32,4096]{1,0:T(8,128)(2,1)S(1)}, bf16[32,4096]{1,0:T(8,128)(2,1)S(1)}, u32[]{:S(2)}, u32[]{:S(2)}) collective-permute-start(bf16[32,4096]{1,0:T(8,128)(2,1)S(1)} %collective-permute-done.4.refs_2_), channel_id=1, source_target_pairs={{0,2},{2,0},{4,6},{6,4},{8,10},{10,8},{1,3},{3,1},{5,7},{7,5},{9,1... | collective-permute-start | bytes 786440 | tf_op jit(solution)/shard_map/ppermute | solution.py:500
  36.4 8.0 %collective-permute-start.9 = (bf16[32,4096]{1,0:T(8,128)(2,1)S(1)}, bf16[32,4096]{1,0:T(8,128)(2,1)S(1)}, u32[]{:S(2)}, u32[]{:S(2)}) collective-permute-start(bf16[32,4096]{1,0:T(8,128)(2,1)S(1)} %collective-permute-done.1.refs_1_), channel_id=1, source_target_pairs={{4,6},{6,4},{8,10},{10,8},{12,14},{14,12},{5,7},{7,5},{9,11},{11,9... | collective-permute-start | bytes 786440 | tf_op jit(solution)/shard_map/ppermute | solution.py:500
  37.1 9.7 %collective-permute-start.17 = (bf16[32,4096]{1,0:T(8,128)(2,1)S(1)}, bf16[32,4096]{1,0:T(8,128)(2,1)S(1)}, u32[]{:S(2)}, u32[]{:S(2)}) collective-permute-start(bf16[32,4096]{1,0:T(8,128)(2,1)S(1)} %collective-permute-done.15.refs_2_), channel_id=1, source_target_pairs={{4,8},{8,12},{5,9},{9,13},{6,10},{10,14},{7,11},{11,15},{20,24},{2... | collective-permute-start | bytes 786440 | tf_op jit(solution)/shard_map/ppermute | solution.py:496
  37.8 15.6 %collective-permute-start.18 = (bf16[32,4096]{1,0:T(8,128)(2,1)S(1)}, bf16[32,4096]{1,0:T(8,128)(2,1)S(1)}, u32[]{:S(2)}, u32[]{:S(2)}) collective-permute-start(bf16[32,4096]{1,0:T(8,128)(2,1)S(1)} %collective-permute-done.16.refs_3_), channel_id=1, source_target_pairs={{4,0},{8,4},{5,1},{9,5},{6,2},{10,6},{7,3},{11,7},{20,16},{24,20},... | collective-permute-start | bytes 786440 | tf_op jit(solution)/shard_map/ppermute | solution.py:497
  40.0 14.1 %collective-permute-start.22 = (bf16[32,4096]{1,0:T(8,128)(2,1)S(1)}, bf16[32,4096]{1,0:T(8,128)(2,1)S(1)}, u32[]{:S(2)}, u32[]{:S(2)}) collective-permute-start(bf16[32,4096]{1,0:T(8,128)(2,1)S(1)} %collective-permute-done.15.refs_2_), channel_id=1, source_target_pairs={{4,6},{6,4},{8,10},{10,8},{12,14},{14,12},{5,7},{7,5},{9,11},{11,9... | collective-permute-start | bytes 786440 | tf_op jit(solution)/shard_map/ppermute | solution.py:500
  43.0 15.0 %collective-permute-start.7 = (bf16[32,4096]{1,0:T(8,128)(2,1)S(1)}, bf16[32,4096]{1,0:T(8,128)(2,1)S(1)}, u32[]{:S(2)}, u32[]{:S(2)}) collective-permute-start(bf16[32,4096]{1,0:T(8,128)(2,1)S(1)} %collective-permute-done.5.refs_4_), channel_id=1, source_target_pairs={{4,0},{5,1},{6,2},{7,3},{20,16},{21,17},{22,18},{23,19}} | collective-permute-start | bytes 786440 | tf_op jit(solution)/shard_map/ppermute | solution.py:497
  44.3 16.5 %collective-permute-start.12 = (bf16[32,4096]{1,0:T(8,128)(2,1)S(1)}, bf16[32,4096]{1,0:T(8,128)(2,1)S(1)}, u32[]{:S(2)}, u32[]{:S(2)}) collective-permute-start(bf16[32,4096]{1,0:T(8,128)(2,1)S(1)} %collective-permute-done.5.refs_4_), channel_id=1, source_target_pairs={{0,2},{2,0},{4,6},{6,4},{1,3},{3,1},{5,7},{7,5},{16,18},{18,16},{2... | collective-permute-start | bytes 786440 | tf_op jit(solution)/shard_map/ppermute | solution.py:500
  46.8 14.8 %collective-permute-start.6 = (bf16[32,4096]{1,0:T(8,128)(2,1)S(1)}, bf16[32,4096]{1,0:T(8,128)(2,1)S(1)}, u32[]{:S(2)}, u32[]{:S(2)}) collective-permute-start(bf16[32,4096]{1,0:T(8,128)(2,1)S(1)} %collective-permute-done.2.refs_3_), channel_id=1, source_target_pairs={{8,12},{9,13},{10,14},{11,15},{24,28},{25,29},{26,30},{27,31}} | collective-permute-start | bytes 786440 | tf_op jit(solution)/shard_map/ppermute | solution.py:496
  53.3 8.9 %collective-permute-start.19 = (bf16[32,4096]{1,0:T(8,128)(2,1)S(1)}, bf16[32,4096]{1,0:T(8,128)(2,1)S(1)}, u32[]{:S(2)}, u32[]{:S(2)}) collective-permute-start(bf16[32,4096]{1,0:T(8,128)(2,1)S(1)} %collective-permute-done.17.refs_4_), channel_id=1, source_target_pairs={{8,12},{9,13},{10,14},{11,15},{24,28},{25,29},{26,30},{27,31}} | collective-permute-start | bytes 786440 | tf_op jit(solution)/shard_map/ppermute | solution.py:496
  54.0 11.3 %collective-permute-start.20 = (bf16[32,4096]{1,0:T(8,128)(2,1)S(1)}, bf16[32,4096]{1,0:T(8,128)(2,1)S(1)}, u32[]{:S(2)}, u32[]{:S(2)}) collective-permute-start(bf16[32,4096]{1,0:T(8,128)(2,1)S(1)} %collective-permute-done.18.refs_5_), channel_id=1, source_target_pairs={{4,0},{5,1},{6,2},{7,3},{20,16},{21,17},{22,18},{23,19}} | collective-permute-start | bytes 786440 | tf_op jit(solution)/shard_map/ppermute | solution.py:497
  58.1 10.8 %collective-permute-start.14 = (bf16[32,4096]{1,0:T(8,128)(2,1)S(1)}, bf16[32,4096]{1,0:T(8,128)(2,1)S(1)}, u32[]{:S(2)}, u32[]{:S(2)}) collective-permute-start(bf16[32,4096]{1,0:T(8,128)(2,1)S(1)} %collective-permute-done.7.refs_6_), channel_id=1, source_target_pairs={{0,2},{2,0},{1,3},{3,1},{16,18},{18,16},{17,19},{19,17}} | collective-permute-start | bytes 786440 | tf_op jit(solution)/shard_map/ppermute | solution.py:500
  60.9 10.8 %collective-permute-start.11 = (bf16[32,4096]{1,0:T(8,128)(2,1)S(1)}, bf16[32,4096]{1,0:T(8,128)(2,1)S(1)}, u32[]{:S(2)}, u32[]{:S(2)}) collective-permute-start(bf16[32,4096]{1,0:T(8,128)(2,1)S(1)} %collective-permute-done.2.refs_3_), channel_id=1, source_target_pairs={{8,10},{10,8},{12,14},{14,12},{9,11},{11,9},{13,15},{15,13},{24,26... | collective-permute-start | bytes 786440 | tf_op jit(solution)/shard_map/ppermute | solution.py:500
  61.6 10.8 %collective-permute-start.13 = (bf16[32,4096]{1,0:T(8,128)(2,1)S(1)}, bf16[32,4096]{1,0:T(8,128)(2,1)S(1)}, u32[]{:S(2)}, u32[]{:S(2)}) collective-permute-start(bf16[32,4096]{1,0:T(8,128)(2,1)S(1)} %collective-permute-done.6.refs_5_), channel_id=1, source_target_pairs={{12,14},{14,12},{13,15},{15,13},{28,30},{30,28},{29,31},{31,29}} | collective-permute-start | bytes 786440 | tf_op jit(solution)/shard_map/ppermute | solution.py:500
  62.3 18.7 %collective-permute-start.23 = (bf16[32,4096]{1,0:T(8,128)(2,1)S(1)}, bf16[32,4096]{1,0:T(8,128)(2,1)S(1)}, u32[]{:S(2)}, u32[]{:S(2)}) collective-permute-start(bf16[32,4096]{1,0:T(8,128)(2,1)S(1)} %collective-permute-done.16.refs_3_), channel_id=1, source_target_pairs={{0,2},{2,0},{4,6},{6,4},{8,10},{10,8},{1,3},{3,1},{5,7},{7,5},{9,1... | collective-permute-start | bytes 786440 | tf_op jit(solution)/shard_map/ppermute | solution.py:500
  65.3 15.7 %collective-permute-start.24 = (bf16[32,4096]{1,0:T(8,128)(2,1)S(1)}, bf16[32,4096]{1,0:T(8,128)(2,1)S(1)}, u32[]{:S(2)}, u32[]{:S(2)}) collective-permute-start(bf16[32,4096]{1,0:T(8,128)(2,1)S(1)} %collective-permute-done.17.refs_4_), channel_id=1, source_target_pairs={{8,10},{10,8},{12,14},{14,12},{9,11},{11,9},{13,15},{15,13},{24,26... | collective-permute-start | bytes 786440 | tf_op jit(solution)/shard_map/ppermute | solution.py:500
  68.9 12.1 %collective-permute-start.25 = (bf16[32,4096]{1,0:T(8,128)(2,1)S(1)}, bf16[32,4096]{1,0:T(8,128)(2,1)S(1)}, u32[]{:S(2)}, u32[]{:S(2)}) collective-permute-start(bf16[32,4096]{1,0:T(8,128)(2,1)S(1)} %collective-permute-done.18.refs_5_), channel_id=1, source_target_pairs={{0,2},{2,0},{4,6},{6,4},{1,3},{3,1},{5,7},{7,5},{16,18},{18,16},{2... | collective-permute-start | bytes 786440 | tf_op jit(solution)/shard_map/ppermute | solution.py:500
  71.7 9.3 %collective-permute-start.26 = (bf16[32,4096]{1,0:T(8,128)(2,1)S(1)}, bf16[32,4096]{1,0:T(8,128)(2,1)S(1)}, u32[]{:S(2)}, u32[]{:S(2)}) collective-permute-start(bf16[32,4096]{1,0:T(8,128)(2,1)S(1)} %collective-permute-done.19.refs_6_), channel_id=1, source_target_pairs={{12,14},{14,12},{13,15},{15,13},{28,30},{30,28},{29,31},{31,29}} | collective-permute-start | bytes 786440 | tf_op jit(solution)/shard_map/ppermute | solution.py:500
  72.4 10.8 %collective-permute-start.27 = (bf16[32,4096]{1,0:T(8,128)(2,1)S(1)}, bf16[32,4096]{1,0:T(8,128)(2,1)S(1)}, u32[]{:S(2)}, u32[]{:S(2)}) collective-permute-start(bf16[32,4096]{1,0:T(8,128)(2,1)S(1)} %collective-permute-done.20.refs_7_), channel_id=1, source_target_pairs={{0,2},{2,0},{1,3},{3,1},{16,18},{18,16},{17,19},{19,17}} | collective-permute-start | bytes 786440 | tf_op jit(solution)/shard_map/ppermute | solution.py:500
  88.8 6.9 %collective-permute-start.28 = (bf16[128,896]{1,0:T(8,128)(2,1)S(1)}, bf16[128,896]{1,0:T(8,128)(2,1)S(1)}, u32[]{:S(2)}, u32[]{:S(2)}) collective-permute-start(bf16[128,896]{1,0:T(8,128)(2,1)S(1)} %dynamic-slice_bitcast_fusion), channel_id=1, source_target_pairs={{0,16},{16,0},{1,17},{17,1},{2,18},{18,2},{3,19},{19,3},{4,20},{20... | collective-permute-start | bytes 688136 | tf_op jit(solution)/shard_map/ppermute | solution.py:24
  95.7 6.1 %collective-permute-start.32 = (bf16[128,896]{1,0:T(8,128)(2,1)S(1)}, bf16[128,896]{1,0:T(8,128)(2,1)S(1)}, u32[]{:S(2)}, u32[]{:S(2)}) collective-permute-start(bf16[128,896]{1,0:T(8,128)(2,1)S(1)} %fusion.13), channel_id=1, source_target_pairs={{0,16},{16,0},{1,17},{17,1},{2,18},{18,2},{3,19},{19,3},{4,20},{20... | collective-permute-start | bytes 688136 | tf_op jit(solution)/shard_map/ppermute | solution.py:24
  97.3 7.9 %collective-permute-start.29 = (bf16[128,896]{1,0:T(8,128)(2,1)S(1)}, bf16[128,896]{1,0:T(8,128)(2,1)S(1)}, u32[]{:S(2)}, u32[]{:S(2)}) collective-permute-start(bf16[128,896]{1,0:T(8,128)(2,1)S(1)} %fusion.13), channel_id=1, source_target_pairs={{0,4},{4,8},{8,12},{12,0},{1,5},{5,9},{9,13},{13,1},{2,6},{6,10},{... | collective-permute-start | bytes 688136 | tf_op jit(solution)/shard_map/ppermute | solution.py:29
  101.9 10.4 %collective-permute-start.33 = (bf16[2,128,896]{2,1,0:T(8,128)(2,1)S(1)}, bf16[2,128,896]{2,1,0:T(8,128)(2,1)S(1)}, u32[]{:S(2)}, u32[]{:S(2)}) collective-permute-start(bf16[2,128,896]{2,1,0:T(8,128)(2,1)S(1)} %pad_maximum_fusion.1.refs_0_), channel_id=1, source_target_pairs={{0,2},{2,0},{1,3},{3,1},{4,6},{6,4},{5,7},{7,5},{8,10},{10,8},{9,1... | collective-permute-start | bytes 1376264 | tf_op jit(solution)/shard_map/ppermute | solution.py:24
  102.8 6.0 %collective-permute-start.39 = (bf16[128,896]{1,0:T(8,128)(2,1)S(1)}, bf16[128,896]{1,0:T(8,128)(2,1)S(1)}, u32[]{:S(2)}, u32[]{:S(2)}) collective-permute-start(bf16[128,896]{1,0:T(8,128)(2,1)S(1)} %fusion.13), channel_id=1, source_target_pairs={{0,12},{4,0},{8,4},{12,8},{1,13},{5,1},{9,5},{13,9},{2,14},{6,2},{... | collective-permute-start | bytes 688136 | tf_op jit(solution)/shard_map/ppermute | solution.py:29
  105.2 6.2 %collective-permute-start.38 = (bf16[128,896]{1,0:T(8,128)(2,1)S(1)}, bf16[128,896]{1,0:T(8,128)(2,1)S(1)}, u32[]{:S(2)}, u32[]{:S(2)}) collective-permute-start(bf16[128,896]{1,0:T(8,128)(2,1)S(1)} %collective-permute-done.29), channel_id=1, source_target_pairs={{4,8},{8,12},{5,9},{9,13},{6,10},{10,14},{7,11},{11,15},{20,24},{2... | collective-permute-start | bytes 688136 | tf_op jit(solution)/shard_map/ppermute | solution.py:526
  108.8 7.9 %collective-permute-start.40 = (bf16[128,896]{1,0:T(8,128)(2,1)S(1)}, bf16[128,896]{1,0:T(8,128)(2,1)S(1)}, u32[]{:S(2)}, u32[]{:S(2)}) collective-permute-start(bf16[128,896]{1,0:T(8,128)(2,1)S(1)} %collective-permute-done.39), channel_id=1, source_target_pairs={{4,0},{8,4},{5,1},{9,5},{6,2},{10,6},{7,3},{11,7},{20,16},{24,20},... | collective-permute-start | bytes 688136 | tf_op jit(solution)/shard_map/ppermute | solution.py:527
  110.1 16.6 %collective-permute-start.34 = (bf16[2,128,896]{2,1,0:T(8,128)(2,1)S(1)}, bf16[2,128,896]{2,1,0:T(8,128)(2,1)S(1)}, u32[]{:S(2)}, u32[]{:S(2)}) collective-permute-start(bf16[2,128,896]{2,1,0:T(8,128)(2,1)S(1)} %pad_maximum_fusion.1.refs_0_), channel_id=1, source_target_pairs={{0,1},{1,0},{2,3},{3,2},{4,5},{5,4},{6,7},{7,6},{8,9},{9,8},{10,11... | collective-permute-start | bytes 1376264 | tf_op jit(solution)/shard_map/ppermute | solution.py:24
  110.2 8.5 %collective-permute-start.45 = (bf16[128,896]{1,0:T(8,128)(2,1)S(1)}, bf16[128,896]{1,0:T(8,128)(2,1)S(1)}, u32[]{:S(2)}, u32[]{:S(2)}) collective-permute-start(bf16[128,896]{1,0:T(8,128)(2,1)S(1)} %collective-permute-done.39), channel_id=1, source_target_pairs={{0,2},{2,0},{1,3},{3,1},{4,6},{6,4},{5,7},{7,5},{8,10},{10,8},{9,1... | collective-permute-start | bytes 688136 | tf_op jit(solution)/shard_map/ppermute | solution.py:24
  111.4 11.7 %collective-permute-start.30 = (bf16[128,896]{1,0:T(8,128)(2,1)S(1)}, bf16[128,896]{1,0:T(8,128)(2,1)S(1)}, u32[]{:S(2)}, u32[]{:S(2)}) collective-permute-start(bf16[128,896]{1,0:T(8,128)(2,1)S(1)} %collective-permute-done.29), channel_id=1, source_target_pairs={{0,2},{2,0},{1,3},{3,1},{4,6},{6,4},{5,7},{7,5},{8,10},{10,8},{9,1... | collective-permute-start | bytes 688136 | tf_op jit(solution)/shard_map/ppermute | solution.py:24
  112.3 15.6 %collective-permute-start.35 = (bf16[2,128,896]{2,1,0:T(8,128)(2,1)S(1)}, bf16[2,128,896]{2,1,0:T(8,128)(2,1)S(1)}, u32[]{:S(2)}, u32[]{:S(2)}) collective-permute-start(bf16[2,128,896]{2,1,0:T(8,128)(2,1)S(1)} %collective-permute-done.33.refs_1_), channel_id=1, source_target_pairs={{0,1},{1,0},{2,3},{3,2},{4,5},{5,4},{6,7},{7,6},{8,9},{9,8},{10,11... | collective-permute-start | bytes 1376264 | tf_op jit(solution)/shard_map/ppermute | solution.py:24
  116.8 8.3 %collective-permute-start.41 = (bf16[128,896]{1,0:T(8,128)(2,1)S(1)}, bf16[128,896]{1,0:T(8,128)(2,1)S(1)}, u32[]{:S(2)}, u32[]{:S(2)}) collective-permute-start(bf16[128,896]{1,0:T(8,128)(2,1)S(1)} %broadcast_select_fusion), channel_id=1, source_target_pairs={{0,16},{16,0},{1,17},{17,1},{2,18},{18,2},{3,19},{19,3},{4,20},{20... | collective-permute-start | bytes 688136 | tf_op jit(solution)/shard_map/ppermute | solution.py:24
  118.7 17.0 %collective-permute-start.46 = (bf16[2,128,896]{2,1,0:T(8,128)(2,1)S(1)}, bf16[2,128,896]{2,1,0:T(8,128)(2,1)S(1)}, u32[]{:S(2)}, u32[]{:S(2)}) collective-permute-start(bf16[2,128,896]{2,1,0:T(8,128)(2,1)S(1)} %pad_maximum_fusion.3.refs_0_), channel_id=1, source_target_pairs={{0,16},{16,0},{1,17},{17,1},{2,18},{18,2},{3,19},{19,3},{4,20},{20... | collective-permute-start | bytes 1376264 | tf_op jit(solution)/shard_map/ppermute | solution.py:24
  123.1 19.4 %collective-permute-start.47 = (bf16[2,128,896]{2,1,0:T(8,128)(2,1)S(1)}, bf16[2,128,896]{2,1,0:T(8,128)(2,1)S(1)}, u32[]{:S(2)}, u32[]{:S(2)}) collective-permute-start(bf16[2,128,896]{2,1,0:T(8,128)(2,1)S(1)} %pad_maximum_fusion.3.refs_0_), channel_id=1, source_target_pairs={{0,1},{1,0},{2,3},{3,2},{4,5},{5,4},{6,7},{7,6},{8,9},{9,8},{10,11... | collective-permute-start | bytes 1376264 | tf_op jit(solution)/shard_map/ppermute | solution.py:24
  125.1 17.4 %collective-permute-start.31 = (bf16[2,128,896]{2,1,0:T(8,128)(2,1)S(1)}, bf16[2,128,896]{2,1,0:T(8,128)(2,1)S(1)}, u32[]{:S(2)}, u32[]{:S(2)}) collective-permute-start(bf16[2,128,896]{2,1,0:T(8,128)(2,1)S(1)} %pad_maximum_fusion.refs_0_), channel_id=1, source_target_pairs={{0,16},{16,0},{1,17},{17,1},{2,18},{18,2},{3,19},{19,3},{4,20},{20... | collective-permute-start | bytes 1376264 | tf_op jit(solution)/shard_map/ppermute | solution.py:24
  126.7 10.9 %collective-permute-start.42 = (bf16[2,128,896]{2,1,0:T(8,128)(2,1)S(1)}, bf16[2,128,896]{2,1,0:T(8,128)(2,1)S(1)}, u32[]{:S(2)}, u32[]{:S(2)}) collective-permute-start(bf16[2,128,896]{2,1,0:T(8,128)(2,1)S(1)} %pad_maximum_fusion.2.refs_4_), channel_id=1, source_target_pairs={{0,2},{2,0},{1,3},{3,1},{4,6},{6,4},{5,7},{7,5},{8,10},{10,8},{9,1... | collective-permute-start | bytes 1376264 | tf_op jit(solution)/shard_map/ppermute | solution.py:24
  135.8 7.3 %collective-permute-start.48 = (bf16[2,128,896]{2,1,0:T(8,128)(2,1)S(1)}, bf16[2,128,896]{2,1,0:T(8,128)(2,1)S(1)}, u32[]{:S(2)}, u32[]{:S(2)}) collective-permute-start(bf16[2,128,896]{2,1,0:T(8,128)(2,1)S(1)} %collective-permute-done.46.refs_1_), channel_id=1, source_target_pairs={{0,1},{1,0},{2,3},{3,2},{4,5},{5,4},{6,7},{7,6},{8,9},{9,8},{10,11... | collective-permute-start | bytes 1376264 | tf_op jit(solution)/shard_map/ppermute | solution.py:24
  135.8 15.5 %collective-permute-start.36 = (bf16[2,128,896]{2,1,0:T(8,128)(2,1)S(1)}, bf16[2,128,896]{2,1,0:T(8,128)(2,1)S(1)}, u32[]{:S(2)}, u32[]{:S(2)}) collective-permute-start(bf16[2,128,896]{2,1,0:T(8,128)(2,1)S(1)} %pad_maximum_fusion.refs_0_), channel_id=1, source_target_pairs={{0,1},{1,0},{2,3},{3,2},{4,5},{5,4},{6,7},{7,6},{8,9},{9,8},{10,11... | collective-permute-start | bytes 1376264 | tf_op jit(solution)/shard_map/ppermute | solution.py:24
  137.6 13.7 %collective-permute-start.43 = (bf16[2,128,896]{2,1,0:T(8,128)(2,1)S(1)}, bf16[2,128,896]{2,1,0:T(8,128)(2,1)S(1)}, u32[]{:S(2)}, u32[]{:S(2)}) collective-permute-start(bf16[2,128,896]{2,1,0:T(8,128)(2,1)S(1)} %pad_maximum_fusion.2.refs_4_), channel_id=1, source_target_pairs={{0,1},{1,0},{2,3},{3,2},{4,5},{5,4},{6,7},{7,6},{8,9},{9,8},{10,11... | collective-permute-start | bytes 1376264 | tf_op jit(solution)/shard_map/ppermute | solution.py:24
  142.5 8.8 %collective-permute-start.44 = (bf16[2,128,896]{2,1,0:T(8,128)(2,1)S(1)}, bf16[2,128,896]{2,1,0:T(8,128)(2,1)S(1)}, u32[]{:S(2)}, u32[]{:S(2)}) collective-permute-start(bf16[2,128,896]{2,1,0:T(8,128)(2,1)S(1)} %collective-permute-done.42.refs_5_), channel_id=1, source_target_pairs={{0,1},{1,0},{2,3},{3,2},{4,5},{5,4},{6,7},{7,6},{8,9},{9,8},{10,11... | collective-permute-start | bytes 1376264 | tf_op jit(solution)/shard_map/ppermute | solution.py:24
  142.5 8.8 %collective-permute-start.37 = (bf16[2,128,896]{2,1,0:T(8,128)(2,1)S(1)}, bf16[2,128,896]{2,1,0:T(8,128)(2,1)S(1)}, u32[]{:S(2)}, u32[]{:S(2)}) collective-permute-start(bf16[2,128,896]{2,1,0:T(8,128)(2,1)S(1)} %collective-permute-done.31.refs_1_), channel_id=1, source_target_pairs={{0,1},{1,0},{2,3},{3,2},{4,5},{5,4},{6,7},{7,6},{8,9},{9,8},{10,11... | collective-permute-start | bytes 1376264 | tf_op jit(solution)/shard_map/ppermute | solution.py:24
  167.8 19.1 %collective-permute-start.49 = (bf16[2,256,1792]{2,1,0:T(8,128)(2,1)S(1)}, bf16[2,256,1792]{2,1,0:T(8,128)(2,1)S(1)}, u32[]{:S(2)}, u32[]{:S(2)}) collective-permute-start(bf16[2,256,1792]{2,1,0:T(8,128)(2,1)S(1)} %get-tuple-element.56), channel_id=1, source_target_pairs={{0,1},{1,0},{2,3},{3,2},{4,5},{5,4},{6,7},{7,6},{8,9},{9,8},{10,11... | collective-permute-start | bytes 5505032 | tf_op jit(solution)/shard_map/ppermute | solution.py:24
  179.2 20.7 %collective-permute-start.56 = (bf16[2,256,1792]{2,1,0:T(8,128)(2,1)S(1)}, bf16[2,256,1792]{2,1,0:T(8,128)(2,1)S(1)}, u32[]{:S(2)}, u32[]{:S(2)}) collective-permute-start(bf16[2,256,1792]{2,1,0:T(8,128)(2,1)S(1)} %get-tuple-element.61), channel_id=1, source_target_pairs={{0,1},{1,0},{2,3},{3,2},{4,5},{5,4},{6,7},{7,6},{8,9},{9,8},{10,11... | collective-permute-start | bytes 5505032 | tf_op jit(solution)/shard_map/ppermute | solution.py:24
  187.3 12.5 %collective-permute-start.50 = (bf16[128,1792]{1,0:T(8,128)(2,1)S(1)}, bf16[128,1792]{1,0:T(8,128)(2,1)S(1)}, u32[]{:S(2)}, u32[]{:S(2)}) collective-permute-start(bf16[128,1792]{1,0:T(8,128)(2,1)S(1)} %slice_bitcast_fusion.2), channel_id=1, source_target_pairs={{0,16},{16,0},{1,17},{17,1},{2,18},{18,2},{3,19},{19,3},{4,20},{20... | collective-permute-start | bytes 1376264 | tf_op jit(solution)/shard_map/ppermute | solution.py:24
  189.2 14.2 %collective-permute-start.53 = (bf16[2,128,896]{2,1,0:T(8,128)(2,1)S(1)}, bf16[2,128,896]{2,1,0:T(8,128)(2,1)S(1)}, u32[]{:S(2)}, u32[]{:S(2)}) collective-permute-start(bf16[2,128,896]{2,1,0:T(8,128)(2,1)S(1)} %constant_dynamic-slice_fusion.2), channel_id=1, source_target_pairs={{0,2},{2,0},{1,3},{3,1},{4,6},{6,4},{5,7},{7,5},{8,10},{10,8},{9,1... | collective-permute-start | bytes 1376264 | tf_op jit(solution)/shard_map/ppermute | solution.py:24
  200.5 19.1 %collective-permute-start.60 = (bf16[128,1792]{1,0:T(8,128)(2,1)S(1)}, bf16[128,1792]{1,0:T(8,128)(2,1)S(1)}, u32[]{:S(2)}, u32[]{:S(2)}) collective-permute-start(bf16[128,1792]{1,0:T(8,128)(2,1)S(1)} %slice_bitcast_fusion), channel_id=1, source_target_pairs={{0,16},{16,0},{1,17},{17,1},{2,18},{18,2},{3,19},{19,3},{4,20},{20... | collective-permute-start | bytes 1376264 | tf_op jit(solution)/shard_map/ppermute | solution.py:24
  202.2 8.6 %collective-permute-start.51 = (bf16[128,896]{1,0:T(8,128)(2,1)S(1)}, bf16[128,896]{1,0:T(8,128)(2,1)S(1)}, u32[]{:S(2)}, u32[]{:S(2)}) collective-permute-start(bf16[128,896]{1,0:T(8,128)(2,1)S(1)} %constant_dynamic-slice_fusion.3), channel_id=1, source_target_pairs={{0,2},{2,0},{1,3},{3,1},{4,6},{6,4},{5,7},{7,5},{8,10},{10,8},{9,1... | collective-permute-start | bytes 688136 | tf_op jit(solution)/shard_map/ppermute | solution.py:24
  203.7 13.4 %collective-permute-start.54 = (bf16[128,896]{1,0:T(8,128)(2,1)S(1)}, bf16[128,896]{1,0:T(8,128)(2,1)S(1)}, u32[]{:S(2)}, u32[]{:S(2)}) collective-permute-start(bf16[128,896]{1,0:T(8,128)(2,1)S(1)} %slice_bitcast_fusion.6), channel_id=1, source_target_pairs={{0,16},{16,0},{1,17},{17,1},{2,18},{18,2},{3,19},{19,3},{4,20},{20... | collective-permute-start | bytes 688136 | tf_op jit(solution)/shard_map/ppermute | solution.py:24
  204.5 14.1 %collective-permute-start.57 = (bf16[2,128,896]{2,1,0:T(8,128)(2,1)S(1)}, bf16[2,128,896]{2,1,0:T(8,128)(2,1)S(1)}, u32[]{:S(2)}, u32[]{:S(2)}) collective-permute-start(bf16[2,128,896]{2,1,0:T(8,128)(2,1)S(1)} %constant_dynamic-slice_fusion.1), channel_id=1, source_target_pairs={{0,2},{2,0},{1,3},{3,1},{4,6},{6,4},{5,7},{7,5},{8,10},{10,8},{9,1... | collective-permute-start | bytes 1376264 | tf_op jit(solution)/shard_map/ppermute | solution.py:24
  211.0 16.5 %collective-permute-start.52 = (bf16[128,896]{1,0:T(8,128)(2,1)S(1)}, bf16[128,896]{1,0:T(8,128)(2,1)S(1)}, u32[]{:S(2)}, u32[]{:S(2)}) collective-permute-start(bf16[128,896]{1,0:T(8,128)(2,1)S(1)} %add_convert_fusion.6), channel_id=1, source_target_pairs={{0,8},{4,12},{8,0},{12,4},{1,9},{5,13},{9,1},{13,5},{2,10},{6,14},... | collective-permute-start | bytes 688136 | tf_op jit(solution)/shard_map/ppermute | solution.py:29
  217.1 10.4 %collective-permute-start.55 = (bf16[128,896]{1,0:T(8,128)(2,1)S(1)}, bf16[128,896]{1,0:T(8,128)(2,1)S(1)}, u32[]{:S(2)}, u32[]{:S(2)}) collective-permute-start(bf16[128,896]{1,0:T(8,128)(2,1)S(1)} %fusion.11), channel_id=1, source_target_pairs={{0,4},{4,8},{8,12},{12,0},{1,5},{5,9},{9,13},{13,1},{2,6},{6,10},{... | collective-permute-start | bytes 688136 | tf_op jit(solution)/shard_map/ppermute | solution.py:29
  218.8 6.1 %collective-permute-start.58 = (bf16[128,896]{1,0:T(8,128)(2,1)S(1)}, bf16[128,896]{1,0:T(8,128)(2,1)S(1)}, u32[]{:S(2)}, u32[]{:S(2)}) collective-permute-start(bf16[128,896]{1,0:T(8,128)(2,1)S(1)} %slice_bitcast_fusion.4), channel_id=1, source_target_pairs={{0,16},{16,0},{1,17},{17,1},{2,18},{18,2},{3,19},{19,3},{4,20},{20... | collective-permute-start | bytes 688136 | tf_op jit(solution)/shard_map/ppermute | solution.py:24
  219.9 7.6 %collective-permute-start.61 = (bf16[128,896]{1,0:T(8,128)(2,1)S(1)}, bf16[128,896]{1,0:T(8,128)(2,1)S(1)}, u32[]{:S(2)}, u32[]{:S(2)}) collective-permute-start(bf16[128,896]{1,0:T(8,128)(2,1)S(1)} %constant_dynamic-slice_fusion), channel_id=1, source_target_pairs={{0,2},{2,0},{1,3},{3,1},{4,6},{6,4},{5,7},{7,5},{8,10},{10,8},{9,1... | collective-permute-start | bytes 688136 | tf_op jit(solution)/shard_map/ppermute | solution.py:24
  224.9 6.1 %collective-permute-start.59 = (bf16[128,896]{1,0:T(8,128)(2,1)S(1)}, bf16[128,896]{1,0:T(8,128)(2,1)S(1)}, u32[]{:S(2)}, u32[]{:S(2)}) collective-permute-start(bf16[128,896]{1,0:T(8,128)(2,1)S(1)} %fusion.10), channel_id=1, source_target_pairs={{0,12},{4,0},{8,4},{12,8},{1,13},{5,1},{9,5},{13,9},{2,14},{6,2},{... | collective-permute-start | bytes 688136 | tf_op jit(solution)/shard_map/ppermute | solution.py:29
  231.3 1.4 collective-permute-start.62
  (4 other events, 22.9 us)

commit v5 on v3

--- a/solution.py
+++ b/solution.py
@@ -80,7 +80,7 @@
             out_specs=pl.BlockSpec((tile, heads, LAT), lambda r, length: (r, 0, 0)),
         ),
         out_shape=jax.ShapeDtypeStruct((rows, heads, LAT), BF16),
-        compiler_params=pltpu.CompilerParams(vmem_limit_bytes=16 * MIB),
+        compiler_params=pltpu.CompilerParams(vmem_limit_bytes=6 * MIB),
         cost_estimate=pl.CostEstimate(
             flops=2 * rows * heads * positions * (depth + LAT),
             bytes_accessed=2 * rows * (heads * (depth + LAT) + positions * depth),
@@ -172,7 +172,7 @@
             pltpu.VMEM((2 * width, count * size), F32),
             pltpu.SemaphoreType.DMA((count + 2 * (depth // min(2048, depth)),)),
         ],
-        compiler_params=pltpu.CompilerParams(vmem_limit_bytes=16 * MIB),
+        compiler_params=pltpu.CompilerParams(vmem_limit_bytes=12 * MIB),
         cost_estimate=pl.CostEstimate(
             flops=4 * count * size * depth * width,
             bytes_accessed=2 * depth * (2 * width + count * size),
@@ -312,7 +312,7 @@
             pltpu.SemaphoreType.DMA((steps, 2, len(units), 2)),
             pltpu.SemaphoreType.DMA((steps, 2, 2)),
         ],
-        compiler_params=pltpu.CompilerParams(vmem_limit_bytes=(12 + 10 * len(units)) * MIB),
+        compiler_params=pltpu.CompilerParams(vmem_limit_bytes=(3 + 11 * len(units)) * MIB),
         cost_estimate=pl.CostEstimate(
             flops=4 * rows * len(units) * depth * columns,
             bytes_accessed=4 * len(units) * depth * columns,

time: 235 us -> 235 us (level)
  no operation moved by 1% of the time
where the time goes in v5:
time: 235 us; the launch traced here: 234 us
  waiting for transfers between devices  84.2 us (36%)
  starting transfers between devices  71.9 us (31%)
  Pallas kernels  46 us (20%)
  matrix products  21 us (9%)
  local copies, waits for them, and re-layouts  5.28 us (2%)
  other arithmetic  4.93 us (2%)
    ppermute x30, waiting for transfers between devices, swap(): return lax.ppermute(value, axis, [(0, 1), (1, 0)])  48.6 us
    pallas_call x3, Pallas kernels, hidden_part(): pl.pallas_call(functools.partial(hidden_kernel, layout, first, last), in_...  28.2 us
    ppermute x30, starting transfers between devices, swap(): return lax.ppermute(value, axis, [(0, 1), (1, 0)])  23.6 us
    ppermute x14, starting transfers between devices, on_device(): lax.ppermute(value, ('line', 'side'), [(2 * i + y, 2 * i + 1 - y) for i i...  23.3 us
    dot_general x2, matrix products, on_device(): jnp.dot(rows, w_down[0], preferred_element_type=F32)  19 us
    ppermute x6, waiting for transfers between devices, on_device(): lefts.append(lax.ppermute(lefts[-1], 'line', left))  12.4 us
    ppermute x6, starting transfers between devices, on_device(): rights.append(lax.ppermute(rights[-1], 'line', right))  11.8 us
    pallas_call x2, Pallas kernels, project(): pl.pallas_call(functools.partial(project_kernel, slots, start, first), in...  11.2 us
  transfers between devices with their start and end apart: 63, of which 26 were waited for; matrix products, arithmetic and copies ran while one was open for 7% of the time, Pallas kernels for 12%

profile of v5, /device:TPU:0, one launch (start us, length us, event | category | flops | bytes accessed | tf_op | source)
XLA Modules:
  0.0 234.3 jit_solution(15490429922023924791)
XLA Ops:
  1.1 6.7 %shard_map.109 = bf16[32,64,512]{2,1,0:T(8,128)(2,1)S(1)} custom-call(s32[32]{0:T(128)S(1)} %copy-done, bf16[32,64,576]{2,1,0:T(8,128)(2,1)} %query_ref.1, bf16[32,576,128]{2,1,0:T(8,128)(2,1)} %bitcast.121), custom_call_target="tpu_custom_call" | custom-call | flops 570425344 | bytes 9175040 | tf_op jit(solution)/shard_map/pallas_call | solution.py:71
  7.9 2.0 fusion.19
  10.0 4.5 %collective-permute-start.1 = (bf16[32,4096]{1,0:T(8,128)(2,1)S(1)}, bf16[32,4096]{1,0:T(8,128)(2,1)S(1)}, u32[]{:S(2)}, u32[]{:S(2)}) collective-permute-start(bf16[32,4096]{1,0:T(8,128)(2,1)S(1)} %get-tuple-element.67.refs_0_), channel_id=1, source_target_pairs={{0,4},{4,8},{8,12},{1,5},{5,9},{9,13},{2,6},{6,10},{10,14},{3,7},{... | collective-permute-start | bytes 786440 | tf_op jit(solution)/shard_map/ppermute | solution.py:403
  14.5 1.3 collective-permute-start.4
  15.8 1.6 collective-permute-start.8
  19.4 4.6 %collective-permute-start.15 = (bf16[32,4096]{1,0:T(8,128)(2,1)S(1)}, bf16[32,4096]{1,0:T(8,128)(2,1)S(1)}, u32[]{:S(2)}, u32[]{:S(2)}) collective-permute-start(bf16[32,4096]{1,0:T(8,128)(2,1)S(1)} %get-tuple-element.37.refs_1_), channel_id=1, source_target_pairs={{0,4},{4,8},{8,12},{1,5},{5,9},{9,13},{2,6},{6,10},{10,14},{3,7},{... | collective-permute-start | bytes 786440 | tf_op jit(solution)/shard_map/ppermute | solution.py:403
  24.0 1.3 collective-permute-start.16
  26.0 1.2 collective-permute-start.21
  27.1 2.7 %collective-permute-done.15.refs_2_ = bf16[32,4096]{1,0:T(8,128)(2,1)S(1)} collective-permute-done((bf16[32,4096]{1,0:T(8,128)(2,1)S(1)}, bf16[32,4096]{1,0:T(8,128)(2,1)S(1)}, u32[]{:S(2)}, u32[]{:S(2)}) %collective-permute-start.15) | collective-permute-done | bytes 262176 | tf_op jit(solution)/shard_map/ppermute | solution.py:403
  29.8 1.3 collective-permute-start.5
  31.1 2.9 %collective-permute-done.16.refs_3_ = bf16[32,4096]{1,0:T(8,128)(2,1)S(1)} collective-permute-done((bf16[32,4096]{1,0:T(8,128)(2,1)S(1)}, bf16[32,4096]{1,0:T(8,128)(2,1)S(1)}, u32[]{:S(2)}, u32[]{:S(2)}) %collective-permute-start.16) | collective-permute-done | bytes 262176 | tf_op jit(solution)/shard_map/ppermute | solution.py:404
  33.9 2.4 %collective-permute-start.10 = (bf16[32,4096]{1,0:T(8,128)(2,1)S(1)}, bf16[32,4096]{1,0:T(8,128)(2,1)S(1)}, u32[]{:S(2)}, u32[]{:S(2)}) collective-permute-start(bf16[32,4096]{1,0:T(8,128)(2,1)S(1)} %collective-permute-done.4.refs_2_), channel_id=1, source_target_pairs={{0,2},{2,0},{4,6},{6,4},{8,10},{10,8},{1,3},{3,1},{5,7},{7,5},{9,1... | collective-permute-start | bytes 786440 | tf_op jit(solution)/shard_map/ppermute | solution.py:407
  37.8 1.3 collective-permute-start.18
  40.6 2.4 %collective-permute-done.10.refs_9_ = bf16[32,4096]{1,0:T(8,128)(2,1)S(1)} collective-permute-done((bf16[32,4096]{1,0:T(8,128)(2,1)S(1)}, bf16[32,4096]{1,0:T(8,128)(2,1)S(1)}, u32[]{:S(2)}, u32[]{:S(2)}) %collective-permute-start.10) | collective-permute-done | bytes 262176 | tf_op jit(solution)/shard_map/ppermute | solution.py:407
  43.0 1.3 collective-permute-start.7
  44.3 2.4 %collective-permute-start.12 = (bf16[32,4096]{1,0:T(8,128)(2,1)S(1)}, bf16[32,4096]{1,0:T(8,128)(2,1)S(1)}, u32[]{:S(2)}, u32[]{:S(2)}) collective-permute-start(bf16[32,4096]{1,0:T(8,128)(2,1)S(1)} %collective-permute-done.5.refs_4_), channel_id=1, source_target_pairs={{0,2},{2,0},{4,6},{6,4},{1,3},{3,1},{5,7},{7,5},{16,18},{18,16},{2... | collective-permute-start | bytes 786440 | tf_op jit(solution)/shard_map/ppermute | solution.py:407
  47.5 5.9 %collective-permute-done.18.refs_5_ = bf16[32,4096]{1,0:T(8,128)(2,1)S(1)} collective-permute-done((bf16[32,4096]{1,0:T(8,128)(2,1)S(1)}, bf16[32,4096]{1,0:T(8,128)(2,1)S(1)}, u32[]{:S(2)}, u32[]{:S(2)}) %collective-permute-start.18) | collective-permute-done | bytes 262176 | tf_op jit(solution)/shard_map/ppermute | solution.py:404
  54.0 1.3 collective-permute-start.20
  55.3 2.7 %collective-permute-done.7.refs_6_ = bf16[32,4096]{1,0:T(8,128)(2,1)S(1)} collective-permute-done((bf16[32,4096]{1,0:T(8,128)(2,1)S(1)}, bf16[32,4096]{1,0:T(8,128)(2,1)S(1)}, u32[]{:S(2)}, u32[]{:S(2)}) %collective-permute-start.7) | collective-permute-done | bytes 262176 | tf_op jit(solution)/shard_map/ppermute | solution.py:404
  58.1 2.8 %collective-permute-start.14 = (bf16[32,4096]{1,0:T(8,128)(2,1)S(1)}, bf16[32,4096]{1,0:T(8,128)(2,1)S(1)}, u32[]{:S(2)}, u32[]{:S(2)}) collective-permute-start(bf16[32,4096]{1,0:T(8,128)(2,1)S(1)} %collective-permute-done.7.refs_6_), channel_id=1, source_target_pairs={{0,2},{2,0},{1,3},{3,1},{16,18},{18,16},{17,19},{19,17}} | collective-permute-start | bytes 786440 | tf_op jit(solution)/shard_map/ppermute | solution.py:407
  62.3 3.0 %collective-permute-start.23 = (bf16[32,4096]{1,0:T(8,128)(2,1)S(1)}, bf16[32,4096]{1,0:T(8,128)(2,1)S(1)}, u32[]{:S(2)}, u32[]{:S(2)}) collective-permute-start(bf16[32,4096]{1,0:T(8,128)(2,1)S(1)} %collective-permute-done.16.refs_3_), channel_id=1, source_target_pairs={{0,2},{2,0},{4,6},{6,4},{8,10},{10,8},{1,3},{3,1},{5,7},{7,5},{9,1... | collective-permute-start | bytes 786440 | tf_op jit(solution)/shard_map/ppermute | solution.py:407
  66.0 2.9 %collective-permute-done.14.refs_13_ = bf16[32,4096]{1,0:T(8,128)(2,1)S(1)} collective-permute-done((bf16[32,4096]{1,0:T(8,128)(2,1)S(1)}, bf16[32,4096]{1,0:T(8,128)(2,1)S(1)}, u32[]{:S(2)}, u32[]{:S(2)}) %collective-permute-start.14) | collective-permute-done | bytes 262176 | tf_op jit(solution)/shard_map/ppermute | solution.py:407
  68.9 2.8 %collective-permute-start.25 = (bf16[32,4096]{1,0:T(8,128)(2,1)S(1)}, bf16[32,4096]{1,0:T(8,128)(2,1)S(1)}, u32[]{:S(2)}, u32[]{:S(2)}) collective-permute-start(bf16[32,4096]{1,0:T(8,128)(2,1)S(1)} %collective-permute-done.18.refs_5_), channel_id=1, source_target_pairs={{0,2},{2,0},{4,6},{6,4},{1,3},{3,1},{5,7},{7,5},{16,18},{18,16},{2... | collective-permute-start | bytes 786440 | tf_op jit(solution)/shard_map/ppermute | solution.py:407
  72.4 3.0 %collective-permute-start.27 = (bf16[32,4096]{1,0:T(8,128)(2,1)S(1)}, bf16[32,4096]{1,0:T(8,128)(2,1)S(1)}, u32[]{:S(2)}, u32[]{:S(2)}) collective-permute-start(bf16[32,4096]{1,0:T(8,128)(2,1)S(1)} %collective-permute-done.20.refs_7_), channel_id=1, source_target_pairs={{0,2},{2,0},{1,3},{3,1},{16,18},{18,16},{17,19},{19,17}} | collective-permute-start | bytes 786440 | tf_op jit(solution)/shard_map/ppermute | solution.py:407
  75.4 5.6 %shard_map.110.refs_0_ = f32[256,896]{1,0:T(8,128)S(1)} custom-call(s32[17]{0:T(128)S(1)} %stack.169.place_ref, bf16[448,8192]{1,0:T(8,128)(2,1)} %bitcast.119, bf16[448,8192]{1,0:T(8,128)(2,1)} %collective-permute-done.3.sibling_ref, bf16[32,4096]{1,0:T(8,128)(2,1)S(1)} %get-tuple-element.67.refs_0_, bf16[32,4096]{1,0:T(8,128)(2,1)S(1)} %collective-permute-done.1.refs_1_, ...), custom_call_target="tpu_custom_call" | custom-call | flops 1879048192 | bytes 9437184 | tf_op jit(solution)/shard_map/pallas_call | solution.py:161
  81.0 2.1 collective-permute-done.27.refs_14_
  83.2 5.6 %shard_map.111 = bf16[256,896]{1,0:T(8,128)(2,1)S(1)} custom-call(s32[17]{0:T(128)S(1)} %stack.169.place_ref, bf16[448,8192]{1,0:T(8,128)(2,1)} %bitcast.120, bf16[448,8192]{1,0:T(8,128)(2,1)} %collective-permute-done.3.sibling_ref, f32[256,896]{1,0:T(8,128)S(1)} %shard_map.110.refs_0_, bf16[32,4096]{1,0:T(8,128)(2,1)S(1)} %get-tuple-element.37.refs_1_, ...), custom_call_target="tpu_custom_call" | custom-call | flops 1879048192 | bytes 9437184 | tf_op jit(solution)/shard_map/pallas_call | solution.py:161
  88.8 1.6 collective-permute-start.28
  90.3 5.3 %collective-permute-done.28 = bf16[128,896]{1,0:T(8,128)(2,1)S(1)} collective-permute-done((bf16[128,896]{1,0:T(8,128)(2,1)S(1)}, bf16[128,896]{1,0:T(8,128)(2,1)S(1)}, u32[]{:S(2)}, u32[]{:S(2)}) %collective-permute-start.28) | collective-permute-done | bytes 229408 | tf_op jit(solution)/shard_map/ppermute | solution.py:24
  95.7 1.6 collective-permute-start.32
  97.3 4.5 %collective-permute-done.32 = bf16[128,896]{1,0:T(8,128)(2,1)S(1)} collective-permute-done((bf16[128,896]{1,0:T(8,128)(2,1)S(1)}, bf16[128,896]{1,0:T(8,128)(2,1)S(1)}, u32[]{:S(2)}, u32[]{:S(2)}) %collective-permute-start.32) | collective-permute-done | bytes 229408 | tf_op jit(solution)/shard_map/ppermute | solution.py:24
  102.8 2.4 %collective-permute-done.29 = bf16[128,896]{1,0:T(8,128)(2,1)S(1)} collective-permute-done((bf16[128,896]{1,0:T(8,128)(2,1)S(1)}, bf16[128,896]{1,0:T(8,128)(2,1)S(1)}, u32[]{:S(2)}, u32[]{:S(2)}) %collective-permute-start.29) | collective-permute-done | bytes 229408 | tf_op jit(solution)/shard_map/ppermute | solution.py:29
  105.9 3.0 %collective-permute-done.39 = bf16[128,896]{1,0:T(8,128)(2,1)S(1)} collective-permute-done((bf16[128,896]{1,0:T(8,128)(2,1)S(1)}, bf16[128,896]{1,0:T(8,128)(2,1)S(1)}, u32[]{:S(2)}, u32[]{:S(2)}) %collective-permute-start.39) | collective-permute-done | bytes 229408 | tf_op jit(solution)/shard_map/ppermute | solution.py:29
  108.9 1.5 collective-permute-start.40
  110.4 1.2 collective-permute-start.45
  112.5 4.3 %collective-permute-done.40 = bf16[128,896]{1,0:T(8,128)(2,1)S(1)} collective-permute-done((bf16[128,896]{1,0:T(8,128)(2,1)S(1)}, bf16[128,896]{1,0:T(8,128)(2,1)S(1)}, u32[]{:S(2)}, u32[]{:S(2)}) %collective-permute-start.40) | collective-permute-done | bytes 229408 | tf_op jit(solution)/shard_map/ppermute | solution.py:434
  116.8 1.6 collective-permute-start.41
  118.9 1.6 collective-permute-start.46
  120.5 2.8 %collective-permute-done.30 = bf16[128,896]{1,0:T(8,128)(2,1)S(1)} collective-permute-done((bf16[128,896]{1,0:T(8,128)(2,1)S(1)}, bf16[128,896]{1,0:T(8,128)(2,1)S(1)}, u32[]{:S(2)}, u32[]{:S(2)}) %collective-permute-start.30) | collective-permute-done | bytes 229408 | tf_op jit(solution)/shard_map/ppermute | solution.py:24
  123.4 1.6 collective-permute-done.41
  125.1 1.5 collective-permute-start.31
  126.6 1.2 collective-permute-start.42
  127.8 7.7 %shard_map.112 = (f32[512,1024]{1,0:T(8,128)S(1)}, f32[512,1024]{1,0:T(8,128)S(1)}) custom-call(s32[2]{0:T(128)S(1)} %get-tuple-element.41.place_ref, bf16[2,128,896]{2,1,0:T(8,128)(2,1)S(1)} %pad_maximum_fusion.3.refs_0_, bf16[2,128,896]{2,1,0:T(8,128)(2,1)S(1)} %collective-permute-done.33.refs_1_, ...), custom_call_target="tpu_custom_call" | custom-call | flops 3758096384 | bytes 7340032 | tf_op jit(solution)/shard_map/pallas_call | solution.py:302
  136.1 1.7 collective-permute-done.42.refs_5_
  137.8 4.8 %collective-permute-done.31.refs_1_ = bf16[2,128,896]{2,1,0:T(8,128)(2,1)S(1)} collective-permute-done((bf16[2,128,896]{2,1,0:T(8,128)(2,1)S(1)}, bf16[2,128,896]{2,1,0:T(8,128)(2,1)S(1)}, u32[]{:S(2)}, u32[]{:S(2)}) %collective-permute-start.31) | collective-permute-done | bytes 458784 | tf_op jit(solution)/shard_map/ppermute | solution.py:24
  143.1 8.2 %shard_map.113 = (f32[512,1024]{1,0:T(8,128)S(1)}, f32[512,1024]{1,0:T(8,128)S(1)}) custom-call(s32[2]{0:T(128)S(1)} %get-tuple-element.47.place_ref, bf16[2,128,896]{2,1,0:T(8,128)(2,1)S(1)} %pad_maximum_fusion.5.refs_0_, bf16[2,128,896]{2,1,0:T(8,128)(2,1)S(1)} %collective-permute-done.46.refs_1_, ...), custom_call_target="tpu_custom_call" | custom-call | flops 3758096384 | bytes 7340032 | tf_op jit(solution)/shard_map/pallas_call | solution.py:302
  151.4 12.2 %shard_map.114 = bf16[512,1024]{1,0:T(8,128)(2,1)S(1)} custom-call(s32[3]{0:T(128)S(1)} %pad_add_fusion.2.place_ref, bf16[2,128,896]{2,1,0:T(8,128)(2,1)S(1)} %pad_maximum_fusion.2.refs_0_, bf16[2,128,896]{2,1,0:T(8,128)(2,1)S(1)} %collective-permute-done.31.refs_1_, bf16[2,128,896]{2,1,0:T(8,128)(2,1)S(1)} %collective-permute-done.36.refs_2_, ...), custom_call_target="tpu_custom_call" | custom-call | flops 7516192768 | bytes 14680064 | tf_op jit(solution)/shard_map/pallas_call | solution.py:302
  163.6 9.6 %fusion.7 = bf16[256,7168]{1,0:T(8,128)(2,1)S(1)} fusion(bf16[1,1024,7168]{2,1,0:T(8,128)(2,1)} %param.19, bf16[512,1024]{1,0:T(8,128)(2,1)S(1)} %shard_map.114), kind=kOutput, calls=%fused_computation.5 | convolution fusion | flops 3759931392 | bytes 18874368 | tf_op jit(solution)/shard_map/dot_general | solution.py:475
  173.2 2.2 dynamic-slice_bitcast_fusion.3
  176.4 9.4 %fusion.4 = bf16[256,7168]{1,0:T(8,128)(2,1)S(1)} fusion(bf16[1,1024,7168]{2,1,0:T(8,128)(2,1)} %param.19, bf16[512,1024]{1,0:T(8,128)(2,1)S(1)} %shard_map.114), kind=kOutput, calls=%fused_computation.4 | convolution fusion | flops 3759931392 | bytes 18874368 | tf_op jit(solution)/shard_map/dot_general | solution.py:475
  185.8 1.3 fusion.14
  187.1 1.6 collective-permute-start.50
  188.9 1.2 collective-permute-start.53
  190.1 9.6 %collective-permute-done.50 = bf16[128,1792]{1,0:T(8,128)(2,1)S(1)} collective-permute-done((bf16[128,1792]{1,0:T(8,128)(2,1)S(1)}, bf16[128,1792]{1,0:T(8,128)(2,1)S(1)}, u32[]{:S(2)}, u32[]{:S(2)}) %collective-permute-start.50) | collective-permute-done | bytes 458784 | tf_op jit(solution)/shard_map/ppermute | solution.py:24
  199.8 1.3 fusion.12
  201.1 1.6 collective-permute-start.60
  202.8 1.2 collective-permute-start.51
  206.1 5.4 %collective-permute-done.51 = bf16[128,896]{1,0:T(8,128)(2,1)S(1)} collective-permute-done((bf16[128,896]{1,0:T(8,128)(2,1)S(1)}, bf16[128,896]{1,0:T(8,128)(2,1)S(1)}, u32[]{:S(2)}, u32[]{:S(2)}) %collective-permute-start.51) | collective-permute-done | bytes 229408 | tf_op jit(solution)/shard_map/ppermute | solution.py:24
  211.7 6.1 %collective-permute-done.54 = bf16[128,896]{1,0:T(8,128)(2,1)S(1)} collective-permute-done((bf16[128,896]{1,0:T(8,128)(2,1)S(1)}, bf16[128,896]{1,0:T(8,128)(2,1)S(1)}, u32[]{:S(2)}, u32[]{:S(2)}) %collective-permute-start.54) | collective-permute-done | bytes 229408 | tf_op jit(solution)/shard_map/ppermute | solution.py:24
  220.7 1.2 collective-permute-start.61
  221.8 3.7 %collective-permute-done.58 = bf16[128,896]{1,0:T(8,128)(2,1)S(1)} collective-permute-done((bf16[128,896]{1,0:T(8,128)(2,1)S(1)}, bf16[128,896]{1,0:T(8,128)(2,1)S(1)}, u32[]{:S(2)}, u32[]{:S(2)}) %collective-permute-start.58) | collective-permute-done | bytes 229408 | tf_op jit(solution)/shard_map/ppermute | solution.py:24
  225.6 2.6 %collective-permute-start.59 = (bf16[128,896]{1,0:T(8,128)(2,1)S(1)}, bf16[128,896]{1,0:T(8,128)(2,1)S(1)}, u32[]{:S(2)}, u32[]{:S(2)}) collective-permute-start(bf16[128,896]{1,0:T(8,128)(2,1)S(1)} %fusion.24), channel_id=1, source_target_pairs={{0,12},{4,0},{8,4},{12,8},{1,13},{5,1},{9,5},{13,9},{2,14},{6,2},{... | collective-permute-start | bytes 688136 | tf_op jit(solution)/shard_map/ppermute | solution.py:29
  228.1 3.5 %collective-permute-done.59 = bf16[128,896]{1,0:T(8,128)(2,1)S(1)} collective-permute-done((bf16[128,896]{1,0:T(8,128)(2,1)S(1)}, bf16[128,896]{1,0:T(8,128)(2,1)S(1)}, u32[]{:S(2)}, u32[]{:S(2)}) %collective-permute-start.59) | collective-permute-done | bytes 229408 | tf_op jit(solution)/shard_map/ppermute | solution.py:29
  232.1 1.3 collective-permute-done.62
  (128 shorter events, 23.3 us)
Async XLA Ops:
  0.0 37.1 %collective-permute-start.3 = (bf16[448,8192]{1,0:T(8,128)(2,1)}, bf16[448,8192]{1,0:T(8,128)(2,1)}, u32[]{:S(2)}, u32[]{:S(2)}) collective-permute-start(bf16[448,8192]{1,0:T(8,128)(2,1)} %bitcast.118), channel_id=1, source_target_pairs={{0,1},{1,0},{2,3},{3,2},{4,5},{5,4},{6,7},{7,6},{8,9},{9,8},{10,11... | collective-permute-start | bytes 22020104 | tf_op jit(solution)/shard_map/ppermute | solution.py:24
  9.9 7.9 %copy-start.3 = (f32[512,8]{0,1:T(8,128)S(1)}, f32[512,8]{0,1:T(8,128)}, u32[]{:S(2)}) copy-start(f32[512,8]{0,1:T(8,128)} %param.21) | copy-start | bytes 49156
  10.0 13.9 %collective-permute-start.1 = (bf16[32,4096]{1,0:T(8,128)(2,1)S(1)}, bf16[32,4096]{1,0:T(8,128)(2,1)S(1)}, u32[]{:S(2)}, u32[]{:S(2)}) collective-permute-start(bf16[32,4096]{1,0:T(8,128)(2,1)S(1)} %get-tuple-element.67.refs_0_), channel_id=1, source_target_pairs={{0,4},{4,8},{8,12},{1,5},{5,9},{9,13},{2,6},{6,10},{10,14},{3,7},{... | collective-permute-start | bytes 786440 | tf_op jit(solution)/shard_map/ppermute | solution.py:403
  14.5 10.7 %collective-permute-start.4 = (bf16[32,4096]{1,0:T(8,128)(2,1)S(1)}, bf16[32,4096]{1,0:T(8,128)(2,1)S(1)}, u32[]{:S(2)}, u32[]{:S(2)}) collective-permute-start(bf16[32,4096]{1,0:T(8,128)(2,1)S(1)} %get-tuple-element.67.refs_0_), channel_id=1, source_target_pairs={{4,0},{8,4},{12,8},{5,1},{9,5},{13,9},{6,2},{10,6},{14,10},{7,3},{... | collective-permute-start | bytes 786440 | tf_op jit(solution)/shard_map/ppermute | solution.py:404
  15.8 10.1 %collective-permute-start.8 = (bf16[32,4096]{1,0:T(8,128)(2,1)S(1)}, bf16[32,4096]{1,0:T(8,128)(2,1)S(1)}, u32[]{:S(2)}, u32[]{:S(2)}) collective-permute-start(bf16[32,4096]{1,0:T(8,128)(2,1)S(1)} %get-tuple-element.67.refs_0_), channel_id=1, source_target_pairs={{0,2},{2,0},{4,6},{6,4},{8,10},{10,8},{12,14},{14,12},{1,3},{3,1},... | collective-permute-start | bytes 786440 | tf_op jit(solution)/shard_map/ppermute | solution.py:407
  17.7 1.4 collective-permute-start
  19.4 10.4 %collective-permute-start.15 = (bf16[32,4096]{1,0:T(8,128)(2,1)S(1)}, bf16[32,4096]{1,0:T(8,128)(2,1)S(1)}, u32[]{:S(2)}, u32[]{:S(2)}) collective-permute-start(bf16[32,4096]{1,0:T(8,128)(2,1)S(1)} %get-tuple-element.37.refs_1_), channel_id=1, source_target_pairs={{0,4},{4,8},{8,12},{1,5},{5,9},{9,13},{2,6},{6,10},{10,14},{3,7},{... | collective-permute-start | bytes 786440 | tf_op jit(solution)/shard_map/ppermute | solution.py:403
  24.0 10.0 %collective-permute-start.16 = (bf16[32,4096]{1,0:T(8,128)(2,1)S(1)}, bf16[32,4096]{1,0:T(8,128)(2,1)S(1)}, u32[]{:S(2)}, u32[]{:S(2)}) collective-permute-start(bf16[32,4096]{1,0:T(8,128)(2,1)S(1)} %get-tuple-element.37.refs_1_), channel_id=1, source_target_pairs={{4,0},{8,4},{12,8},{5,1},{9,5},{13,9},{6,2},{10,6},{14,10},{7,3},{... | collective-permute-start | bytes 786440 | tf_op jit(solution)/shard_map/ppermute | solution.py:404
  25.3 11.1 %collective-permute-start.2 = (bf16[32,4096]{1,0:T(8,128)(2,1)S(1)}, bf16[32,4096]{1,0:T(8,128)(2,1)S(1)}, u32[]{:S(2)}, u32[]{:S(2)}) collective-permute-start(bf16[32,4096]{1,0:T(8,128)(2,1)S(1)} %collective-permute-done.1.refs_1_), channel_id=1, source_target_pairs={{4,8},{8,12},{5,9},{9,13},{6,10},{10,14},{7,11},{11,15},{20,24},{2... | collective-permute-start | bytes 786440 | tf_op jit(solution)/shard_map/ppermute | solution.py:403
  26.0 11.8 %collective-permute-start.21 = (bf16[32,4096]{1,0:T(8,128)(2,1)S(1)}, bf16[32,4096]{1,0:T(8,128)(2,1)S(1)}, u32[]{:S(2)}, u32[]{:S(2)}) collective-permute-start(bf16[32,4096]{1,0:T(8,128)(2,1)S(1)} %get-tuple-element.37.refs_1_), channel_id=1, source_target_pairs={{0,2},{2,0},{4,6},{6,4},{8,10},{10,8},{12,14},{14,12},{1,3},{3,1},... | collective-permute-start | bytes 786440 | tf_op jit(solution)/shard_map/ppermute | solution.py:407
  29.8 10.2 %collective-permute-start.5 = (bf16[32,4096]{1,0:T(8,128)(2,1)S(1)}, bf16[32,4096]{1,0:T(8,128)(2,1)S(1)}, u32[]{:S(2)}, u32[]{:S(2)}) collective-permute-start(bf16[32,4096]{1,0:T(8,128)(2,1)S(1)} %collective-permute-done.4.refs_2_), channel_id=1, source_target_pairs={{4,0},{8,4},{5,1},{9,5},{6,2},{10,6},{7,3},{11,7},{20,16},{24,20},... | collective-permute-start | bytes 786440 | tf_op jit(solution)/shard_map/ppermute | solution.py:404
  33.9 9.1 %collective-permute-start.10 = (bf16[32,4096]{1,0:T(8,128)(2,1)S(1)}, bf16[32,4096]{1,0:T(8,128)(2,1)S(1)}, u32[]{:S(2)}, u32[]{:S(2)}) collective-permute-start(bf16[32,4096]{1,0:T(8,128)(2,1)S(1)} %collective-permute-done.4.refs_2_), channel_id=1, source_target_pairs={{0,2},{2,0},{4,6},{6,4},{8,10},{10,8},{1,3},{3,1},{5,7},{7,5},{9,1... | collective-permute-start | bytes 786440 | tf_op jit(solution)/shard_map/ppermute | solution.py:407
  36.4 8.0 %collective-permute-start.9 = (bf16[32,4096]{1,0:T(8,128)(2,1)S(1)}, bf16[32,4096]{1,0:T(8,128)(2,1)S(1)}, u32[]{:S(2)}, u32[]{:S(2)}) collective-permute-start(bf16[32,4096]{1,0:T(8,128)(2,1)S(1)} %collective-permute-done.1.refs_1_), channel_id=1, source_target_pairs={{4,6},{6,4},{8,10},{10,8},{12,14},{14,12},{5,7},{7,5},{9,11},{11,9... | collective-permute-start | bytes 786440 | tf_op jit(solution)/shard_map/ppermute | solution.py:407
  37.1 9.7 %collective-permute-start.17 = (bf16[32,4096]{1,0:T(8,128)(2,1)S(1)}, bf16[32,4096]{1,0:T(8,128)(2,1)S(1)}, u32[]{:S(2)}, u32[]{:S(2)}) collective-permute-start(bf16[32,4096]{1,0:T(8,128)(2,1)S(1)} %collective-permute-done.15.refs_2_), channel_id=1, source_target_pairs={{4,8},{8,12},{5,9},{9,13},{6,10},{10,14},{7,11},{11,15},{20,24},{2... | collective-permute-start | bytes 786440 | tf_op jit(solution)/shard_map/ppermute | solution.py:403
  37.8 15.6 %collective-permute-start.18 = (bf16[32,4096]{1,0:T(8,128)(2,1)S(1)}, bf16[32,4096]{1,0:T(8,128)(2,1)S(1)}, u32[]{:S(2)}, u32[]{:S(2)}) collective-permute-start(bf16[32,4096]{1,0:T(8,128)(2,1)S(1)} %collective-permute-done.16.refs_3_), channel_id=1, source_target_pairs={{4,0},{8,4},{5,1},{9,5},{6,2},{10,6},{7,3},{11,7},{20,16},{24,20},... | collective-permute-start | bytes 786440 | tf_op jit(solution)/shard_map/ppermute | solution.py:404
  40.0 14.1 %collective-permute-start.22 = (bf16[32,4096]{1,0:T(8,128)(2,1)S(1)}, bf16[32,4096]{1,0:T(8,128)(2,1)S(1)}, u32[]{:S(2)}, u32[]{:S(2)}) collective-permute-start(bf16[32,4096]{1,0:T(8,128)(2,1)S(1)} %collective-permute-done.15.refs_2_), channel_id=1, source_target_pairs={{4,6},{6,4},{8,10},{10,8},{12,14},{14,12},{5,7},{7,5},{9,11},{11,9... | collective-permute-start | bytes 786440 | tf_op jit(solution)/shard_map/ppermute | solution.py:407
  43.0 15.0 %collective-permute-start.7 = (bf16[32,4096]{1,0:T(8,128)(2,1)S(1)}, bf16[32,4096]{1,0:T(8,128)(2,1)S(1)}, u32[]{:S(2)}, u32[]{:S(2)}) collective-permute-start(bf16[32,4096]{1,0:T(8,128)(2,1)S(1)} %collective-permute-done.5.refs_4_), channel_id=1, source_target_pairs={{4,0},{5,1},{6,2},{7,3},{20,16},{21,17},{22,18},{23,19}} | collective-permute-start | bytes 786440 | tf_op jit(solution)/shard_map/ppermute | solution.py:404
  44.3 16.5 %collective-permute-start.12 = (bf16[32,4096]{1,0:T(8,128)(2,1)S(1)}, bf16[32,4096]{1,0:T(8,128)(2,1)S(1)}, u32[]{:S(2)}, u32[]{:S(2)}) collective-permute-start(bf16[32,4096]{1,0:T(8,128)(2,1)S(1)} %collective-permute-done.5.refs_4_), channel_id=1, source_target_pairs={{0,2},{2,0},{4,6},{6,4},{1,3},{3,1},{5,7},{7,5},{16,18},{18,16},{2... | collective-permute-start | bytes 786440 | tf_op jit(solution)/shard_map/ppermute | solution.py:407
  46.8 14.8 %collective-permute-start.6 = (bf16[32,4096]{1,0:T(8,128)(2,1)S(1)}, bf16[32,4096]{1,0:T(8,128)(2,1)S(1)}, u32[]{:S(2)}, u32[]{:S(2)}) collective-permute-start(bf16[32,4096]{1,0:T(8,128)(2,1)S(1)} %collective-permute-done.2.refs_3_), channel_id=1, source_target_pairs={{8,12},{9,13},{10,14},{11,15},{24,28},{25,29},{26,30},{27,31}} | collective-permute-start | bytes 786440 | tf_op jit(solution)/shard_map/ppermute | solution.py:403
  53.4 8.9 %collective-permute-start.19 = (bf16[32,4096]{1,0:T(8,128)(2,1)S(1)}, bf16[32,4096]{1,0:T(8,128)(2,1)S(1)}, u32[]{:S(2)}, u32[]{:S(2)}) collective-permute-start(bf16[32,4096]{1,0:T(8,128)(2,1)S(1)} %collective-permute-done.17.refs_4_), channel_id=1, source_target_pairs={{8,12},{9,13},{10,14},{11,15},{24,28},{25,29},{26,30},{27,31}} | collective-permute-start | bytes 786440 | tf_op jit(solution)/shard_map/ppermute | solution.py:403
  54.0 11.3 %collective-permute-start.20 = (bf16[32,4096]{1,0:T(8,128)(2,1)S(1)}, bf16[32,4096]{1,0:T(8,128)(2,1)S(1)}, u32[]{:S(2)}, u32[]{:S(2)}) collective-permute-start(bf16[32,4096]{1,0:T(8,128)(2,1)S(1)} %collective-permute-done.18.refs_5_), channel_id=1, source_target_pairs={{4,0},{5,1},{6,2},{7,3},{20,16},{21,17},{22,18},{23,19}} | collective-permute-start | bytes 786440 | tf_op jit(solution)/shard_map/ppermute | solution.py:404
  58.1 10.8 %collective-permute-start.14 = (bf16[32,4096]{1,0:T(8,128)(2,1)S(1)}, bf16[32,4096]{1,0:T(8,128)(2,1)S(1)}, u32[]{:S(2)}, u32[]{:S(2)}) collective-permute-start(bf16[32,4096]{1,0:T(8,128)(2,1)S(1)} %collective-permute-done.7.refs_6_), channel_id=1, source_target_pairs={{0,2},{2,0},{1,3},{3,1},{16,18},{18,16},{17,19},{19,17}} | collective-permute-start | bytes 786440 | tf_op jit(solution)/shard_map/ppermute | solution.py:407
  60.9 10.8 %collective-permute-start.11 = (bf16[32,4096]{1,0:T(8,128)(2,1)S(1)}, bf16[32,4096]{1,0:T(8,128)(2,1)S(1)}, u32[]{:S(2)}, u32[]{:S(2)}) collective-permute-start(bf16[32,4096]{1,0:T(8,128)(2,1)S(1)} %collective-permute-done.2.refs_3_), channel_id=1, source_target_pairs={{8,10},{10,8},{12,14},{14,12},{9,11},{11,9},{13,15},{15,13},{24,26... | collective-permute-start | bytes 786440 | tf_op jit(solution)/shard_map/ppermute | solution.py:407
  61.6 10.8 %collective-permute-start.13 = (bf16[32,4096]{1,0:T(8,128)(2,1)S(1)}, bf16[32,4096]{1,0:T(8,128)(2,1)S(1)}, u32[]{:S(2)}, u32[]{:S(2)}) collective-permute-start(bf16[32,4096]{1,0:T(8,128)(2,1)S(1)} %collective-permute-done.6.refs_5_), channel_id=1, source_target_pairs={{12,14},{14,12},{13,15},{15,13},{28,30},{30,28},{29,31},{31,29}} | collective-permute-start | bytes 786440 | tf_op jit(solution)/shard_map/ppermute | solution.py:407
  62.3 18.7 %collective-permute-start.23 = (bf16[32,4096]{1,0:T(8,128)(2,1)S(1)}, bf16[32,4096]{1,0:T(8,128)(2,1)S(1)}, u32[]{:S(2)}, u32[]{:S(2)}) collective-permute-start(bf16[32,4096]{1,0:T(8,128)(2,1)S(1)} %collective-permute-done.16.refs_3_), channel_id=1, source_target_pairs={{0,2},{2,0},{4,6},{6,4},{8,10},{10,8},{1,3},{3,1},{5,7},{7,5},{9,1... | collective-permute-start | bytes 786440 | tf_op jit(solution)/shard_map/ppermute | solution.py:407
  65.3 15.7 %collective-permute-start.24 = (bf16[32,4096]{1,0:T(8,128)(2,1)S(1)}, bf16[32,4096]{1,0:T(8,128)(2,1)S(1)}, u32[]{:S(2)}, u32[]{:S(2)}) collective-permute-start(bf16[32,4096]{1,0:T(8,128)(2,1)S(1)} %collective-permute-done.17.refs_4_), channel_id=1, source_target_pairs={{8,10},{10,8},{12,14},{14,12},{9,11},{11,9},{13,15},{15,13},{24,26... | collective-permute-start | bytes 786440 | tf_op jit(solution)/shard_map/ppermute | solution.py:407
  68.9 12.2 %collective-permute-start.25 = (bf16[32,4096]{1,0:T(8,128)(2,1)S(1)}, bf16[32,4096]{1,0:T(8,128)(2,1)S(1)}, u32[]{:S(2)}, u32[]{:S(2)}) collective-permute-start(bf16[32,4096]{1,0:T(8,128)(2,1)S(1)} %collective-permute-done.18.refs_5_), channel_id=1, source_target_pairs={{0,2},{2,0},{4,6},{6,4},{1,3},{3,1},{5,7},{7,5},{16,18},{18,16},{2... | collective-permute-start | bytes 786440 | tf_op jit(solution)/shard_map/ppermute | solution.py:407
  71.7 9.4 %collective-permute-start.26 = (bf16[32,4096]{1,0:T(8,128)(2,1)S(1)}, bf16[32,4096]{1,0:T(8,128)(2,1)S(1)}, u32[]{:S(2)}, u32[]{:S(2)}) collective-permute-start(bf16[32,4096]{1,0:T(8,128)(2,1)S(1)} %collective-permute-done.19.refs_6_), channel_id=1, source_target_pairs={{12,14},{14,12},{13,15},{15,13},{28,30},{30,28},{29,31},{31,29}} | collective-permute-start | bytes 786440 | tf_op jit(solution)/shard_map/ppermute | solution.py:407
  72.4 10.8 %collective-permute-start.27 = (bf16[32,4096]{1,0:T(8,128)(2,1)S(1)}, bf16[32,4096]{1,0:T(8,128)(2,1)S(1)}, u32[]{:S(2)}, u32[]{:S(2)}) collective-permute-start(bf16[32,4096]{1,0:T(8,128)(2,1)S(1)} %collective-permute-done.20.refs_7_), channel_id=1, source_target_pairs={{0,2},{2,0},{1,3},{3,1},{16,18},{18,16},{17,19},{19,17}} | collective-permute-start | bytes 786440 | tf_op jit(solution)/shard_map/ppermute | solution.py:407
  88.8 6.8 %collective-permute-start.28 = (bf16[128,896]{1,0:T(8,128)(2,1)S(1)}, bf16[128,896]{1,0:T(8,128)(2,1)S(1)}, u32[]{:S(2)}, u32[]{:S(2)}) collective-permute-start(bf16[128,896]{1,0:T(8,128)(2,1)S(1)} %dynamic-slice_bitcast_fusion.4), channel_id=1, source_target_pairs={{0,16},{16,0},{1,17},{17,1},{2,18},{18,2},{3,19},{19,3},{4,20},{20... | collective-permute-start | bytes 688136 | tf_op jit(solution)/shard_map/ppermute | solution.py:24
  95.7 6.1 %collective-permute-start.32 = (bf16[128,896]{1,0:T(8,128)(2,1)S(1)}, bf16[128,896]{1,0:T(8,128)(2,1)S(1)}, u32[]{:S(2)}, u32[]{:S(2)}) collective-permute-start(bf16[128,896]{1,0:T(8,128)(2,1)S(1)} %fusion.27), channel_id=1, source_target_pairs={{0,16},{16,0},{1,17},{17,1},{2,18},{18,2},{3,19},{19,3},{4,20},{20... | collective-permute-start | bytes 688136 | tf_op jit(solution)/shard_map/ppermute | solution.py:24
  97.3 7.9 %collective-permute-start.29 = (bf16[128,896]{1,0:T(8,128)(2,1)S(1)}, bf16[128,896]{1,0:T(8,128)(2,1)S(1)}, u32[]{:S(2)}, u32[]{:S(2)}) collective-permute-start(bf16[128,896]{1,0:T(8,128)(2,1)S(1)} %fusion.27), channel_id=1, source_target_pairs={{0,4},{4,8},{8,12},{12,0},{1,5},{5,9},{9,13},{13,1},{2,6},{6,10},{... | collective-permute-start | bytes 688136 | tf_op jit(solution)/shard_map/ppermute | solution.py:29
  101.9 10.6 %collective-permute-start.33 = (bf16[2,128,896]{2,1,0:T(8,128)(2,1)S(1)}, bf16[2,128,896]{2,1,0:T(8,128)(2,1)S(1)}, u32[]{:S(2)}, u32[]{:S(2)}) collective-permute-start(bf16[2,128,896]{2,1,0:T(8,128)(2,1)S(1)} %pad_maximum_fusion.3.refs_0_), channel_id=1, source_target_pairs={{0,2},{2,0},{1,3},{3,1},{4,6},{6,4},{5,7},{7,5},{8,10},{10,8},{9,1... | collective-permute-start | bytes 1376264 | tf_op jit(solution)/shard_map/ppermute | solution.py:24
  102.8 6.0 %collective-permute-start.39 = (bf16[128,896]{1,0:T(8,128)(2,1)S(1)}, bf16[128,896]{1,0:T(8,128)(2,1)S(1)}, u32[]{:S(2)}, u32[]{:S(2)}) collective-permute-start(bf16[128,896]{1,0:T(8,128)(2,1)S(1)} %fusion.27), channel_id=1, source_target_pairs={{0,12},{4,0},{8,4},{12,8},{1,13},{5,1},{9,5},{13,9},{2,14},{6,2},{... | collective-permute-start | bytes 688136 | tf_op jit(solution)/shard_map/ppermute | solution.py:29
  105.2 6.4 %collective-permute-start.38 = (bf16[128,896]{1,0:T(8,128)(2,1)S(1)}, bf16[128,896]{1,0:T(8,128)(2,1)S(1)}, u32[]{:S(2)}, u32[]{:S(2)}) collective-permute-start(bf16[128,896]{1,0:T(8,128)(2,1)S(1)} %collective-permute-done.29), channel_id=1, source_target_pairs={{4,8},{8,12},{5,9},{9,13},{6,10},{10,14},{7,11},{11,15},{20,24},{2... | collective-permute-start | bytes 688136 | tf_op jit(solution)/shard_map/ppermute | solution.py:433
  108.9 7.9 %collective-permute-start.40 = (bf16[128,896]{1,0:T(8,128)(2,1)S(1)}, bf16[128,896]{1,0:T(8,128)(2,1)S(1)}, u32[]{:S(2)}, u32[]{:S(2)}) collective-permute-start(bf16[128,896]{1,0:T(8,128)(2,1)S(1)} %collective-permute-done.39), channel_id=1, source_target_pairs={{4,0},{8,4},{5,1},{9,5},{6,2},{10,6},{7,3},{11,7},{20,16},{24,20},... | collective-permute-start | bytes 688136 | tf_op jit(solution)/shard_map/ppermute | solution.py:434
  110.3 16.3 %collective-permute-start.34 = (bf16[2,128,896]{2,1,0:T(8,128)(2,1)S(1)}, bf16[2,128,896]{2,1,0:T(8,128)(2,1)S(1)}, u32[]{:S(2)}, u32[]{:S(2)}) collective-permute-start(bf16[2,128,896]{2,1,0:T(8,128)(2,1)S(1)} %pad_maximum_fusion.3.refs_0_), channel_id=1, source_target_pairs={{0,1},{1,0},{2,3},{3,2},{4,5},{5,4},{6,7},{7,6},{8,9},{9,8},{10,11... | collective-permute-start | bytes 1376264 | tf_op jit(solution)/shard_map/ppermute | solution.py:24
  110.4 8.5 %collective-permute-start.45 = (bf16[128,896]{1,0:T(8,128)(2,1)S(1)}, bf16[128,896]{1,0:T(8,128)(2,1)S(1)}, u32[]{:S(2)}, u32[]{:S(2)}) collective-permute-start(bf16[128,896]{1,0:T(8,128)(2,1)S(1)} %collective-permute-done.39), channel_id=1, source_target_pairs={{0,2},{2,0},{1,3},{3,1},{4,6},{6,4},{5,7},{7,5},{8,10},{10,8},{9,1... | collective-permute-start | bytes 688136 | tf_op jit(solution)/shard_map/ppermute | solution.py:24
  111.6 11.8 %collective-permute-start.30 = (bf16[128,896]{1,0:T(8,128)(2,1)S(1)}, bf16[128,896]{1,0:T(8,128)(2,1)S(1)}, u32[]{:S(2)}, u32[]{:S(2)}) collective-permute-start(bf16[128,896]{1,0:T(8,128)(2,1)S(1)} %collective-permute-done.29), channel_id=1, source_target_pairs={{0,2},{2,0},{1,3},{3,1},{4,6},{6,4},{5,7},{7,5},{8,10},{10,8},{9,1... | collective-permute-start | bytes 688136 | tf_op jit(solution)/shard_map/ppermute | solution.py:24
  112.5 15.3 %collective-permute-start.35 = (bf16[2,128,896]{2,1,0:T(8,128)(2,1)S(1)}, bf16[2,128,896]{2,1,0:T(8,128)(2,1)S(1)}, u32[]{:S(2)}, u32[]{:S(2)}) collective-permute-start(bf16[2,128,896]{2,1,0:T(8,128)(2,1)S(1)} %collective-permute-done.33.refs_1_), channel_id=1, source_target_pairs={{0,1},{1,0},{2,3},{3,2},{4,5},{5,4},{6,7},{7,6},{8,9},{9,8},{10,11... | collective-permute-start | bytes 1376264 | tf_op jit(solution)/shard_map/ppermute | solution.py:24
  116.8 8.3 %collective-permute-start.41 = (bf16[128,896]{1,0:T(8,128)(2,1)S(1)}, bf16[128,896]{1,0:T(8,128)(2,1)S(1)}, u32[]{:S(2)}, u32[]{:S(2)}) collective-permute-start(bf16[128,896]{1,0:T(8,128)(2,1)S(1)} %broadcast_select_fusion), channel_id=1, source_target_pairs={{0,16},{16,0},{1,17},{17,1},{2,18},{18,2},{3,19},{19,3},{4,20},{20... | collective-permute-start | bytes 688136 | tf_op jit(solution)/shard_map/ppermute | solution.py:24
  118.9 16.5 %collective-permute-start.46 = (bf16[2,128,896]{2,1,0:T(8,128)(2,1)S(1)}, bf16[2,128,896]{2,1,0:T(8,128)(2,1)S(1)}, u32[]{:S(2)}, u32[]{:S(2)}) collective-permute-start(bf16[2,128,896]{2,1,0:T(8,128)(2,1)S(1)} %pad_maximum_fusion.5.refs_0_), channel_id=1, source_target_pairs={{0,16},{16,0},{1,17},{17,1},{2,18},{18,2},{3,19},{19,3},{4,20},{20... | collective-permute-start | bytes 1376264 | tf_op jit(solution)/shard_map/ppermute | solution.py:24
  123.3 19.2 %collective-permute-start.47 = (bf16[2,128,896]{2,1,0:T(8,128)(2,1)S(1)}, bf16[2,128,896]{2,1,0:T(8,128)(2,1)S(1)}, u32[]{:S(2)}, u32[]{:S(2)}) collective-permute-start(bf16[2,128,896]{2,1,0:T(8,128)(2,1)S(1)} %pad_maximum_fusion.5.refs_0_), channel_id=1, source_target_pairs={{0,1},{1,0},{2,3},{3,2},{4,5},{5,4},{6,7},{7,6},{8,9},{9,8},{10,11... | collective-permute-start | bytes 1376264 | tf_op jit(solution)/shard_map/ppermute | solution.py:24
  125.1 17.5 %collective-permute-start.31 = (bf16[2,128,896]{2,1,0:T(8,128)(2,1)S(1)}, bf16[2,128,896]{2,1,0:T(8,128)(2,1)S(1)}, u32[]{:S(2)}, u32[]{:S(2)}) collective-permute-start(bf16[2,128,896]{2,1,0:T(8,128)(2,1)S(1)} %pad_maximum_fusion.2.refs_0_), channel_id=1, source_target_pairs={{0,16},{16,0},{1,17},{17,1},{2,18},{18,2},{3,19},{19,3},{4,20},{20... | collective-permute-start | bytes 1376264 | tf_op jit(solution)/shard_map/ppermute | solution.py:24
  126.6 11.1 %collective-permute-start.42 = (bf16[2,128,896]{2,1,0:T(8,128)(2,1)S(1)}, bf16[2,128,896]{2,1,0:T(8,128)(2,1)S(1)}, u32[]{:S(2)}, u32[]{:S(2)}) collective-permute-start(bf16[2,128,896]{2,1,0:T(8,128)(2,1)S(1)} %pad_maximum_fusion.4.refs_4_), channel_id=1, source_target_pairs={{0,2},{2,0},{1,3},{3,1},{4,6},{6,4},{5,7},{7,5},{8,10},{10,8},{9,1... | collective-permute-start | bytes 1376264 | tf_op jit(solution)/shard_map/ppermute | solution.py:24
  135.5 7.6 %collective-permute-start.48 = (bf16[2,128,896]{2,1,0:T(8,128)(2,1)S(1)}, bf16[2,128,896]{2,1,0:T(8,128)(2,1)S(1)}, u32[]{:S(2)}, u32[]{:S(2)}) collective-permute-start(bf16[2,128,896]{2,1,0:T(8,128)(2,1)S(1)} %collective-permute-done.46.refs_1_), channel_id=1, source_target_pairs={{0,1},{1,0},{2,3},{3,2},{4,5},{5,4},{6,7},{7,6},{8,9},{9,8},{10,11... | collective-permute-start | bytes 1376264 | tf_op jit(solution)/shard_map/ppermute | solution.py:24
  135.6 15.7 %collective-permute-start.36 = (bf16[2,128,896]{2,1,0:T(8,128)(2,1)S(1)}, bf16[2,128,896]{2,1,0:T(8,128)(2,1)S(1)}, u32[]{:S(2)}, u32[]{:S(2)}) collective-permute-start(bf16[2,128,896]{2,1,0:T(8,128)(2,1)S(1)} %pad_maximum_fusion.2.refs_0_), channel_id=1, source_target_pairs={{0,1},{1,0},{2,3},{3,2},{4,5},{5,4},{6,7},{7,6},{8,9},{9,8},{10,11... | collective-permute-start | bytes 1376264 | tf_op jit(solution)/shard_map/ppermute | solution.py:24
  137.8 13.6 %collective-permute-start.43 = (bf16[2,128,896]{2,1,0:T(8,128)(2,1)S(1)}, bf16[2,128,896]{2,1,0:T(8,128)(2,1)S(1)}, u32[]{:S(2)}, u32[]{:S(2)}) collective-permute-start(bf16[2,128,896]{2,1,0:T(8,128)(2,1)S(1)} %pad_maximum_fusion.4.refs_4_), channel_id=1, source_target_pairs={{0,1},{1,0},{2,3},{3,2},{4,5},{5,4},{6,7},{7,6},{8,9},{9,8},{10,11... | collective-permute-start | bytes 1376264 | tf_op jit(solution)/shard_map/ppermute | solution.py:24
  142.6 8.8 %collective-permute-start.44 = (bf16[2,128,896]{2,1,0:T(8,128)(2,1)S(1)}, bf16[2,128,896]{2,1,0:T(8,128)(2,1)S(1)}, u32[]{:S(2)}, u32[]{:S(2)}) collective-permute-start(bf16[2,128,896]{2,1,0:T(8,128)(2,1)S(1)} %collective-permute-done.42.refs_5_), channel_id=1, source_target_pairs={{0,1},{1,0},{2,3},{3,2},{4,5},{5,4},{6,7},{7,6},{8,9},{9,8},{10,11... | collective-permute-start | bytes 1376264 | tf_op jit(solution)/shard_map/ppermute | solution.py:24
  142.6 8.8 %collective-permute-start.37 = (bf16[2,128,896]{2,1,0:T(8,128)(2,1)S(1)}, bf16[2,128,896]{2,1,0:T(8,128)(2,1)S(1)}, u32[]{:S(2)}, u32[]{:S(2)}) collective-permute-start(bf16[2,128,896]{2,1,0:T(8,128)(2,1)S(1)} %collective-permute-done.31.refs_1_), channel_id=1, source_target_pairs={{0,1},{1,0},{2,3},{3,2},{4,5},{5,4},{6,7},{7,6},{8,9},{9,8},{10,11... | collective-permute-start | bytes 1376264 | tf_op jit(solution)/shard_map/ppermute | solution.py:24
  175.6 10.2 %collective-permute-start.49 = (bf16[2,256,1792]{2,1,0:T(8,128)(2,1)S(1)}, bf16[2,256,1792]{2,1,0:T(8,128)(2,1)S(1)}, u32[]{:S(2)}, u32[]{:S(2)}) collective-permute-start(bf16[2,256,1792]{2,1,0:T(8,128)(2,1)S(1)} %pad_maximum_fusion), channel_id=1, source_target_pairs={{0,1},{1,0},{2,3},{3,2},{4,5},{5,4},{6,7},{7,6},{8,9},{9,8},{10,11... | collective-permute-start | bytes 5505032 | tf_op jit(solution)/shard_map/ppermute | solution.py:24
  175.9 23.9 %collective-permute-start.56 = (bf16[2,256,1792]{2,1,0:T(8,128)(2,1)S(1)}, bf16[2,256,1792]{2,1,0:T(8,128)(2,1)S(1)}, u32[]{:S(2)}, u32[]{:S(2)}) collective-permute-start(bf16[2,256,1792]{2,1,0:T(8,128)(2,1)S(1)} %pad_maximum_fusion.1), channel_id=1, source_target_pairs={{0,1},{1,0},{2,3},{3,2},{4,5},{5,4},{6,7},{7,6},{8,9},{9,8},{10,11... | collective-permute-start | bytes 5505032 | tf_op jit(solution)/shard_map/ppermute | solution.py:24
  187.1 12.5 %collective-permute-start.50 = (bf16[128,1792]{1,0:T(8,128)(2,1)S(1)}, bf16[128,1792]{1,0:T(8,128)(2,1)S(1)}, u32[]{:S(2)}, u32[]{:S(2)}) collective-permute-start(bf16[128,1792]{1,0:T(8,128)(2,1)S(1)} %slice.67), channel_id=1, source_target_pairs={{0,16},{16,0},{1,17},{17,1},{2,18},{18,2},{3,19},{19,3},{4,20},{20... | collective-permute-start | bytes 1376264 | tf_op jit(solution)/shard_map/ppermute | solution.py:24
  188.9 15.1 %collective-permute-start.53 = (bf16[2,128,896]{2,1,0:T(8,128)(2,1)S(1)}, bf16[2,128,896]{2,1,0:T(8,128)(2,1)S(1)}, u32[]{:S(2)}, u32[]{:S(2)}) collective-permute-start(bf16[2,128,896]{2,1,0:T(8,128)(2,1)S(1)} %constant_dynamic-slice_fusion.2), channel_id=1, source_target_pairs={{0,2},{2,0},{1,3},{3,1},{4,6},{6,4},{5,7},{7,5},{8,10},{10,8},{9,1... | collective-permute-start | bytes 1376264 | tf_op jit(solution)/shard_map/ppermute | solution.py:24
  201.1 19.3 %collective-permute-start.60 = (bf16[128,1792]{1,0:T(8,128)(2,1)S(1)}, bf16[128,1792]{1,0:T(8,128)(2,1)S(1)}, u32[]{:S(2)}, u32[]{:S(2)}) collective-permute-start(bf16[128,1792]{1,0:T(8,128)(2,1)S(1)} %slice.73), channel_id=1, source_target_pairs={{0,16},{16,0},{1,17},{17,1},{2,18},{18,2},{3,19},{19,3},{4,20},{20... | collective-permute-start | bytes 1376264 | tf_op jit(solution)/shard_map/ppermute | solution.py:24
  202.8 8.6 %collective-permute-start.51 = (bf16[128,896]{1,0:T(8,128)(2,1)S(1)}, bf16[128,896]{1,0:T(8,128)(2,1)S(1)}, u32[]{:S(2)}, u32[]{:S(2)}) collective-permute-start(bf16[128,896]{1,0:T(8,128)(2,1)S(1)} %constant_dynamic-slice_fusion.3), channel_id=1, source_target_pairs={{0,2},{2,0},{1,3},{3,1},{4,6},{6,4},{5,7},{7,5},{8,10},{10,8},{9,1... | collective-permute-start | bytes 688136 | tf_op jit(solution)/shard_map/ppermute | solution.py:24
  204.3 13.4 %collective-permute-start.54 = (bf16[128,896]{1,0:T(8,128)(2,1)S(1)}, bf16[128,896]{1,0:T(8,128)(2,1)S(1)}, u32[]{:S(2)}, u32[]{:S(2)}) collective-permute-start(bf16[128,896]{1,0:T(8,128)(2,1)S(1)} %slice_bitcast_fusion.4), channel_id=1, source_target_pairs={{0,16},{16,0},{1,17},{17,1},{2,18},{18,2},{3,19},{19,3},{4,20},{20... | collective-permute-start | bytes 688136 | tf_op jit(solution)/shard_map/ppermute | solution.py:24
  205.1 14.1 %collective-permute-start.57 = (bf16[2,128,896]{2,1,0:T(8,128)(2,1)S(1)}, bf16[2,128,896]{2,1,0:T(8,128)(2,1)S(1)}, u32[]{:S(2)}, u32[]{:S(2)}) collective-permute-start(bf16[2,128,896]{2,1,0:T(8,128)(2,1)S(1)} %constant_dynamic-slice_fusion.1), channel_id=1, source_target_pairs={{0,2},{2,0},{1,3},{3,1},{4,6},{6,4},{5,7},{7,5},{8,10},{10,8},{9,1... | collective-permute-start | bytes 1376264 | tf_op jit(solution)/shard_map/ppermute | solution.py:24
  211.6 16.6 %collective-permute-start.52 = (bf16[128,896]{1,0:T(8,128)(2,1)S(1)}, bf16[128,896]{1,0:T(8,128)(2,1)S(1)}, u32[]{:S(2)}, u32[]{:S(2)}) collective-permute-start(bf16[128,896]{1,0:T(8,128)(2,1)S(1)} %add_convert_fusion.6), channel_id=1, source_target_pairs={{0,8},{4,12},{8,0},{12,4},{1,9},{5,13},{9,1},{13,5},{2,10},{6,14},... | collective-permute-start | bytes 688136 | tf_op jit(solution)/shard_map/ppermute | solution.py:29
  217.8 10.4 %collective-permute-start.55 = (bf16[128,896]{1,0:T(8,128)(2,1)S(1)}, bf16[128,896]{1,0:T(8,128)(2,1)S(1)}, u32[]{:S(2)}, u32[]{:S(2)}) collective-permute-start(bf16[128,896]{1,0:T(8,128)(2,1)S(1)} %fusion.25), channel_id=1, source_target_pairs={{0,4},{4,8},{8,12},{12,0},{1,5},{5,9},{9,13},{13,1},{2,6},{6,10},{... | collective-permute-start | bytes 688136 | tf_op jit(solution)/shard_map/ppermute | solution.py:29
  219.4 6.1 %collective-permute-start.58 = (bf16[128,896]{1,0:T(8,128)(2,1)S(1)}, bf16[128,896]{1,0:T(8,128)(2,1)S(1)}, u32[]{:S(2)}, u32[]{:S(2)}) collective-permute-start(bf16[128,896]{1,0:T(8,128)(2,1)S(1)} %slice_bitcast_fusion.2), channel_id=1, source_target_pairs={{0,16},{16,0},{1,17},{17,1},{2,18},{18,2},{3,19},{19,3},{4,20},{20... | collective-permute-start | bytes 688136 | tf_op jit(solution)/shard_map/ppermute | solution.py:24
  220.7 7.5 %collective-permute-start.61 = (bf16[128,896]{1,0:T(8,128)(2,1)S(1)}, bf16[128,896]{1,0:T(8,128)(2,1)S(1)}, u32[]{:S(2)}, u32[]{:S(2)}) collective-permute-start(bf16[128,896]{1,0:T(8,128)(2,1)S(1)} %constant_dynamic-slice_fusion), channel_id=1, source_target_pairs={{0,2},{2,0},{1,3},{3,1},{4,6},{6,4},{5,7},{7,5},{8,10},{10,8},{9,1... | collective-permute-start | bytes 688136 | tf_op jit(solution)/shard_map/ppermute | solution.py:24
  225.6 6.1 %collective-permute-start.59 = (bf16[128,896]{1,0:T(8,128)(2,1)S(1)}, bf16[128,896]{1,0:T(8,128)(2,1)S(1)}, u32[]{:S(2)}, u32[]{:S(2)}) collective-permute-start(bf16[128,896]{1,0:T(8,128)(2,1)S(1)} %fusion.24), channel_id=1, source_target_pairs={{0,12},{4,0},{8,4},{12,8},{1,13},{5,1},{9,5},{13,9},{2,14},{6,2},{... | collective-permute-start | bytes 688136 | tf_op jit(solution)/shard_map/ppermute | solution.py:29
  232.0 1.4 collective-permute-start.62
  (4 other events, 22.9 us)
